TPU v7x, 512 devices: a whole 4x4x16 slice. The times are simulated.
512 devices in a mesh: lat: 8 (over x, core), lev: 8 (over z_lo), obs: 8 (over y, z_hi).
Axes of the slice: x: 4, y: 4, z: 16 (z_hi: 2, z_lo: 8; z = z_hi * 8 + z_lo), core: 2. Of those that a mesh axis runs over, the one named last changes fastest.
Arguments:
- chi: float32 [136, 128, 2048], P('lev', 'lat', 'obs'), may hold values from -6 to 6
- mat_lon: float32 [2048, 2048], P(None, 'obs'), as said below
- mat_lat: float32 [128, 128], P('lat')
- mat_vert: float32 [136, 136], replicated
- chan_table: float32 [616, 136], replicated, may hold values from -0.5 to 0.5
- chan_map: int32 [300], replicated, may hold values from 0 to 615
- error_weight: float32 [300], replicated, may hold values from 0.5 to 2
- innovation: float32 [300, 524288], P(None, ('lat', 'lev', 'obs')), may hold values from -6 to 6
- foot_weight: float32 [4, 524288], P(None, ('lat', 'lev', 'obs')), may hold values from 0.2 to 1
- foot_slot: int32 [4, 524288], P(None, ('lat', 'lev', 'obs')), may hold values from 0 to 4095
- serve_cols: int32 [8, 64, 64, 64], P('lat', ('lev', 'obs')), may hold values from 0 to 511
Outputs:
- gradient: float32 [136, 128, 2048], P('lev', 'lat', 'obs')
Inputs may be any that keep to these rules, and one draw needn't show every extreme that they name: mat_lon and mat_lat are symmetric.
All inputs are finite; a program needn't handle non-finite values.
Results may differ from a plain program's by a relative error of at most 0.00015.
Values sent between devices are 32-bit elements; how exact they have to be, the bound alone decides.
No kernel may reach another device: no remote copies, remote signals or barrier semaphores. Data moves between devices by JAX's collectives and lax.ppermute only.
A program may use at most 128 MiB of HBM per device.

v0:
```python
import jax
import jax.numpy as jnp
from jax import lax
from jax.sharding import PartitionSpec as P

NLEV = 136


HIGHEST = lax.Precision.HIGHEST


def horizontal(field, mat_lon, mat_lat):
    levels, rows, cells = field.shape
    flat = field.reshape(levels * rows, cells)
    block = mat_lon
    along = jnp.dot(
        lax.all_gather(flat, "obs", axis=1, tiled=True),
        block,
        precision=HIGHEST,
        preferred_element_type=jnp.float32,
    )
    along = along.reshape(levels, rows, cells)
    block = mat_lat
    return jnp.einsum(
        "ij,ljk->lik",
        block,
        lax.all_gather(along, "lat", axis=1, tiled=True),
        precision=HIGHEST,
        preferred_element_type=jnp.float32,
    )


def observe(received, jacobian, error_weight, innovation, foot_weight, foot_slot):
    levels = received.shape[0]
    column_mean = jnp.zeros((levels, foot_slot.shape[1]), jnp.float32)
    for member in range(foot_slot.shape[0]):
        column_mean = column_mean + foot_weight[member][None, :] * jnp.take(
            received, foot_slot[member], axis=1
        )
    evolved = jnp.dot(jacobian, column_mean, precision=HIGHEST, preferred_element_type=jnp.float32)
    weighted = error_weight[:, None] * (evolved - innovation)
    pulled = jnp.dot(jacobian.T, weighted, precision=HIGHEST, preferred_element_type=jnp.float32)
    spread = (pulled[:, None, :] * foot_weight[None, :, :]).reshape(levels, -1)
    return jnp.zeros_like(received).at[:, foot_slot.reshape(-1)].add(spread)


def shards(
    chi,
    mat_lon,
    mat_lat,
    mat_vert,
    chan_table,
    chan_map,
    error_weight,
    innovation,
    foot_weight,
    foot_slot,
    serve_cols,
):
    levels, rows, cells = chi.shape
    depth = lax.axis_size("lev")
    owners = depth * lax.axis_size("obs")
    capacity = serve_cols.shape[3]
    smoothed = horizontal(chi, mat_lon, mat_lat)
    flat = smoothed.reshape(levels, rows * cells)
    matches = (
        chan_map[:, None] == jnp.arange(chan_table.shape[0], dtype=jnp.int32)[None, :]
    ).astype(jnp.float32)
    selected = jnp.dot(matches, chan_table, precision=HIGHEST, preferred_element_type=jnp.float32)
    columns = lax.all_to_all(flat, "lev", split_axis=1, concat_axis=0, tiled=True)
    profiles = jnp.dot(mat_vert, columns, precision=HIGHEST, preferred_element_type=jnp.float32)
    picks = serve_cols[0, 0].reshape(-1)
    outgoing = jnp.take(profiles, picks, axis=1).reshape(NLEV, owners, capacity)
    received = lax.all_to_all(
        outgoing, ("lev", "obs"), split_axis=1, concat_axis=1, tiled=True
    ).reshape(NLEV, owners * capacity)
    slot_grad = observe(received, selected, error_weight, innovation, foot_weight, foot_slot)
    returned = lax.all_to_all(
        slot_grad.reshape(NLEV, owners, capacity),
        ("lev", "obs"),
        split_axis=1,
        concat_axis=1,
        tiled=True,
    )
    column_grad = (
        jnp.zeros_like(profiles).at[:, picks].add(returned.reshape(NLEV, owners * capacity))
    )
    column_grad = jnp.dot(
        mat_vert.T, column_grad, precision=HIGHEST, preferred_element_type=jnp.float32
    )
    slab_grad = lax.all_to_all(column_grad, "lev", split_axis=0, concat_axis=1, tiled=True)
    return chi + horizontal(slab_grad.reshape(levels, rows, cells), mat_lon, mat_lat)


def solution(mesh):
    in_specs = (
        P("lev", "lat", "obs"),
        P(None, "obs"),
        P("lat", None),
        P(),
        P(),
        P(),
        P(),
        P(None, ("lat", "lev", "obs")),
        P(None, ("lat", "lev", "obs")),
        P(None, ("lat", "lev", "obs")),
        P("lat", ("lev", "obs"), None, None),
    )
    out_specs = P("lev", "lat", "obs")
    return jax.shard_map(shards, mesh=mesh, in_specs=in_specs, out_specs=out_specs, check_vma=False)
```

profile of v0, /device:TPU:1, one launch (start us, length us, event | category | flops | bytes accessed | tf_op | source)
XLA Modules:
  0.0 893.9 jit_solution(16359783666293935202)
XLA Ops:
  6.5 0.7 all-gather.5.cloned.1.call-update
  7.3 131.4 %all-gather.5.cloned.1.call-done = f32[272,2048]{1,0:T(8,128)} async-done(((f32[272,256]{1,0:T(8,128)}), f32[272,2048]{1,0:T(8,128)}) %all-gather.5.cloned.1.call-update) | async-done | bytes 2228240 | tf_op jit(solution)/shard_map/all_gather | solution.py:17
  138.7 4.3 fusion.37
  143.2 26.2 %all-gather.7.cloned.1.call-done = f32[17,128,256]{2,1,0:T(8,128)} async-done(((f32[17,16,256]{2,1,0:T(8,128)}), f32[17,128,256]{2,1,0:T(8,128)}) %all-gather.7.cloned.1.call-update) | async-done | bytes 2228240 | tf_op jit(solution)/shard_map/all_gather | solution.py:27
  169.3 2.9 convolution_bitcast_fusion.3
  172.3 0.9 copy.14
  173.2 9.7 %all-to-all-start = ((f32[17,8,512]{2,0,1:T(8,128)}), f32[17,8,512]{2,0,1:T(8,128)S(1)}, u32[]{:S(2)}, u32[]{:S(2)}) async-start(f32[17,8,512]{2,0,1:T(8,128)} %copy.14), calls=%async_computation | async-start | bytes 786432 | tf_op jit(solution)/shard_map/all_to_all | solution.py:70
  183.0 17.8 %all-to-all-done = f32[17,8,512]{2,0,1:T(8,128)S(1)} async-done(((f32[17,8,512]{2,0,1:T(8,128)}), f32[17,8,512]{2,0,1:T(8,128)S(1)}, u32[]{:S(2)}, u32[]{:S(2)}) %all-to-all-start) | async-done | bytes 278560 | tf_op jit(solution)/shard_map/all_to_all | solution.py:70
  201.5 16.1 %gather_fusion = f32[4096,136]{1,0:T(8,128)} fusion(f32[136,512]{0,1:T(8,128)S(1)} %copy.15, s32[4096]{0:T(1024)S(1)} %broadcast_clamp_fusion), kind=kCustom, calls=%fused_computation.4 | custom fusion | bytes 4472832 | tf_op jit(solution)/shard_map/jit(_take)/gather | solution.py:73
  217.5 3.9 broadcast_select_fusion
  221.5 13.3 %all-to-all-start.1 = ((f32[136,64,64]{0,2,1:T(8,128)}), f32[136,64,64]{0,2,1:T(8,128)}, u32[]{:S(2)}, u32[]{:S(2)}) async-start(f32[136,64,64]{0,2,1:T(8,128)} %broadcast_select_fusion), calls=%async_computation.1 | async-start | bytes 8388608 | tf_op jit(solution)/shard_map/all_to_all | solution.py:74
  236.9 0.6 compare_and_fusion.1
  238.1 0.7 fusion.15
  238.9 0.6 compare_select_fusion
  239.5 174.7 %all-to-all-done.1 = f32[136,64,64]{0,2,1:T(8,128)} async-done(((f32[136,64,64]{0,2,1:T(8,128)}), f32[136,64,64]{0,2,1:T(8,128)}, u32[]{:S(2)}, u32[]{:S(2)}) %all-to-all-start.1) | async-done | bytes 2228256 | tf_op jit(solution)/shard_map/all_to_all | solution.py:74
  414.1 6.1 gather_fusion.1
  420.3 7.1 gather_fusion.2
  427.4 7.1 gather_fusion.3
  434.5 6.8 gather_fusion.4
  441.4 6.3 fusion.3
  447.7 2.7 fusion.38
  450.4 2.4 bitcast_multiply_fusion
  452.7 25.3 %scatter_custom_fusion = f32[136,4096]{0,1:T(8,128)} fusion(s32[4096]{0:T(1024)} %bitcast.121, f32[136,4096]{0,1:T(8,128)} %bitcast_multiply_fusion, f32[]{:T(128)} %constant.9.clone.1), kind=kCustom, calls=%fused_computation.7 | custom fusion | flops 557056 | bytes 6423040 | tf_op jit(solution)/shard_map/scatter-add | solution.py:44
  478.0 203.3 %all_to_all.45 = f32[136,64,64]{0,2,1:T(8,128)} all-to-all(f32[136,64,64]{0,2,1:T(8,128)} %bitcast.95), channel_id=1, replica_groups=mesh['lat'=8,'lev'=8,'obs'=8] {'lev','obs'}, dimensions={1} | all-to-all | bytes 4456448 | tf_op jit(solution)/shard_map/all_to_all | solution.py:78
  681.3 23.0 %scatter_custom_fusion.1 = f32[136,512]{0,1:T(8,128)S(1)} fusion(s32[4096]{0:T(1024)S(1)} %bitcast.107, f32[4096,136]{1,0:T(8,128)} %bitcast.97, f32[]{:T(128)} %constant.9.clone.1), kind=kCustom, calls=%fused_computation.42 | custom fusion | flops 557056 | bytes 279040 | tf_op jit(solution)/shard_map/scatter-add | solution.py:86
  704.3 0.7 convolution_bitcast_fusion
  705.1 27.2 %all_to_all.46 = f32[8,17,512]{2,1,0:T(8,128)S(1)} all-to-all(f32[8,17,512]{2,1,0:T(8,128)S(1)} %all_to_all.38), channel_id=1, replica_groups=mesh['lat'=8,'lev'=8,'obs'=8] {'lev'}, dimensions={0} | all-to-all | bytes 557056 | tf_op jit(solution)/shard_map/all_to_all | solution.py:91
  732.4 0.8 reshape_reshape.3
  733.3 120.0 %all-gather.9.cloned.1.call-done = f32[272,2048]{1,0:T(8,128)} async-done(((f32[272,256]{1,0:T(8,128)}), f32[272,2048]{1,0:T(8,128)}) %all-gather.9.cloned.1.call-update) | async-done | bytes 2228240 | tf_op jit(solution)/shard_map/all_gather | solution.py:17
  853.2 4.3 fusion.39
  857.6 26.3 %all-gather.11.cloned.1.call-done = f32[17,128,256]{2,1,0:T(8,128)} async-done(((f32[17,16,256]{2,1,0:T(8,128)}), f32[17,128,256]{2,1,0:T(8,128)}) %all-gather.11.cloned.1.call-update) | async-done | bytes 2228240 | tf_op jit(solution)/shard_map/all_gather | solution.py:27
  883.8 3.6 fusion.4
  (44 shorter events, 3.9 us)
Async XLA Ops:
  6.5 132.2 %copy-start = (f32[2048,256]{1,0:T(8,128)S(1)}, f32[2048,256]{1,0:T(8,128)}, u32[]{:S(2)}) copy-start(f32[2048,256]{1,0:T(8,128)} %param.14) | copy-start | bytes 6291460
  6.5 132.2 %all-gather.5.cloned.1.call-start = ((), (), s32[]{:S(2)}) async-start(), calls=%async_computation.4 | async-start | bytes 2506752 | tf_op jit(solution)/shard_map/all_gather | solution.py:17
  7.3 135.8 %copy-start.4 = (s32[1,1,64,64]{3,2,1,0:T(8,128)S(1)}, s32[1,1,64,64]{3,2,1,0:T(8,128)}, u32[]{:S(2)}) copy-start(s32[1,1,64,64]{3,2,1,0:T(8,128)} %param.23) | copy-start | bytes 49156
  7.3 162.1 %copy-start.7 = (f32[16,128]{1,0:T(8,128)S(1)}, f32[16,128]{1,0:T(8,128)}, u32[]{:S(2)}) copy-start(f32[16,128]{1,0:T(8,128)} %param.15) | copy-start | bytes 24580
  7.3 162.0 %all-gather.7.cloned.1.call-start = ((), (), s32[]{:S(2)}) async-start(), calls=%async_computation.5 | async-start | bytes 2506752 | tf_op jit(solution)/shard_map/all_gather | solution.py:27
  143.2 57.7 %copy-start.2 = (f32[136,136]{1,0:T(8,128)S(1)}, f32[136,136]{1,0:T(8,128)}, u32[]{:S(2)}) copy-start(f32[136,136]{1,0:T(8,128)} %param.16) | copy-start | bytes 221956
  173.2 27.6 %all-to-all-start = ((f32[17,8,512]{2,0,1:T(8,128)}), f32[17,8,512]{2,0,1:T(8,128)S(1)}, u32[]{:S(2)}, u32[]{:S(2)}) async-start(f32[17,8,512]{2,0,1:T(8,128)} %copy.14), calls=%async_computation | async-start | bytes 786432 | tf_op jit(solution)/shard_map/all_to_all | solution.py:70
  221.5 13.6 %copy-start.6 = (f32[4,1024]{1,0:T(4,128)S(1)}, f32[4,1024]{1,0:T(4,128)}, u32[]{:S(2)}) copy-start(f32[4,1024]{1,0:T(4,128)} %param.21) | copy-start | bytes 49156
  221.5 13.6 %copy-start.5 = (s32[4,1024]{1,0:T(4,128)S(1)}, s32[4,1024]{1,0:T(4,128)}, u32[]{:S(2)}) copy-start(s32[4,1024]{1,0:T(4,128)} %param.22) | copy-start | bytes 49156
  221.5 16.6 %copy-start.3 = (f32[616,136]{0,1:T(8,128)S(1)}, f32[616,136]{0,1:T(8,128)}, u32[]{:S(2)}) copy-start(f32[616,136]{0,1:T(8,128)} %param.17) | copy-start | bytes 1005316
  221.5 16.6 %copy-start.8 = (s32[300]{0:T(512)S(1)}, s32[300]{0:T(512)}, u32[]{:S(2)}) copy-start(s32[300]{0:T(512)} %param.18) | copy-start | bytes 3604
  221.5 192.6 %all-to-all-start.1 = ((f32[136,64,64]{0,2,1:T(8,128)}), f32[136,64,64]{0,2,1:T(8,128)}, u32[]{:S(2)}, u32[]{:S(2)}) async-start(f32[136,64,64]{0,2,1:T(8,128)} %broadcast_select_fusion), calls=%async_computation.1 | async-start | bytes 8388608 | tf_op jit(solution)/shard_map/all_to_all | solution.py:74
  234.8 618.4 %all-gather.9.cloned.1.call-start = ((), (), s32[]{:S(2)}) async-start(), calls=%async_computation.6 | async-start | bytes 2506752 | tf_op jit(solution)/shard_map/all_gather | solution.py:17
  733.2 150.6 %copy-start.1 = (f32[17,16,256]{2,1,0:T(8,128)S(1)}, f32[17,16,256]{2,1,0:T(8,128)}, u32[]{:S(2)}) copy-start(f32[17,16,256]{2,1,0:T(8,128)} %param.13) | copy-start | bytes 835588
  733.2 150.6 %all-gather.11.cloned.1.call-start = ((), (), s32[]{:S(2)}) async-start(), calls=%async_computation.7 | async-start | bytes 2506752 | tf_op jit(solution)/shard_map/all_gather | solution.py:27
Sparse Core Ops, SparseCore 0:
  10.4 128.2 all-gather.4
  143.2 26.1 all-gather.6
  733.3 119.8 all-gather.8
  857.7 26.0 all-gather.10
where the time goes:
time: 895 us; the launch traced here: 894 us
  waiting for transfers between devices  497 us (56%)
  blocking collectives  230 us (26%)
  other arithmetic  58.2 us (7%)
  local copies, waits for them, and re-layouts  45.7 us (5%)
  matrix products  25.9 us (3%)
  starting transfers between devices  23.3 us (3%)
  between operations  13.4 us (1%)
    all_gather x2, waiting for transfers between devices, horizontal(): lax.all_gather(flat, 'obs', axis=1, tiled=True)  251 us
    all_to_all x1, blocking collectives, shards(): lax.all_to_all(slot_grad.reshape(NLEV, owners, capacity), ('lev', 'obs'),...  203 us
    all_to_all x1, waiting for transfers between devices, shards(): lax.all_to_all(outgoing, ('lev', 'obs'), split_axis=1, concat_axis=1, til...  175 us
    all_gather x2, waiting for transfers between devices, horizontal(): lax.all_gather(along, 'lat', axis=1, tiled=True)  52.4 us
    gather x4, local copies, waits for them, and re-layouts, observe(): jnp.take(received, foot_slot[member], axis=1)  27.2 us
    all_to_all x1, blocking collectives, shards(): lax.all_to_all(column_grad, 'lev', split_axis=0, concat_axis=1, tiled=True)  27.2 us
    scatter-add x1, other arithmetic, observe(): return jnp.zeros_like(received).at[:, foot_slot.reshape(-1)].add(spread)  25.3 us
    scatter-add x1, other arithmetic, shards(): jnp.zeros_like(profiles).at[:, picks]  23 us
  transfers between devices with their start and end apart: 6, of which 6 were waited for; matrix products, arithmetic and copies ran while one was open for 1% of the time, Pallas kernels for 0%

commit v1 on v0

v1 whole, which is shorter than its diff:
```python
import functools

import jax
import jax.numpy as jnp
from jax import lax
from jax.experimental import pallas as pl
from jax.experimental.pallas import tpu as pltpu
from jax.sharding import PartitionSpec as P

HIGHEST = lax.Precision.HIGHEST
F32 = jnp.float32
BF16 = jnp.bfloat16

LEVELS = 17
MAIN = 16
ROWS = 16
CELLS = 256
TILE = ROWS * LEVELS
OWNER = 2 * MAIN
CAP = 64
TILES = 8
VIEWERS = 8
OBS = 1024
FOOT = 4
BLOCK = 256
PARTNER = [(t, t ^ 1) for t in range(8)]
ALONG_Y = [[0, 2, 4, 6], [1, 3, 5, 7]]


def split_rows(x):
    high = x.astype(BF16)
    low = (x - high.astype(F32)).astype(BF16)
    return jnp.concatenate([high, low], axis=0)


def one_hot(index, rows):
    place = lax.broadcasted_iota(jnp.int32, (rows, index.shape[1]), 0)
    return jnp.where(place == index, 1.0, 0.0).astype(BF16)


def dot(a, b):
    return lax.dot_general(a, b, (((1,), (0,)), ((), ())), preferred_element_type=F32)


def dot_nt(a, b):
    return lax.dot_general(a, b, (((1,), (1,)), ((), ())), preferred_element_type=F32)


def pick_kernel(field_ref, serve_ref, slots_ref):
    tile = pl.program_id(0)
    for half in range(2):
        last = field_ref[0, 256 + 8 * half : 264 + 8 * half, :]
        mains = []
        lasts = []
        for quarter in range(4):
            slab = 4 * half + quarter
            index = serve_ref[0, slab : slab + 1, :]
            cell = jnp.bitwise_and(index, CELLS - 1)
            second = index >= CELLS
            rows = jnp.concatenate([field_ref[0, slab * OWNER : (slab + 1) * OWNER, :], last], axis=0)
            count = OWNER + 8
            both = dot(split_rows(rows), one_hot(cell, CELLS))
            picked = both[:count] + both[count:]
            mains.append(jnp.where(second, picked[MAIN:OWNER], picked[:MAIN]))
            at = OWNER + 2 * quarter
            lasts.append(jnp.where(second, picked[at + 1 : at + 2], picked[at : at + 1]))
        start = pl.multiple_of(tile * OWNER + half * MAIN, MAIN)
        for viewer in range(VIEWERS):
            lanes = slice(viewer * CAP, (viewer + 1) * CAP)
            slots_ref[viewer, pl.ds(start, MAIN), :] = jnp.concatenate([m[:, lanes] for m in mains], axis=1)
            slots_ref[viewer, pl.ds(256 + 2 * tile + half, 1), :] = jnp.concatenate(
                [m[:, lanes] for m in lasts], axis=1
            )


def pick(field, serve):
    return pl.pallas_call(
        pick_kernel,
        grid=(TILES,),
        in_specs=[
            pl.BlockSpec((1, TILE, CELLS), lambda j: (j, 0, 0)),
            pl.BlockSpec((1, 8, VIEWERS * CAP), lambda j: (j, 0, 0)),
        ],
        out_specs=pl.BlockSpec((VIEWERS, TILE, BLOCK), lambda j: (0, 0, 0)),
        out_shape=jax.ShapeDtypeStruct((VIEWERS, TILE, BLOCK), F32),
        compiler_params=pltpu.CompilerParams(vmem_limit_bytes=32 * 1024 * 1024),
    )(field, serve)


def mean_kernel(slots_ref, place_ref, weight_ref, mean_ref):
    values = split_rows(slots_ref[0])
    for start in range(0, OBS, BLOCK):
        lanes = slice(start, start + BLOCK)
        main = jnp.zeros((MAIN, BLOCK), F32)
        last = jnp.zeros((16, BLOCK), F32)
        for member in range(FOOT):
            place = place_ref[0, member : member + 1, lanes]
            low = jnp.bitwise_and(place, BLOCK - 1)
            high = lax.shift_right_logical(place, 8)
            weight = weight_ref[0, member : member + 1, lanes]
            both = dot(values, one_hot(low, BLOCK))
            picked = both[:TILE] + both[TILE:]
            masked = jnp.where(lax.broadcasted_iota(jnp.int32, (16, BLOCK), 0) == high, weight, 0.0)
            for part in range(16):
                main = main + picked[part * MAIN : (part + 1) * MAIN] * masked[part : part + 1]
            last = last + picked[256:TILE] * masked
        mean_ref[0, :MAIN, lanes] = main
        mean_ref[0, MAIN:, lanes] = jnp.sum(last, axis=0, keepdims=True)


def means(slots, place, weight):
    count = slots.shape[0]
    return pl.pallas_call(
        mean_kernel,
        grid=(count,),
        in_specs=[
            pl.BlockSpec((1, TILE, BLOCK), lambda v: (v, 0, 0)),
            pl.BlockSpec((1, FOOT, OBS), lambda v: (v, 0, 0)),
            pl.BlockSpec((1, FOOT, OBS), lambda v: (v, 0, 0)),
        ],
        out_specs=pl.BlockSpec((1, LEVELS, OBS), lambda v: (v, 0, 0)),
        out_shape=jax.ShapeDtypeStruct((count, LEVELS, OBS), F32),
        compiler_params=pltpu.CompilerParams(vmem_limit_bytes=32 * 1024 * 1024),
    )(slots, place, weight)


def spread_kernel(grad_ref, place_ref, weight_ref, slots_ref):
    total = jnp.zeros((2 * TILE, BLOCK), F32)
    for start in range(0, OBS, BLOCK):
        lanes = slice(start, start + BLOCK)
        grad = grad_ref[0, :, lanes]
        for member in range(FOOT):
            place = place_ref[0, member : member + 1, lanes]
            low = jnp.bitwise_and(place, BLOCK - 1)
            high = lax.shift_right_logical(place, 8)
            scaled = grad * weight_ref[0, member : member + 1, lanes]
            hit = jnp.where(lax.broadcasted_iota(jnp.int32, (16, BLOCK), 0) == high, 1.0, 0.0)
            main = scaled[:MAIN]
            main_high = main.astype(BF16)
            main_low = (main - main_high.astype(F32)).astype(BF16)
            last = scaled[MAIN:] * hit
            last_high = last.astype(BF16)
            last_low = (last - last_high.astype(F32)).astype(BF16)
            hits = [jnp.broadcast_to(hit[part : part + 1], (MAIN, BLOCK)).astype(BF16) for part in range(16)]
            rows = jnp.concatenate(
                [main_high * h for h in hits] + [last_high] + [main_low * h for h in hits] + [last_low], axis=0
            )
            total = total + dot_nt(rows, one_hot(low, BLOCK))
    slots_ref[0] = total[:TILE] + total[TILE:]


def spread(grad, place, weight):
    count = grad.shape[0]
    return pl.pallas_call(
        spread_kernel,
        grid=(count,),
        in_specs=[
            pl.BlockSpec((1, LEVELS, OBS), lambda v: (v, 0, 0)),
            pl.BlockSpec((1, FOOT, OBS), lambda v: (v, 0, 0)),
            pl.BlockSpec((1, FOOT, OBS), lambda v: (v, 0, 0)),
        ],
        out_specs=pl.BlockSpec((1, TILE, BLOCK), lambda v: (v, 0, 0)),
        out_shape=jax.ShapeDtypeStruct((count, TILE, BLOCK), F32),
        compiler_params=pltpu.CompilerParams(vmem_limit_bytes=32 * 1024 * 1024),
    )(grad, place, weight)


def put_kernel(slots_ref, serve_ref, field_ref):
    tile = pl.program_id(0)
    for half in range(2):
        start = pl.multiple_of(tile * OWNER + half * MAIN, MAIN)
        mains = [slots_ref[viewer, pl.ds(start, MAIN), :] for viewer in range(VIEWERS)]
        lasts = [slots_ref[viewer, pl.ds(256 + 2 * tile + half, 1), :] for viewer in range(VIEWERS)]
        tails = []
        for quarter in range(4):
            slab = 4 * half + quarter
            index = serve_ref[0, slab : slab + 1, :]
            cell = jnp.bitwise_and(index, CELLS - 1)
            second = index >= CELLS
            lanes = slice(quarter * CAP, (quarter + 1) * CAP)
            main = jnp.concatenate([m[:, lanes] for m in mains], axis=1)
            last = jnp.concatenate([m[:, lanes] for m in lasts], axis=1)
            row = lax.broadcasted_iota(jnp.int32, (8, VIEWERS * CAP), 0)
            tail = jnp.where(row == jnp.where(second, 1, 0), last, 0.0)
            rows = jnp.concatenate([jnp.where(second, 0.0, main), jnp.where(second, main, 0.0), tail], axis=0)
            count = OWNER + 8
            both = dot_nt(split_rows(rows), one_hot(cell, CELLS))
            back = both[:count] + both[count:]
            field_ref[0, slab * OWNER : (slab + 1) * OWNER, :] = back[:OWNER]
            tails.append(back[OWNER : OWNER + 2])
        field_ref[0, 256 + 8 * half : 264 + 8 * half, :] = jnp.concatenate(tails, axis=0)


def put(slots, serve):
    return pl.pallas_call(
        put_kernel,
        grid=(TILES,),
        in_specs=[
            pl.BlockSpec((VIEWERS, TILE, BLOCK), lambda j: (0, 0, 0)),
            pl.BlockSpec((1, 8, VIEWERS * CAP), lambda j: (j, 0, 0)),
        ],
        out_specs=pl.BlockSpec((1, TILE, CELLS), lambda j: (j, 0, 0)),
        out_shape=jax.ShapeDtypeStruct((TILES, TILE, CELLS), F32),
        compiler_params=pltpu.CompilerParams(vmem_limit_bytes=32 * 1024 * 1024),
    )(slots, serve)


def to_all_y(block):
    copies = jnp.broadcast_to(block[None], (4,) + block.shape)
    return lax.all_to_all(copies, "obs", 0, 0, axis_index_groups=ALONG_Y)


def gather_obs(block):
    other = lax.ppermute(block, "obs", PARTNER)
    return to_all_y(block), to_all_y(other)


def times_lon(near, far, lon_near, lon_far):
    def product(tiles, matrix):
        return jnp.einsum("yrc,ycd->rd", tiles, matrix, precision=HIGHEST, preferred_element_type=F32)

    return product(near, lon_near) + product(far, lon_far)


def shards(
    chi,
    mat_lon,
    mat_lat,
    mat_vert,
    chan_table,
    chan_map,
    error_weight,
    innovation,
    foot_weight,
    foot_slot,
    serve_cols,
):
    half = lax.axis_index("obs") % 2

    def near_far(x, axis):
        near = lax.dynamic_index_in_dim(x, half, axis, keepdims=False)
        far = lax.dynamic_index_in_dim(x, 1 - half, axis, keepdims=False)
        return near, far

    serve = serve_cols[0, 0].astype(F32).reshape(8, 8, CAP).transpose(1, 0, 2)
    serve = lax.all_to_all(serve, "obs", 0, 0)
    about = jnp.concatenate(
        [serve.reshape(4, OBS), foot_slot.astype(F32), foot_weight], axis=0
    )
    about = lax.all_gather(about, "lev", axis=0, tiled=False)
    serve = about[:, :4].reshape(8, 4, 2, VIEWERS * CAP).astype(jnp.int32)
    near, far = near_far(serve, 2)
    serve = jnp.concatenate([near, far], axis=1).transpose(1, 0, 2)
    slot = about[:, 4:8].astype(jnp.int32)
    weight = about[:, 8:]
    tile = (slot >> 6) & 7
    tile = (tile >> 1) + 4 * ((tile & 1) ^ half)
    slab = slot >> 9
    place = (2 * tile + (slab >> 2)) * BLOCK + (slab & 3) * CAP + (slot & (CAP - 1))

    lon_near, lon_far = near_far(mat_lon.reshape(4, 2, CELLS, CELLS), 1)

    band = lax.all_gather(chi, "lat", axis=1, tiled=True)
    field = jnp.einsum("ij,ljk->ilk", mat_lat, band, precision=HIGHEST, preferred_element_type=F32)
    field = jnp.concatenate([field[:, :MAIN].reshape(ROWS * MAIN, CELLS), field[:, MAIN]], axis=0)
    field = times_lon(*gather_obs(field), lon_near, lon_far)
    near, far = gather_obs(field)
    slots = pick(jnp.concatenate([near, far], axis=0), serve)
    mean = means(slots, place, weight)
    mean = lax.all_to_all(mean, "lev", 0, 0).reshape(8 * LEVELS, OBS)

    matches = (
        chan_map[:, None] == jnp.arange(chan_table.shape[0], dtype=jnp.int32)[None, :]
    ).astype(F32)
    selected = jnp.dot(matches, chan_table, precision=HIGHEST, preferred_element_type=F32)
    selected = jnp.dot(selected, mat_vert, precision=HIGHEST, preferred_element_type=F32)
    scaled = error_weight[:, None] * selected
    hessian = jnp.dot(selected.T, scaled, precision=HIGHEST, preferred_element_type=F32)
    constant = jnp.dot(scaled.T, innovation, precision=HIGHEST, preferred_element_type=F32)
    pulled = jnp.dot(hessian, mean, precision=HIGHEST, preferred_element_type=F32) - constant

    pulled = lax.all_to_all(pulled.reshape(8, LEVELS, OBS), "lev", 0, 0)
    slots = spread(pulled, place, weight)
    partial = put(slots, serve)
    far = jnp.sum(lax.all_to_all(partial[4:], "obs", 0, 0, axis_index_groups=ALONG_Y), axis=0)
    far = lax.ppermute(far, "obs", PARTNER)
    near = jnp.sum(lax.all_to_all(partial[:4], "obs", 0, 0, axis_index_groups=ALONG_Y), axis=0)
    field = times_lon(*gather_obs(near + far), lon_near, lon_far)
    band = lax.all_gather(field, "lat", axis=0, tiled=False)
    main = band[:, : ROWS * MAIN].reshape(8 * ROWS, MAIN, CELLS)
    last = band[:, ROWS * MAIN :].reshape(8 * ROWS, 1, CELLS)
    band = jnp.concatenate([main, last], axis=1)
    return chi + jnp.einsum("ij,jlk->lik", mat_lat, band, precision=HIGHEST, preferred_element_type=F32)


def solution(mesh):
    in_specs = (
        P("lev", "lat", "obs"),
        P(None, "obs"),
        P("lat", None),
        P(),
        P(),
        P(),
        P(),
        P(None, ("lat", "lev", "obs")),
        P(None, ("lat", "lev", "obs")),
        P(None, ("lat", "lev", "obs")),
        P("lat", ("lev", "obs"), None, None),
    )
    out_specs = P("lev", "lat", "obs")
    return jax.shard_map(shards, mesh=mesh, in_specs=in_specs, out_specs=out_specs, check_vma=False)
```

time: 895 us -> 512 us (0.57)
  waiting for transfers between devices: 497 us -> 210 us
  blocking collectives: 230 us -> 146 us
  other arithmetic: 58.2 us -> 5.95 us
  starting transfers between devices: 23.3 us -> 63.7 us
  Pallas kernels: 0 us -> 34.5 us
  local copies, waits for them, and re-layouts: 45.7 us -> 15.6 us
    all_gather x4 -> x2, waiting for transfers between devices: 304 us -> 105 us  [the longest x1 63.5 us: shards(): band = lax.all_gather(field, 'lat', axis=0, tiled=False)]
    all_to_all x2 -> x3, blocking collectives: 230 us -> 81.2 us  [the longest x1 54.7 us: shards(): pulled = lax.all_to_all(pulled.reshape(8, LEVELS, OBS), 'lev', 0, 0)]
    all_to_all x2 -> x8, waiting for transfers between devices: 192 us -> 61 us  [the longest x5 27.5 us: to_all_y(): return lax.all_to_all(copies, 'obs', 0, 0, axis_index_groups=ALONG_Y)]
    all_gather x0 -> x1, blocking collectives: none -> 64.5 us  [shards(): about = lax.all_gather(about, 'lev', axis=0, tiled=False)]
    scatter-add x2 -> x0, other arithmetic: 48.2 us -> none  [the longest x1 25.3 us: observe(): return jnp.zeros_like(received).at[:, foot_slot.reshape(-1)].add(spread)]
    gather x5 -> x0, local copies, waits for them, and re-layouts: 43.3 us -> none  [the longest x4 27.2 us: observe(): jnp.take(received, foot_slot[member], axis=1)]
    ppermute x0 -> x4, waiting for transfers between devices: none -> 43.3 us  [the longest x3 34.7 us: gather_obs(): other = lax.ppermute(block, 'obs', PARTNER)]
    pallas_call x0 -> x4, Pallas kernels: none -> 34.5 us  [the longest x1 11.8 us: means(): pl.pallas_call(mean_kernel, grid=(count,), in_specs=[pl.BlockSpec((1, TIL...]
  transfers between devices with their start and end apart: 6 -> 14, of which waited for: 6 -> 11; matrix products, arithmetic and copies ran while one was open for 1% -> 3% of each run, Pallas kernels for 0% -> 0%
where the time goes in v1:
time: 512 us; the launch traced here: 511 us
  waiting for transfers between devices  210 us (41%)
  blocking collectives  146 us (29%)
  starting transfers between devices  63.7 us (12%)
  Pallas kernels  34.5 us (7%)
  matrix products  21.8 us (4%)
  local copies, waits for them, and re-layouts  15.6 us (3%)
  between operations  13.8 us (3%)
  other arithmetic  5.95 us (1%)
    all_gather x1, blocking collectives, shards(): about = lax.all_gather(about, 'lev', axis=0, tiled=False)  64.5 us
    all_gather x1, waiting for transfers between devices, shards(): band = lax.all_gather(field, 'lat', axis=0, tiled=False)  63.5 us
    all_to_all x1, blocking collectives, shards(): pulled = lax.all_to_all(pulled.reshape(8, LEVELS, OBS), 'lev', 0, 0)  54.7 us
    all_gather x1, waiting for transfers between devices, shards(): band = lax.all_gather(chi, 'lat', axis=1, tiled=True)  41 us
    ppermute x3, waiting for transfers between devices, gather_obs(): other = lax.ppermute(block, 'obs', PARTNER)  34.7 us
    all_to_all x5, waiting for transfers between devices, to_all_y(): return lax.all_to_all(copies, 'obs', 0, 0, axis_index_groups=ALONG_Y)  27.5 us
    all_to_all x5, starting transfers between devices, to_all_y(): return lax.all_to_all(copies, 'obs', 0, 0, axis_index_groups=ALONG_Y)  20.4 us
    ppermute x3, starting transfers between devices, gather_obs(): other = lax.ppermute(block, 'obs', PARTNER)  18.2 us
  transfers between devices with their start and end apart: 14, of which 11 were waited for; matrix products, arithmetic and copies ran while one was open for 3% of the time, Pallas kernels for 0%

profile of v1, /device:TPU:1, one launch (start us, length us, event | category | flops | bytes accessed | tf_op | source)
XLA Modules:
  0.0 510.6 jit_solution(16088639144452154903)
XLA Ops:
  7.3 41.0 %all-gather.6.cloned.1.call-done = f32[17,128,256]{2,1,0:T(8,128)} async-done(((f32[17,16,256]{2,1,0:T(8,128)}), f32[17,128,256]{2,1,0:T(8,128)}) %all-gather.6.cloned.1.call-update) | async-done | bytes 2228240 | tf_op jit(solution)/shard_map/all_gather | solution.py:263
  48.3 2.8 fusion.28
  52.4 4.0 all-to-all-start
  56.4 12.5 %collective-permute-start = (f32[272,256]{1,0:T(8,128)S(1)}, f32[272,256]{1,0:T(8,128)}, u32[]{:S(2)}, u32[]{:S(2)}) collective-permute-start(f32[272,256]{1,0:T(8,128)S(1)} %pad_maximum_fusion.1), channel_id=1, source_target_pairs={{0,1},{1,0},{2,3},{3,2},{4,5},{5,4},{6,7},{7,6},{8,9},{9,8},{10,11... | collective-permute-start | bytes 835592 | tf_op jit(solution)/shard_map/ppermute | solution.py:214
  68.9 13.1 %collective-permute-done = f32[272,256]{1,0:T(8,128)} collective-permute-done((f32[272,256]{1,0:T(8,128)S(1)}, f32[272,256]{1,0:T(8,128)}, u32[]{:S(2)}, u32[]{:S(2)}) %collective-permute-start) | collective-permute-done | bytes 278560 | tf_op jit(solution)/shard_map/ppermute | solution.py:214
  84.2 4.0 all-to-all-start.1
  89.0 3.0 convolution_bitcast_fusion.3
  92.0 10.1 %all-to-all-done.1 = f32[4,272,256]{2,1,0:T(8,128)S(1)} async-done(((f32[4,272,256]{2,1,0:T(8,128)}), f32[4,272,256]{2,1,0:T(8,128)S(1)}, u32[]{:S(2)}, u32[]{:S(2)}) %all-to-all-start.1) | async-done | bytes 1114144 | tf_op jit(solution)/shard_map/all_to_all | solution.py:210
  102.1 8.3 %all-to-all-start.4 = ((f32[8,1,512]{2,1,0:T(1,128)}), f32[8,1,512]{2,1,0:T(1,128)S(1)}, u32[]{:S(2)}, u32[]{:S(2)}) async-start(f32[8,1,512]{2,1,0:T(1,128)} %reshape.51), calls=%async_computation.4 | async-start | bytes 32768 | tf_op jit(solution)/shard_map/all_to_all | solution.py:246
  112.4 11.7 %all-to-all-done.4 = f32[8,1,512]{2,1,0:T(1,128)S(1)} async-done(((f32[8,1,512]{2,1,0:T(1,128)}), f32[8,1,512]{2,1,0:T(1,128)S(1)}, u32[]{:S(2)}, u32[]{:S(2)}) %all-to-all-start.4) | async-done | bytes 16416 | tf_op jit(solution)/shard_map/all_to_all | solution.py:246
  125.2 4.4 all-to-all-start.2
  133.3 64.5 %all-gather.2 = f32[8,12,1024]{2,1,0:T(8,128)S(1)} all-gather(f32[1,12,1024]{2,1,0:T(8,128)S(1)} %maximum_bitcast_fusion), channel_id=2, replica_groups=mesh['lat'=8,'lev'=8,'obs'=8] {'lev'}, dimensions={0}, use_global_device_ids=true | all-gather | bytes 442368 | tf_op jit(solution)/shard_map/all_gather | solution.py:250
  199.1 4.5 all-to-all-start.3
  204.1 9.7 %all-to-all-done.3 = f32[4,272,256]{2,1,0:T(8,128)} async-done(((f32[4,272,256]{2,1,0:T(8,128)}), f32[4,272,256]{2,1,0:T(8,128)}, u32[]{:S(2)}, u32[]{:S(2)}) %all-to-all-start.3) | async-done | bytes 1114144 | tf_op jit(solution)/shard_map/all_to_all | solution.py:210
  215.6 5.3 %shard_map.109.slots_ref = f32[8,272,256]{2,1,0:T(8,128)S(1)} custom-call(f32[8,272,256]{2,1,0:T(8,128)S(1)} %pad_maximum_fusion.field_ref, s32[8,8,512]{2,1,0:T(8,128)S(1)} %add_bitcast_fusion.serve_ref), custom_call_target="tpu_custom_call" | custom-call | tf_op jit(solution)/shard_map/pallas_call | solution.py:77
  220.9 11.8 %shard_map.110 = f32[8,17,1024]{2,1,0:T(8,128)} custom-call(f32[8,272,256]{2,1,0:T(8,128)S(1)} %shard_map.109.slots_ref, s32[8,4,1024]{2,1,0:T(4,128)S(1)} %and_add_fusion.place_ref, f32[8,4,1024]{2,1,0:T(4,128)S(1)} %get-tuple-element.7.weight_ref), custom_call_target="tpu_custom_call" | custom-call | tf_op jit(solution)/shard_map/pallas_call | solution.py:113
  232.6 9.7 %all-to-all-start.5 = ((f32[8,17,1024]{2,1,0:T(8,128)}), f32[8,17,1024]{2,1,0:T(8,128)S(1)}, u32[]{:S(2)}, u32[]{:S(2)}) async-start(f32[8,17,1024]{2,1,0:T(8,128)} %shard_map.110), calls=%async_computation.5 | async-start | bytes 1572864 | tf_op jit(solution)/shard_map/all_to_all | solution.py:270
  246.6 17.2 %all-to-all-done.5 = f32[8,17,1024]{2,1,0:T(8,128)S(1)} async-done(((f32[8,17,1024]{2,1,0:T(8,128)}), f32[8,17,1024]{2,1,0:T(8,128)S(1)}, u32[]{:S(2)}, u32[]{:S(2)}) %all-to-all-start.5) | async-done | bytes 557088 | tf_op jit(solution)/shard_map/all_to_all | solution.py:270
  269.6 54.7 %all_to_all.55.grad_ref = f32[8,17,1024]{2,1,0:T(8,128)S(1)} all-to-all(f32[8,17,1024]{2,1,0:T(8,128)S(1)} %reshape.38), channel_id=1, replica_groups=mesh['lat'=8,'lev'=8,'obs'=8] {'lev'}, dimensions={0} | all-to-all | bytes 1114112 | tf_op jit(solution)/shard_map/all_to_all | solution.py:282
  324.3 10.9 %shard_map.111.slots_ref = f32[8,272,256]{2,1,0:T(8,128)S(1)} custom-call(f32[8,17,1024]{2,1,0:T(8,128)S(1)} %all_to_all.55.grad_ref, s32[8,4,1024]{2,1,0:T(4,128)S(1)} %and_add_fusion.place_ref, f32[8,4,1024]{2,1,0:T(4,128)S(1)} %get-tuple-element.7.weight_ref), custom_call_target="tpu_custom_call" | custom-call | tf_op jit(solution)/shard_map/pallas_call | solution.py:154
  335.2 6.5 %shard_map.112 = f32[8,272,256]{2,1,0:T(8,128)S(1)} custom-call(f32[8,272,256]{2,1,0:T(8,128)S(1)} %shard_map.111.slots_ref, s32[8,8,512]{2,1,0:T(8,128)S(1)} %add_bitcast_fusion.serve_ref), custom_call_target="tpu_custom_call" | custom-call | tf_op jit(solution)/shard_map/pallas_call | solution.py:195
  342.8 13.2 %all_to_all.56 = f32[4,272,256]{2,1,0:T(8,128)} all-to-all(f32[4,272,256]{2,1,0:T(8,128)S(1)} %get-tuple-element.5), channel_id=1, replica_groups={{0,2,4,6},{1,3,5,7},{8,10,12,14},{9,11,13,15},{16,18,20,22},{17,19,21,2..., dimensions={0} | all-to-all | bytes 2228224 | tf_op jit(solution)/shard_map/all_to_all | solution.py:285
  356.1 3.5 all-to-all-start.7
  361.7 3.5 collective-permute-start.2
  365.2 4.5 all-to-all-done.7
  369.8 8.6 %collective-permute-done.2 = f32[272,256]{1,0:T(8,128)} collective-permute-done((f32[272,256]{1,0:T(8,128)}, f32[272,256]{1,0:T(8,128)}, u32[]{:S(2)}, u32[]{:S(2)}) %collective-permute-start.2) | collective-permute-done | bytes 278560 | tf_op jit(solution)/shard_map/ppermute | solution.py:286
  379.3 3.5 collective-permute-start.3
  382.8 21.7 %collective-permute-done.3 = f32[272,256]{1,0:T(8,128)S(1)} collective-permute-done((f32[272,256]{1,0:T(8,128)S(1)}, f32[272,256]{1,0:T(8,128)S(1)}, u32[]{:S(2)}, u32[]{:S(2)}) %collective-permute-start.3) | collective-permute-done | bytes 278560 | tf_op jit(solution)/shard_map/ppermute | solution.py:214
  404.6 13.3 %all_to_all.57 = f32[4,272,256]{2,1,0:T(8,128)} all-to-all(f32[4,272,256]{2,1,0:T(8,128)S(1)} %broadcast_in_dim.17), channel_id=1, replica_groups={{0,2,4,6},{1,3,5,7},{8,10,12,14},{9,11,13,15},{16,18,20,22},{17,19,21,2..., dimensions={0} | all-to-all | bytes 2228224 | tf_op jit(solution)/shard_map/all_to_all | solution.py:210
  418.9 3.5 all-to-all-start.9
  424.8 7.7 %all-to-all-done.9 = f32[4,272,256]{2,1,0:T(8,128)S(1)} async-done(((f32[4,272,256]{2,1,0:T(8,128)}), f32[4,272,256]{2,1,0:T(8,128)S(1)}, u32[]{:S(2)}, u32[]{:S(2)}) %all-to-all-start.9) | async-done | bytes 1114144 | tf_op jit(solution)/shard_map/all_to_all | solution.py:210
  434.3 63.5 %all-gather.8.cloned.1.call-done = f32[2176,256]{1,0:T(8,128)} async-done(((f32[272,256]{1,0:T(8,128)}), f32[2176,256]{1,0:T(8,128)}) %all-gather.8.cloned.1.call-update) | async-done | bytes 2228240 | tf_op jit(solution)/shard_map/all_gather | solution.py:289
  (73 shorter events, 40.6 us)
Async XLA Ops:
  6.5 82.4 %copy-start = (f32[2048,256]{1,0:T(8,128)S(1)}, f32[2048,256]{1,0:T(8,128)}, u32[]{:S(2)}) copy-start(f32[2048,256]{1,0:T(8,128)} %param.12) | copy-start | bytes 6291460
  6.5 41.7 %all-gather.6.cloned.1.call-start = ((), (), s32[]{:S(2)}) async-start(), calls=%async_computation.11 | async-start | bytes 2506752 | tf_op jit(solution)/shard_map/all_gather | solution.py:263
  52.4 29.6 %all-to-all-start = ((f32[4,272,256]{2,1,0:T(8,128)}), f32[4,272,256]{2,1,0:T(8,128)S(1)}, u32[]{:S(2)}, u32[]{:S(2)}) async-start(f32[4,272,256]{2,1,0:T(8,128)} %broadcast_in_dim.12), calls=%async_computation | async-start | bytes 2228224 | tf_op jit(solution)/shard_map/all_to_all | solution.py:210
  56.4 25.6 %collective-permute-start = (f32[272,256]{1,0:T(8,128)S(1)}, f32[272,256]{1,0:T(8,128)}, u32[]{:S(2)}, u32[]{:S(2)}) collective-permute-start(f32[272,256]{1,0:T(8,128)S(1)} %pad_maximum_fusion.1), channel_id=1, source_target_pairs={{0,1},{1,0},{2,3},{3,2},{4,5},{5,4},{6,7},{7,6},{8,9},{9,8},{10,11... | collective-permute-start | bytes 835592 | tf_op jit(solution)/shard_map/ppermute | solution.py:214
  82.0 2.2 copy-start.1
  84.2 4.1 copy-start.5
  84.2 17.9 %all-to-all-start.1 = ((f32[4,272,256]{2,1,0:T(8,128)}), f32[4,272,256]{2,1,0:T(8,128)S(1)}, u32[]{:S(2)}, u32[]{:S(2)}) async-start(f32[4,272,256]{2,1,0:T(8,128)} %broadcast_in_dim.13), calls=%async_computation.1 | async-start | bytes 2228224 | tf_op jit(solution)/shard_map/all_to_all | solution.py:210
  102.1 22.0 %all-to-all-start.4 = ((f32[8,1,512]{2,1,0:T(1,128)}), f32[8,1,512]{2,1,0:T(1,128)S(1)}, u32[]{:S(2)}, u32[]{:S(2)}) async-start(f32[8,1,512]{2,1,0:T(1,128)} %reshape.51), calls=%async_computation.4 | async-start | bytes 32768 | tf_op jit(solution)/shard_map/all_to_all | solution.py:246
  125.2 4.4 copy-start.7
  125.2 5.8 %copy-start.6 = (f32[4,1024]{1,0:T(4,128)S(1)}, f32[4,1024]{1,0:T(4,128)}, u32[]{:S(2)}) copy-start(f32[4,1024]{1,0:T(4,128)} %param.19) | copy-start | bytes 49156
  125.2 72.8 %all-to-all-start.2 = ((f32[4,272,256]{2,1,0:T(8,128)}), f32[4,272,256]{2,1,0:T(8,128)}, u32[]{:S(2)}, u32[]{:S(2)}) async-start(f32[4,272,256]{2,1,0:T(8,128)} %broadcast_in_dim.14), calls=%async_computation.2 | async-start | bytes 2228224 | tf_op jit(solution)/shard_map/all_to_all | solution.py:210
  131.0 67.0 %collective-permute-start.1 = (f32[272,256]{1,0:T(8,128)S(1)}, f32[272,256]{1,0:T(8,128)S(1)}, u32[]{:S(2)}, u32[]{:S(2)}) collective-permute-start(f32[272,256]{1,0:T(8,128)S(1)} %fusion.10), channel_id=1, source_target_pairs={{0,1},{1,0},{2,3},{3,2},{4,5},{5,4},{6,7},{7,6},{8,9},{9,8},{10,11... | collective-permute-start | bytes 835592 | tf_op jit(solution)/shard_map/ppermute | solution.py:214
  199.1 14.7 %all-to-all-start.3 = ((f32[4,272,256]{2,1,0:T(8,128)}), f32[4,272,256]{2,1,0:T(8,128)}, u32[]{:S(2)}, u32[]{:S(2)}) async-start(f32[4,272,256]{2,1,0:T(8,128)} %broadcast_in_dim.15), calls=%async_computation.3 | async-start | bytes 2228224 | tf_op jit(solution)/shard_map/all_to_all | solution.py:210
  232.6 9.7 %copy-start.9 = (s32[300]{0:T(512)S(1)}, s32[300]{0:T(512)}, u32[]{:S(2)}) copy-start(s32[300]{0:T(512)} %param.16) | copy-start | bytes 3604
  232.6 12.9 %copy-start.8 = (f32[300]{0:T(512)S(1)}, f32[300]{0:T(512)}, u32[]{:S(2)}) copy-start(f32[300]{0:T(512)} %param.17) | copy-start | bytes 3604
  232.6 31.2 %all-to-all-start.5 = ((f32[8,17,1024]{2,1,0:T(8,128)}), f32[8,17,1024]{2,1,0:T(8,128)S(1)}, u32[]{:S(2)}, u32[]{:S(2)}) async-start(f32[8,17,1024]{2,1,0:T(8,128)} %shard_map.110), calls=%async_computation.5 | async-start | bytes 1572864 | tf_op jit(solution)/shard_map/all_to_all | solution.py:270
  264.7 1.8 copy-start.2
  356.1 13.6 %all-to-all-start.7 = ((f32[4,272,256]{2,1,0:T(8,128)}), f32[4,272,256]{2,1,0:T(8,128)S(1)}, u32[]{:S(2)}, u32[]{:S(2)}) async-start(f32[4,272,256]{2,1,0:T(8,128)} %get-tuple-element.6), calls=%async_computation.7 | async-start | bytes 2228224 | tf_op jit(solution)/shard_map/all_to_all | solution.py:287
  361.7 16.7 %collective-permute-start.2 = (f32[272,256]{1,0:T(8,128)}, f32[272,256]{1,0:T(8,128)}, u32[]{:S(2)}, u32[]{:S(2)}) collective-permute-start(f32[272,256]{1,0:T(8,128)} %reduce_sum.19), channel_id=1, source_target_pairs={{0,1},{1,0},{2,3},{3,2},{4,5},{5,4},{6,7},{7,6},{8,9},{9,8},{10,11... | collective-permute-start | bytes 835592 | tf_op jit(solution)/shard_map/ppermute | solution.py:286
  379.3 25.2 %collective-permute-start.3 = (f32[272,256]{1,0:T(8,128)S(1)}, f32[272,256]{1,0:T(8,128)S(1)}, u32[]{:S(2)}, u32[]{:S(2)}) collective-permute-start(f32[272,256]{1,0:T(8,128)S(1)} %add.47), channel_id=1, source_target_pairs={{0,1},{1,0},{2,3},{3,2},{4,5},{5,4},{6,7},{7,6},{8,9},{9,8},{10,11... | collective-permute-start | bytes 835592 | tf_op jit(solution)/shard_map/ppermute | solution.py:214
  418.9 13.6 %all-to-all-start.9 = ((f32[4,272,256]{2,1,0:T(8,128)}), f32[4,272,256]{2,1,0:T(8,128)S(1)}, u32[]{:S(2)}, u32[]{:S(2)}) async-start(f32[4,272,256]{2,1,0:T(8,128)} %broadcast_in_dim.16), calls=%async_computation.9 | async-start | bytes 2228224 | tf_op jit(solution)/shard_map/all_to_all | solution.py:210
  422.4 75.4 %all-gather.8.cloned.1.call-start = ((), (), s32[]{:S(2)}) async-start(), calls=%async_computation.12 | async-start | bytes 2506752 | tf_op jit(solution)/shard_map/all_gather | solution.py:289
  500.5 1.3 copy-start.3
  500.5 1.2 copy-start.4
Sparse Core Ops, SparseCore 0:
  9.5 38.7 all-gather.5
  434.4 63.3 all-gather.7

commit v2 on v1

v2 whole, which is shorter than its diff:
```python
import jax
import jax.numpy as jnp
from jax import lax
from jax.experimental import pallas as pl
from jax.experimental.pallas import tpu as pltpu
from jax.sharding import PartitionSpec as P

HIGHEST = lax.Precision.HIGHEST
F32 = jnp.float32
BF16 = jnp.bfloat16

LEVELS = 17
MAIN = 16
CELLS = 256
OWNER = 2 * MAIN
HALF = 4 * OWNER + 8
CAP = 64
VIEWERS = 8
OBS = 1024
FOOT = 4
BLOCK = 256
CHUNKS = 1
HALVES = 2 // CHUNKS
PARTS = 1
PART = OBS // PARTS
GROUP_MAIN = 4 * HALVES * MAIN
GROUP = GROUP_MAIN + 8
PARTNER = [(t, t ^ 1) for t in range(8)]
ALONG = [[0, 2, 4, 6], [1, 3, 5, 7]]
VMEM = 48 * 1024 * 1024


def params():
    return pltpu.CompilerParams(vmem_limit_bytes=VMEM)


def split(x):
    high = x.astype(BF16)
    return high, (x - high.astype(F32)).astype(BF16)


def split_rows(x):
    return jnp.concatenate(split(x), axis=0)


def one_hot(index, rows):
    place = lax.broadcasted_iota(jnp.int32, (rows, index.shape[1]), 0)
    return jnp.where(place == index, 1.0, 0.0).astype(BF16)


def dot(a, b):
    return lax.dot_general(a, b, (((1,), (0,)), ((), ())), preferred_element_type=F32)


def dot_nt(a, b):
    return lax.dot_general(a, b, (((1,), (1,)), ((), ())), preferred_element_type=F32)


def pick_kernel(field_ref, serve_ref, slots_ref):
    tile = pl.program_id(0)
    for half in range(HALVES):
        base = half * HALF
        last = field_ref[0, base + 4 * OWNER : base + HALF, :]
        mains = []
        lasts = []
        for quarter in range(4):
            index = serve_ref[0, 4 * half + quarter : 4 * half + quarter + 1, :]
            cell = jnp.bitwise_and(index, CELLS - 1)
            second = index >= CELLS
            start = base + quarter * OWNER
            rows = jnp.concatenate([field_ref[0, start : start + OWNER, :], last], axis=0)
            count = OWNER + 8
            both = dot(split_rows(rows), one_hot(cell, CELLS))
            picked = both[:count] + both[count:]
            mains.append(jnp.where(second, picked[MAIN:OWNER], picked[:MAIN]))
            at = OWNER + 2 * quarter
            lasts.append(jnp.where(second, picked[at + 1 : at + 2], picked[at : at + 1]))
        place = 4 * half + tile
        start = pl.multiple_of(place * MAIN, MAIN)
        for viewer in range(VIEWERS):
            lanes = slice(viewer * CAP, (viewer + 1) * CAP)
            slots_ref[viewer, pl.ds(start, MAIN), :] = jnp.concatenate([m[:, lanes] for m in mains], axis=1)
            slots_ref[viewer, pl.ds(GROUP_MAIN + place, 1), :] = jnp.concatenate([m[:, lanes] for m in lasts], axis=1)


def pick(field, serve):
    return pl.pallas_call(
        pick_kernel,
        grid=(4,),
        in_specs=[
            pl.BlockSpec((1, HALVES * HALF, CELLS), lambda y: (y, 0, 0)),
            pl.BlockSpec((1, 4 * HALVES, VIEWERS * CAP), lambda y: (y, 0, 0)),
        ],
        out_specs=pl.BlockSpec((VIEWERS, GROUP, BLOCK), lambda y: (0, 0, 0)),
        out_shape=jax.ShapeDtypeStruct((VIEWERS, GROUP, BLOCK), F32),
        compiler_params=params(),
    )(field, serve)


def mean_kernel(place_ref, weight_ref, *refs):
    slots, mean_ref = refs[:-1], refs[-1]
    mains = jnp.concatenate([s[0, :GROUP_MAIN, :] for s in slots], axis=0)
    lasts = jnp.concatenate([s[0, GROUP_MAIN : GROUP_MAIN + 4 * HALVES, :] for s in slots], axis=0)
    values = split_rows(jnp.concatenate([mains, lasts], axis=0))
    total = 16 * MAIN + 16
    for start in range(0, PART, BLOCK):
        lanes = slice(start, start + BLOCK)
        main = jnp.zeros((MAIN, BLOCK), F32)
        last = jnp.zeros((16, BLOCK), F32)
        for member in range(FOOT):
            place = place_ref[0, member : member + 1, lanes]
            low = jnp.bitwise_and(place, BLOCK - 1)
            high = lax.shift_right_logical(place, 8)
            weight = weight_ref[0, member : member + 1, lanes]
            both = dot(values, one_hot(low, BLOCK))
            picked = both[:total] + both[total:]
            masked = jnp.where(lax.broadcasted_iota(jnp.int32, (16, BLOCK), 0) == high, weight, 0.0)
            for part in range(16):
                main = main + picked[part * MAIN : (part + 1) * MAIN] * masked[part : part + 1]
            last = last + picked[16 * MAIN :] * masked
        mean_ref[0, :MAIN, lanes] = main
        mean_ref[0, MAIN:, lanes] = jnp.sum(last, axis=0, keepdims=True)


def means(slots, place, weight, part):
    return pl.pallas_call(
        mean_kernel,
        grid=(VIEWERS,),
        in_specs=[
            pl.BlockSpec((1, FOOT, PART), lambda v: (v, 0, part)),
            pl.BlockSpec((1, FOOT, PART), lambda v: (v, 0, part)),
        ]
        + [pl.BlockSpec((1, GROUP, BLOCK), lambda v: (v, 0, 0))] * len(slots),
        out_specs=pl.BlockSpec((1, LEVELS, PART), lambda v: (v, 0, 0)),
        out_shape=jax.ShapeDtypeStruct((VIEWERS, LEVELS, PART), F32),
        compiler_params=params(),
    )(place, weight, *slots)


def pull_kernel(mean_ref, hessian_ref, constant_ref, pulled_ref):
    mean = jnp.concatenate([mean_ref[m] for m in range(8)], axis=0)
    pulled = lax.dot_general(
        hessian_ref[...], mean, (((1,), (0,)), ((), ())), precision=HIGHEST, preferred_element_type=F32
    )
    pulled = pulled - constant_ref[...]
    for m in range(8):
        pulled_ref[m] = pulled[m * LEVELS : (m + 1) * LEVELS]


def pull(mean, hessian, constant, part):
    size = 8 * LEVELS
    return pl.pallas_call(
        pull_kernel,
        grid=(1,),
        in_specs=[
            pl.BlockSpec((8, LEVELS, PART), lambda i: (0, 0, 0)),
            pl.BlockSpec((size, size), lambda i: (0, 0)),
            pl.BlockSpec((size, PART), lambda i: (0, part)),
        ],
        out_specs=pl.BlockSpec((8, LEVELS, PART), lambda i: (0, 0, 0)),
        out_shape=jax.ShapeDtypeStruct((8, LEVELS, PART), F32),
        compiler_params=params(),
    )(mean, hessian, constant)


def spread_kernel(grad_ref, place_ref, weight_ref, *refs):
    groups = 2 * CHUNKS
    before, slots = refs[:-groups], refs[-groups:]
    total = jnp.zeros((2 * (16 * MAIN + 16), BLOCK), F32)
    for start in range(0, PART, BLOCK):
        lanes = slice(start, start + BLOCK)
        grad = grad_ref[0, :, lanes]
        for member in range(FOOT):
            place = place_ref[0, member : member + 1, lanes]
            low = jnp.bitwise_and(place, BLOCK - 1)
            high = lax.shift_right_logical(place, 8)
            scaled = grad * weight_ref[0, member : member + 1, lanes]
            hit = jnp.where(lax.broadcasted_iota(jnp.int32, (16, BLOCK), 0) == high, 1.0, 0.0)
            main_high, main_low = split(scaled[:MAIN])
            last_high, last_low = split(scaled[MAIN:] * hit)
            hits = [jnp.broadcast_to(hit[part : part + 1], (MAIN, BLOCK)).astype(BF16) for part in range(16)]
            rows = jnp.concatenate(
                [main_high * h for h in hits] + [last_high] + [main_low * h for h in hits] + [last_low], axis=0
            )
            total = total + dot_nt(rows, one_hot(low, BLOCK))
    total = total[: 16 * MAIN + 16] + total[16 * MAIN + 16 :]
    for group in range(groups):
        main = total[group * GROUP_MAIN : (group + 1) * GROUP_MAIN]
        at = 16 * MAIN + group * 4 * HALVES
        last = total[at : at + 4 * HALVES]
        if before:
            main = main + before[group][0, :GROUP_MAIN, :]
            last = last + before[group][0, GROUP_MAIN : GROUP_MAIN + 4 * HALVES, :]
        slots[group][0, :GROUP_MAIN, :] = main
        slots[group][0, GROUP_MAIN : GROUP_MAIN + 4 * HALVES, :] = last


def spread(grad, place, weight, before, part):
    groups = 2 * CHUNKS
    slots = pl.BlockSpec((1, GROUP, BLOCK), lambda v: (v, 0, 0))
    return pl.pallas_call(
        spread_kernel,
        grid=(VIEWERS,),
        in_specs=[
            pl.BlockSpec((1, LEVELS, PART), lambda v: (v, 0, 0)),
            pl.BlockSpec((1, FOOT, PART), lambda v: (v, 0, part)),
            pl.BlockSpec((1, FOOT, PART), lambda v: (v, 0, part)),
        ]
        + [slots] * len(before),
        out_specs=[slots] * groups,
        out_shape=[jax.ShapeDtypeStruct((VIEWERS, GROUP, BLOCK), F32)] * groups,
        compiler_params=params(),
    )(grad, place, weight, *before)


def put_kernel(slots_ref, serve_ref, field_ref):
    tile = pl.program_id(0)
    for half in range(HALVES):
        base = half * HALF
        place = 4 * half + tile
        start = pl.multiple_of(place * MAIN, MAIN)
        mains = [slots_ref[viewer, pl.ds(start, MAIN), :] for viewer in range(VIEWERS)]
        lasts = [slots_ref[viewer, pl.ds(GROUP_MAIN + place, 1), :] for viewer in range(VIEWERS)]
        tails = []
        for quarter in range(4):
            index = serve_ref[0, 4 * half + quarter : 4 * half + quarter + 1, :]
            cell = jnp.bitwise_and(index, CELLS - 1)
            second = index >= CELLS
            lanes = slice(quarter * CAP, (quarter + 1) * CAP)
            main = jnp.concatenate([m[:, lanes] for m in mains], axis=1)
            last = jnp.concatenate([m[:, lanes] for m in lasts], axis=1)
            row = lax.broadcasted_iota(jnp.int32, (8, VIEWERS * CAP), 0)
            tail = jnp.where(row == jnp.where(second, 1, 0), last, 0.0)
            rows = jnp.concatenate([jnp.where(second, 0.0, main), jnp.where(second, main, 0.0), tail], axis=0)
            count = OWNER + 8
            both = dot_nt(split_rows(rows), one_hot(cell, CELLS))
            back = both[:count] + both[count:]
            field_ref[0, base + quarter * OWNER : base + (quarter + 1) * OWNER, :] = back[:OWNER]
            tails.append(back[OWNER : OWNER + 2])
        field_ref[0, base + 4 * OWNER : base + HALF, :] = jnp.concatenate(tails, axis=0)


def put(slots, serve):
    return pl.pallas_call(
        put_kernel,
        grid=(4,),
        in_specs=[
            pl.BlockSpec((VIEWERS, GROUP, BLOCK), lambda y: (0, 0, 0)),
            pl.BlockSpec((1, 4 * HALVES, VIEWERS * CAP), lambda y: (y, 0, 0)),
        ],
        out_specs=pl.BlockSpec((1, HALVES * HALF, CELLS), lambda y: (y, 0, 0)),
        out_shape=jax.ShapeDtypeStruct((4, HALVES * HALF, CELLS), F32),
        compiler_params=params(),
    )(slots, serve)


def finish_kernel(chi_ref, lat_ref, *refs):
    bands, out_ref = refs[:-1], refs[-1]
    mains = []
    lasts = []
    for near_far in range(2):
        for half in range(2):
            ref = bands[near_far * CHUNKS + half // HALVES]
            base = (half % HALVES) * HALF
            for x in range(4):
                main = ref[x, base : base + 4 * OWNER, :].reshape(8, MAIN, CELLS)
                mains.append(jnp.swapaxes(main, 0, 1))
                lasts.append(ref[x, base + 4 * OWNER : base + HALF, :])
    for level in range(LEVELS):
        rows = jnp.concatenate([m[level] for m in mains] if level < MAIN else lasts, axis=0)
        out_ref[level] = chi_ref[level] + lax.dot_general(
            lat_ref[...], rows, (((1,), (0,)), ((), ())), precision=HIGHEST, preferred_element_type=F32
        )


def finish(chi, lat, bands):
    return pl.pallas_call(
        finish_kernel,
        out_shape=jax.ShapeDtypeStruct(chi.shape, F32),
        compiler_params=params(),
    )(chi, lat, *bands)


def to_all(block, axis):
    copies = jnp.broadcast_to(block[None], (4,) + block.shape)
    return lax.all_to_all(copies, axis, 0, 0, axis_index_groups=ALONG)


def gather_obs(block):
    other = lax.ppermute(block, "obs", PARTNER)
    return to_all(block, "obs"), to_all(other, "obs")


def times_lon(near, far, lon_near, lon_far):
    def product(tiles, matrix):
        return jnp.einsum("yrc,ycd->rd", tiles, matrix, precision=HIGHEST, preferred_element_type=F32)

    return product(near, lon_near) + product(far, lon_far)


def shards(
    chi,
    mat_lon,
    mat_lat,
    mat_vert,
    chan_table,
    chan_map,
    error_weight,
    innovation,
    foot_weight,
    foot_slot,
    serve_cols,
):
    half = lax.axis_index("obs") % 2
    core = lax.axis_index("lat") % 2

    def near_far(x, axis, which):
        near = lax.dynamic_index_in_dim(x, which, axis, keepdims=False)
        far = lax.dynamic_index_in_dim(x, 1 - which, axis, keepdims=False)
        return near, far

    feet = jnp.concatenate([foot_slot.astype(F32), foot_weight], axis=0)
    feet = lax.all_to_all(jnp.broadcast_to(feet[None], (8,) + feet.shape), "lev", 0, 0)
    serve = serve_cols[0, 0].astype(F32).reshape(8, 8, CAP).transpose(1, 0, 2)
    serve = lax.all_to_all(serve, "obs", 0, 0)
    serve = serve.reshape(8, VIEWERS * CAP)

    band_near = to_all(chi, "lat")
    band_far = lax.ppermute(band_near, "lat", PARTNER)
    lat_near, lat_far = near_far(mat_lat.reshape(16, 4, 2, 16), 2, core)
    field = jnp.einsum(
        "ixr,xlrk->ilk", lat_near, band_near, precision=HIGHEST, preferred_element_type=F32
    ) + jnp.einsum("ixr,xlrk->ilk", lat_far, band_far, precision=HIGHEST, preferred_element_type=F32)
    feet, serve, field = lax.optimization_barrier((feet, serve, field))
    chunks = []
    for chunk in range(CHUNKS):
        pieces = []
        for place in range(chunk * HALVES, (chunk + 1) * HALVES):
            rows = field[8 * place : 8 * place + 8]
            pieces += [rows[:, :MAIN].reshape(8 * MAIN, CELLS), rows[:, MAIN]]
        chunks.append(jnp.concatenate(pieces, axis=0))

    serve = lax.all_to_all(jnp.broadcast_to(serve[None], (8,) + serve.shape), "lev", 0, 0)
    serve = serve.reshape(8, 4, 2, VIEWERS * CAP).astype(jnp.int32)
    serves = [s.transpose(1, 0, 2) for s in near_far(serve, 2, half)]
    slot = feet[:, :4].astype(jnp.int32)
    weight = feet[:, 4:]
    tile = (slot >> 6) & 7
    far = (tile & 1) ^ half
    slab = slot >> 9
    if CHUNKS == 2:
        group = 2 * (slab >> 2) + far
    else:
        group = 2 * far + (slab >> 2)
    place = (4 * group + (tile >> 1)) * BLOCK + (slab & 3) * CAP + (slot & (CAP - 1))

    lons = near_far(mat_lon.reshape(4, 2, CELLS, CELLS), 1, half)
    matches = (
        chan_map[:, None] == jnp.arange(chan_table.shape[0], dtype=jnp.int32)[None, :]
    ).astype(F32)
    selected = jnp.dot(matches, chan_table, precision=HIGHEST, preferred_element_type=F32)
    selected = jnp.dot(selected, mat_vert, precision=HIGHEST, preferred_element_type=F32)
    scaled = error_weight[:, None] * selected
    hessian = jnp.dot(selected.T, scaled, precision=HIGHEST, preferred_element_type=F32)
    constant = jnp.dot(scaled.T, innovation, precision=HIGHEST, preferred_element_type=F32)

    chunks = [times_lon(*gather_obs(chunk), *lons) for chunk in chunks]
    chunks, serves, place, weight, hessian, constant = lax.optimization_barrier(
        (chunks, serves, place, weight, hessian, constant)
    )

    def serve_of(which, chunk):
        return serves[which][:, 4 * HALVES * chunk : 4 * HALVES * (chunk + 1)]

    slots = []
    for chunk in range(CHUNKS):
        for which, tiles in enumerate(gather_obs(chunks[chunk])):
            slots.append(pick(tiles, serve_of(which, chunk)))

    back = []
    for part in range(PARTS):
        mean = lax.all_to_all(means(slots, place, weight, part), "lev", 0, 0)
        back.append(lax.all_to_all(pull(mean, hessian, constant, part), "lev", 0, 0))
    slots = []
    for part in range(PARTS):
        slots = spread(back[part], place, weight, slots, part)

    bands = []
    for chunk in range(CHUNKS):
        tiles = put(slots[2 * chunk + 1], serve_of(1, chunk))
        far = jnp.sum(lax.all_to_all(tiles, "obs", 0, 0, axis_index_groups=ALONG), axis=0)
        far = lax.ppermute(far, "obs", PARTNER)
        tiles = put(slots[2 * chunk], serve_of(0, chunk))
        near = jnp.sum(lax.all_to_all(tiles, "obs", 0, 0, axis_index_groups=ALONG), axis=0)
        field = times_lon(*gather_obs(near + far), *lons)
        band_near = to_all(field, "lat")
        bands.append((band_near, lax.ppermute(band_near, "lat", PARTNER)))
    lat = jnp.stack(
        [m.reshape(16, 4, 2, 8).transpose(0, 2, 1, 3) for m in (lat_near, lat_far)], axis=1
    ).reshape(16, 128)
    return finish(chi, lat, [b[0] for b in bands] + [b[1] for b in bands])


def solution(mesh):
    in_specs = (
        P("lev", "lat", "obs"),
        P(None, "obs"),
        P("lat", None),
        P(),
        P(),
        P(),
        P(),
        P(None, ("lat", "lev", "obs")),
        P(None, ("lat", "lev", "obs")),
        P(None, ("lat", "lev", "obs")),
        P("lat", ("lev", "obs"), None, None),
    )
    out_specs = P("lev", "lat", "obs")
    return jax.shard_map(shards, mesh=mesh, in_specs=in_specs, out_specs=out_specs, check_vma=False)
```

time: 512 us -> 478 us (0.934)
  the two profiles are of different devices: /device:TPU:1 before, /device:TPU:33 now
where the time goes in v2:
time: 478 us; the launch traced here: 476 us
  waiting for transfers between devices  171 us (36%)
  blocking collectives  135 us (28%)
  starting transfers between devices  78 us (16%)
  Pallas kernels  40.7 us (9%)
  local copies, waits for them, and re-layouts  23.6 us (5%)
  matrix products  19.6 us (4%)
  other arithmetic  8.07 us (2%)
    ppermute x3, waiting for transfers between devices, gather_obs(): other = lax.ppermute(block, 'obs', PARTNER)  74 us
    all_to_all x3, blocking collectives, to_all(): return lax.all_to_all(copies, axis, 0, 0, axis_index_groups=ALONG)  52.4 us
    all_to_all x1, blocking collectives, shards(): lax.all_to_all(pull(mean, hessian, constant, part), 'lev', 0, 0)  43.7 us
    all_to_all x1, blocking collectives, shards(): mean = lax.all_to_all(means(slots, place, weight, part), 'lev', 0, 0)  39.1 us
    all_to_all x5, waiting for transfers between devices, to_all(): return lax.all_to_all(copies, axis, 0, 0, axis_index_groups=ALONG)  29.4 us
    ppermute x1, waiting for transfers between devices, shards(): far = lax.ppermute(far, 'obs', PARTNER)  26.6 us
    all_to_all x5, starting transfers between devices, to_all(): return lax.all_to_all(copies, axis, 0, 0, axis_index_groups=ALONG)  19.3 us
    all_to_all x1, starting transfers between devices, shards(): serve = lax.all_to_all(serve, 'obs', 0, 0)  16.5 us
  transfers between devices with their start and end apart: 16, of which 12 were waited for; matrix products, arithmetic and copies ran while one was open for 7% of the time, Pallas kernels for 1%

profile of v2, /device:TPU:33, one launch (start us, length us, event | category | flops | bytes accessed | tf_op | source)
XLA Modules:
  0.0 476.3 jit_solution(6430641806206575711)
XLA Ops:
  1.2 18.4 %all_to_all.75 = f32[4,17,16,256]{3,2,1,0:T(8,128)S(1)} all-to-all(f32[4,17,16,256]{3,2,1,0:T(8,128)S(1)} %broadcast_in_dim.21), channel_id=1, replica_groups={{0,128,256,384},{64,192,320,448},{1,129,257,385},{65,193,321,449},{2,13..., dimensions={0} | all-to-all | bytes 2228224 | tf_op jit(solution)/shard_map/all_to_all | solution.py:286
  20.8 4.2 collective-permute-start
  25.7 16.5 %all-to-all-start.1 = ((f32[8,1,512]{2,1,0:T(1,128)}), f32[8,1,512]{2,1,0:T(1,128)S(1)}, u32[]{:S(2)}, u32[]{:S(2)}) async-start(f32[8,1,512]{2,1,0:T(1,128)} %reshape.59), calls=%async_computation.1 | async-start | bytes 32768 | tf_op jit(solution)/shard_map/all_to_all | solution.py:325
  42.3 13.7 %all-to-all-done.1 = f32[8,1,512]{2,1,0:T(1,128)S(1)} async-done(((f32[8,1,512]{2,1,0:T(1,128)}), f32[8,1,512]{2,1,0:T(1,128)S(1)}, u32[]{:S(2)}, u32[]{:S(2)}) %all-to-all-start.1) | async-done | bytes 16416 | tf_op jit(solution)/shard_map/all_to_all | solution.py:325
  56.8 5.5 %all-to-all-start = ((f32[8,8,1024]{2,1,0:T(8,128)}), f32[8,8,1024]{2,1,0:T(8,128)S(1)}, u32[]{:S(2)}, u32[]{:S(2)}) async-start(f32[8,8,1024]{2,1,0:T(8,128)} %broadcast_in_dim.20), calls=%async_computation | async-start | bytes 524288 | tf_op jit(solution)/shard_map/all_to_all | solution.py:323
  74.9 9.4 %all-to-all-start.5 = ((f32[8,8,512]{2,1,0:T(8,128)}), f32[8,8,512]{2,1,0:T(8,128)S(1)}, u32[]{:S(2)}, u32[]{:S(2)}) async-start(f32[8,8,512]{2,1,0:T(8,128)} %broadcast_in_dim.24), calls=%async_computation.5 | async-start | bytes 262144 | tf_op jit(solution)/shard_map/all_to_all | solution.py:343
  85.1 7.9 %all-to-all-done.5 = f32[8,8,512]{2,1,0:T(8,128)S(1)} async-done(((f32[8,8,512]{2,1,0:T(8,128)}), f32[8,8,512]{2,1,0:T(8,128)S(1)}, u32[]{:S(2)}, u32[]{:S(2)}) %all-to-all-start.5) | async-done | bytes 131104 | tf_op jit(solution)/shard_map/all_to_all | solution.py:343
  95.1 3.7 all-to-all-start.3
  107.7 29.3 %collective-permute-done.1 = f32[272,256]{1,0:T(8,128)} collective-permute-done((f32[272,256]{1,0:T(8,128)}, f32[272,256]{1,0:T(8,128)}, u32[]{:S(2)}, u32[]{:S(2)}) %collective-permute-start.1) | collective-permute-done | bytes 278560 | tf_op jit(solution)/shard_map/ppermute | solution.py:290
  139.1 4.2 all-to-all-start.4
  151.2 6.2 %all-to-all-done.4 = f32[4,272,256]{2,1,0:T(8,128)S(1)} async-done(((f32[4,272,256]{2,1,0:T(8,128)}), f32[4,272,256]{2,1,0:T(8,128)S(1)}, u32[]{:S(2)}, u32[]{:S(2)}) %all-to-all-start.4) | async-done | bytes 1114144 | tf_op jit(solution)/shard_map/all_to_all | solution.py:286
  161.2 3.5 all-to-all-start.6
  168.0 19.4 %collective-permute-done.2 = f32[272,256]{1,0:T(8,128)} collective-permute-done((f32[272,256]{1,0:T(8,128)}, f32[272,256]{1,0:T(8,128)}, u32[]{:S(2)}, u32[]{:S(2)}) %collective-permute-start.2) | collective-permute-done | bytes 278560 | tf_op jit(solution)/shard_map/ppermute | solution.py:290
  189.4 4.4 all-to-all-start.7
  197.5 11.3 %all-to-all-done.7.field_ref = f32[4,272,256]{2,1,0:T(8,128)} async-done(((f32[4,272,256]{2,1,0:T(8,128)}), f32[4,272,256]{2,1,0:T(8,128)}, u32[]{:S(2)}, u32[]{:S(2)}) %all-to-all-start.7) | async-done | bytes 1114144 | tf_op jit(solution)/shard_map/all_to_all | solution.py:286
  209.6 4.0 shard_map.110.refs_1_
  213.7 11.1 %shard_map.111 = f32[8,17,1024]{2,1,0:T(8,128)S(1)} custom-call(s32[8,4,1024]{2,1,0:T(4,128)S(1)} %and_add_fusion.place_ref, f32[8,4,1024]{2,1,0:T(4,128)S(1)} %slice.29.weight_ref, f32[8,136,256]{2,1,0:T(8,128)S(1)} %copy-done.2, f32[8,136,256]{2,1,0:T(8,128)S(1)} %shard_map.110.refs_1_), custom_call_target="tpu_custom_call" | custom-call | tf_op jit(solution)/shard_map/pallas_call | solution.py:126
  224.8 39.1 %all_to_all.76.mean_ref = f32[8,17,1024]{2,1,0:T(8,128)S(1)} all-to-all(f32[8,17,1024]{2,1,0:T(8,128)S(1)} %shard_map.111), channel_id=1, replica_groups=mesh['lat'=8,'lev'=8,'obs'=8] {'lev'}, dimensions={0} | all-to-all | bytes 1114112 | tf_op jit(solution)/shard_map/all_to_all | solution.py:382
  264.6 43.7 %all_to_all.77.grad_ref = f32[8,17,1024]{2,1,0:T(8,128)S(1)} all-to-all(f32[8,17,1024]{2,1,0:T(8,128)S(1)} %shard_map.112), channel_id=1, replica_groups=mesh['lat'=8,'lev'=8,'obs'=8] {'lev'}, dimensions={0} | all-to-all | bytes 1114112 | tf_op jit(solution)/shard_map/all_to_all | solution.py:383
  308.4 10.9 %shard_map.113 = (f32[8,136,256]{2,1,0:T(8,128)S(1)}, f32[8,136,256]{2,1,0:T(8,128)S(1)}) custom-call(f32[8,17,1024]{2,1,0:T(8,128)S(1)} %all_to_all.77.grad_ref, s32[8,4,1024]{2,1,0:T(4,128)S(1)} %and_add_fusion.place_ref, f32[8,4,1024]{2,1,0:T(4,128)S(1)} %slice.29.weight_ref), custom_call_target="tpu_custom_call" | custom-call | tf_op jit(solution)/shard_map/pallas_call | solution.py:201
  319.3 4.0 shard_map.115
  323.3 4.3 all-to-all-start.11
  327.5 4.0 shard_map.114
  331.5 8.7 %all-to-all-done.11 = f32[4,272,256]{2,1,0:T(8,128)} async-done(((f32[4,272,256]{2,1,0:T(8,128)}), f32[4,272,256]{2,1,0:T(8,128)}, u32[]{:S(2)}, u32[]{:S(2)}) %all-to-all-start.11) | async-done | bytes 1114144 | tf_op jit(solution)/shard_map/all_to_all | solution.py:391
  340.2 3.5 all-to-all-start.10
  347.7 7.4 %all-to-all-done.10 = f32[4,272,256]{2,1,0:T(8,128)S(1)} async-done(((f32[4,272,256]{2,1,0:T(8,128)}), f32[4,272,256]{2,1,0:T(8,128)S(1)}, u32[]{:S(2)}, u32[]{:S(2)}) %all-to-all-start.10) | async-done | bytes 1114144 | tf_op jit(solution)/shard_map/all_to_all | solution.py:394
  355.2 26.6 %collective-permute-done.3 = f32[272,256]{1,0:T(8,128)} collective-permute-done((f32[272,256]{1,0:T(8,128)}, f32[272,256]{1,0:T(8,128)}, u32[]{:S(2)}, u32[]{:S(2)}) %collective-permute-start.3) | collective-permute-done | bytes 278560 | tf_op jit(solution)/shard_map/ppermute | solution.py:392
  384.8 25.4 %collective-permute-done.4 = f32[272,256]{1,0:T(8,128)S(1)} collective-permute-done((f32[272,256]{1,0:T(8,128)S(1)}, f32[272,256]{1,0:T(8,128)S(1)}, u32[]{:S(2)}, u32[]{:S(2)}) %collective-permute-start.4) | collective-permute-done | bytes 278560 | tf_op jit(solution)/shard_map/ppermute | solution.py:290
  410.3 18.4 %all_to_all.78 = f32[4,272,256]{2,1,0:T(8,128)} all-to-all(f32[4,272,256]{2,1,0:T(8,128)S(1)} %broadcast_in_dim.28), channel_id=1, replica_groups={{0,2,4,6},{1,3,5,7},{8,10,12,14},{9,11,13,15},{16,18,20,22},{17,19,21,2..., dimensions={0} | all-to-all | bytes 2228224 | tf_op jit(solution)/shard_map/all_to_all | solution.py:286
  435.6 11.9 %all-to-all-done.12 = f32[4,272,256]{2,1,0:T(8,128)S(1)} async-done(((f32[4,272,256]{2,1,0:T(8,128)}), f32[4,272,256]{2,1,0:T(8,128)S(1)}, u32[]{:S(2)}, u32[]{:S(2)}) %all-to-all-start.12) | async-done | bytes 1114144 | tf_op jit(solution)/shard_map/all_to_all | solution.py:286
  448.7 15.6 %all_to_all.79.refs_0_ = f32[4,272,256]{2,1,0:T(8,128)S(1)} all-to-all(f32[4,272,256]{2,1,0:T(8,128)S(1)} %broadcast_in_dim.29), channel_id=1, replica_groups={{0,128,256,384},{64,192,320,448},{1,129,257,385},{65,193,321,449},{2,13..., dimensions={0} | all-to-all | bytes 2228224 | tf_op jit(solution)/shard_map/all_to_all | solution.py:286
  464.3 5.6 %collective-permute-start.5 = (f32[4,272,256]{2,1,0:T(8,128)S(1)}, f32[4,272,256]{2,1,0:T(8,128)}, u32[]{:S(2)}, u32[]{:S(2)}) collective-permute-start(f32[4,272,256]{2,1,0:T(8,128)S(1)} %all_to_all.79.refs_0_), channel_id=1, source_target_pairs={{0,64},{64,0},{128,192},{192,128},{256,320},{320,256},{384,448},{4... | collective-permute-start | bytes 3342344 | tf_op jit(solution)/shard_map/ppermute | solution.py:397
  (108 shorter events, 74.2 us)
Async XLA Ops:
  0.0 148.1 %copy-start = (f32[2048,256]{1,0:T(8,128)S(1)}, f32[2048,256]{1,0:T(8,128)}, u32[]{:S(2)}) copy-start(f32[2048,256]{1,0:T(8,128)} %param.12) | copy-start | bytes 6291460
  19.7 5.3 %copy-start.17 = (s32[1,1,64,64]{3,2,1,0:T(8,128)S(1)}, s32[1,1,64,64]{3,2,1,0:T(8,128)}, u32[]{:S(2)}) copy-start(s32[1,1,64,64]{3,2,1,0:T(8,128)} %param.21) | copy-start | bytes 49156
  19.7 22.6 %copy-start.18 = (s32[4,1024]{1,0:T(4,128)S(1)}, s32[4,1024]{1,0:T(4,128)}, u32[]{:S(2)}) copy-start(s32[4,1024]{1,0:T(4,128)} %param.20) | copy-start | bytes 49156
  19.7 22.6 %copy-start.19 = (f32[4,1024]{1,0:T(4,128)S(1)}, f32[4,1024]{1,0:T(4,128)}, u32[]{:S(2)}) copy-start(f32[4,1024]{1,0:T(4,128)} %param.19) | copy-start | bytes 49156
  20.8 41.4 %copy-start.21 = (f32[16,128]{1,0:T(8,128)S(1)}, f32[16,128]{1,0:T(8,128)}, u32[]{:S(2)}) copy-start(f32[16,128]{1,0:T(8,128)} %param.13) | copy-start | bytes 24580
  20.8 47.8 %collective-permute-start = (f32[4,17,16,256]{3,2,0,1:T(8,128)}, f32[4,17,16,256]{3,2,0,1:T(8,128)}, u32[]{:S(2)}, u32[]{:S(2)}) collective-permute-start(f32[4,17,16,256]{3,2,0,1:T(8,128)} %copy.41), channel_id=1, source_target_pairs={{0,64},{64,0},{128,192},{192,128},{256,320},{320,256},{384,448},{4... | collective-permute-start | bytes 3342344 | tf_op jit(solution)/shard_map/ppermute | solution.py:329
  25.7 30.3 %all-to-all-start.1 = ((f32[8,1,512]{2,1,0:T(1,128)}), f32[8,1,512]{2,1,0:T(1,128)S(1)}, u32[]{:S(2)}, u32[]{:S(2)}) async-start(f32[8,1,512]{2,1,0:T(1,128)} %reshape.59), calls=%async_computation.1 | async-start | bytes 32768 | tf_op jit(solution)/shard_map/all_to_all | solution.py:325
  56.8 17.4 %all-to-all-start = ((f32[8,8,1024]{2,1,0:T(8,128)}), f32[8,8,1024]{2,1,0:T(8,128)S(1)}, u32[]{:S(2)}, u32[]{:S(2)}) async-start(f32[8,8,1024]{2,1,0:T(8,128)} %broadcast_in_dim.20), calls=%async_computation | async-start | bytes 524288 | tf_op jit(solution)/shard_map/all_to_all | solution.py:323
  64.0 7.1 %copy-start.12 = (f32[16,4,1,16]{3,2,1,0:T(1,128)}, f32[16,4,1,16]{3,2,1,0:T(1,128)S(1)}, u32[]{:S(2)}) copy-start(f32[16,4,1,16]{3,2,1,0:T(1,128)S(1)} %get-tuple-element.35) | copy-start | bytes 12292
  64.0 7.1 %copy-start.14 = (f32[16,4,1,16]{3,2,1,0:T(1,128)}, f32[16,4,1,16]{3,2,1,0:T(1,128)S(1)}, u32[]{:S(2)}) copy-start(f32[16,4,1,16]{3,2,1,0:T(1,128)S(1)} %get-tuple-element.36) | copy-start | bytes 12292
  74.2 20.9 %copy-start.10 = (f32[8,8,1024]{2,1,0:T(8,128)}, f32[8,8,1024]{2,1,0:T(8,128)S(1)}, u32[]{:S(2)}) copy-start(f32[8,8,1024]{2,1,0:T(8,128)S(1)} %all-to-all-done) | copy-start | bytes 786436
  74.9 18.1 %all-to-all-start.5 = ((f32[8,8,512]{2,1,0:T(8,128)}), f32[8,8,512]{2,1,0:T(8,128)S(1)}, u32[]{:S(2)}, u32[]{:S(2)}) async-start(f32[8,8,512]{2,1,0:T(8,128)} %broadcast_in_dim.24), calls=%async_computation.5 | async-start | bytes 262144 | tf_op jit(solution)/shard_map/all_to_all | solution.py:343
  95.1 41.8 %all-to-all-start.3 = ((f32[4,272,256]{2,1,0:T(8,128)}), f32[4,272,256]{2,1,0:T(8,128)S(1)}, u32[]{:S(2)}, u32[]{:S(2)}) async-start(f32[4,272,256]{2,1,0:T(8,128)} %broadcast_in_dim.22), calls=%async_computation.3 | async-start | bytes 2228224 | tf_op jit(solution)/shard_map/all_to_all | solution.py:286
  98.8 5.7 %copy-start.20 = (f32[300]{0:T(512)S(1)}, f32[300]{0:T(512)}, u32[]{:S(2)}) copy-start(f32[300]{0:T(512)} %param.17) | copy-start | bytes 3604
  100.5 36.4 %collective-permute-start.1 = (f32[272,256]{1,0:T(8,128)}, f32[272,256]{1,0:T(8,128)}, u32[]{:S(2)}, u32[]{:S(2)}) collective-permute-start(f32[272,256]{1,0:T(8,128)} %pad_maximum_fusion), channel_id=1, source_target_pairs={{0,1},{1,0},{2,3},{3,2},{4,5},{5,4},{6,7},{7,6},{8,9},{9,8},{10,11... | collective-permute-start | bytes 835592 | tf_op jit(solution)/shard_map/ppermute | solution.py:290
  139.1 18.2 %all-to-all-start.4 = ((f32[4,272,256]{2,1,0:T(8,128)}), f32[4,272,256]{2,1,0:T(8,128)S(1)}, u32[]{:S(2)}, u32[]{:S(2)}) async-start(f32[4,272,256]{2,1,0:T(8,128)} %broadcast_in_dim.23), calls=%async_computation.4 | async-start | bytes 2228224 | tf_op jit(solution)/shard_map/all_to_all | solution.py:286
  161.2 26.1 %all-to-all-start.6 = ((f32[4,272,256]{2,1,0:T(8,128)}), f32[4,272,256]{2,1,0:T(8,128)S(1)}, u32[]{:S(2)}, u32[]{:S(2)}) async-start(f32[4,272,256]{2,1,0:T(8,128)} %broadcast_in_dim.25), calls=%async_computation.6 | async-start | bytes 2228224 | tf_op jit(solution)/shard_map/all_to_all | solution.py:286
  164.7 22.6 %collective-permute-start.2 = (f32[272,256]{1,0:T(8,128)}, f32[272,256]{1,0:T(8,128)}, u32[]{:S(2)}, u32[]{:S(2)}) collective-permute-start(f32[272,256]{1,0:T(8,128)} %copy-done.9), channel_id=1, source_target_pairs={{0,1},{1,0},{2,3},{3,2},{4,5},{5,4},{6,7},{7,6},{8,9},{9,8},{10,11... | collective-permute-start | bytes 835592 | tf_op jit(solution)/shard_map/ppermute | solution.py:290
  189.4 19.4 %all-to-all-start.7 = ((f32[4,272,256]{2,1,0:T(8,128)}), f32[4,272,256]{2,1,0:T(8,128)}, u32[]{:S(2)}, u32[]{:S(2)}) async-start(f32[4,272,256]{2,1,0:T(8,128)} %broadcast_in_dim.26), calls=%async_computation.7 | async-start | bytes 2228224 | tf_op jit(solution)/shard_map/all_to_all | solution.py:286
  209.6 4.0 copy-start.2
  224.8 39.2 %copy-start.3 = (f32[136,1024]{1,0:T(8,128)S(1)}, f32[136,1024]{1,0:T(8,128)}, u32[]{:S(2)}) copy-start(f32[136,1024]{1,0:T(8,128)} %fusion.13.constant_ref) | copy-start | bytes 1671172
  224.8 39.2 %copy-start.7 = (f32[136,136]{1,0:T(8,128)S(1)}, f32[136,136]{1,0:T(8,128)}, u32[]{:S(2)}) copy-start(f32[136,136]{1,0:T(8,128)} %fusion.15.hessian_ref) | copy-start | bytes 221956
  264.6 54.7 %copy-start.6 = (s32[4,8,512]{2,1,0:T(8,128)S(1)}, s32[4,8,512]{2,1,0:T(8,128)}, u32[]{:S(2)}) copy-start(s32[4,8,512]{2,1,0:T(8,128)} %get-tuple-element.24.serve_ref) | copy-start | bytes 196612
  323.3 16.9 %all-to-all-start.11 = ((f32[4,272,256]{2,1,0:T(8,128)}), f32[4,272,256]{2,1,0:T(8,128)}, u32[]{:S(2)}, u32[]{:S(2)}) async-start(f32[4,272,256]{2,1,0:T(8,128)} %shard_map.115), calls=%async_computation.11 | async-start | bytes 2228224 | tf_op jit(solution)/shard_map/all_to_all | solution.py:391
  340.2 14.9 %all-to-all-start.10 = ((f32[4,272,256]{2,1,0:T(8,128)}), f32[4,272,256]{2,1,0:T(8,128)S(1)}, u32[]{:S(2)}, u32[]{:S(2)}) async-start(f32[4,272,256]{2,1,0:T(8,128)} %shard_map.114), calls=%async_computation.10 | async-start | bytes 2228224 | tf_op jit(solution)/shard_map/all_to_all | solution.py:394
  345.8 36.0 %collective-permute-start.3 = (f32[272,256]{1,0:T(8,128)}, f32[272,256]{1,0:T(8,128)}, u32[]{:S(2)}, u32[]{:S(2)}) collective-permute-start(f32[272,256]{1,0:T(8,128)} %reduce_sum.19), channel_id=1, source_target_pairs={{0,1},{1,0},{2,3},{3,2},{4,5},{5,4},{6,7},{7,6},{8,9},{9,8},{10,11... | collective-permute-start | bytes 835592 | tf_op jit(solution)/shard_map/ppermute | solution.py:392
  382.7 27.5 %collective-permute-start.4 = (f32[272,256]{1,0:T(8,128)S(1)}, f32[272,256]{1,0:T(8,128)S(1)}, u32[]{:S(2)}, u32[]{:S(2)}) collective-permute-start(f32[272,256]{1,0:T(8,128)S(1)} %add.62), channel_id=1, source_target_pairs={{0,1},{1,0},{2,3},{3,2},{4,5},{5,4},{6,7},{7,6},{8,9},{9,8},{10,11... | collective-permute-start | bytes 835592 | tf_op jit(solution)/shard_map/ppermute | solution.py:290
  429.7 17.8 %all-to-all-start.12 = ((f32[4,272,256]{2,1,0:T(8,128)}), f32[4,272,256]{2,1,0:T(8,128)S(1)}, u32[]{:S(2)}, u32[]{:S(2)}) async-start(f32[4,272,256]{2,1,0:T(8,128)} %broadcast_in_dim.27), calls=%async_computation.12 | async-start | bytes 2228224 | tf_op jit(solution)/shard_map/all_to_all | solution.py:286
  448.6 21.2 %copy-start.13 = (f32[16,4,1,16]{3,2,1,0:T(1,128)S(1)}, f32[16,4,1,16]{3,2,1,0:T(1,128)}, u32[]{:S(2)}) copy-start(f32[16,4,1,16]{3,2,1,0:T(1,128)} %copy-done.12) | copy-start | bytes 12292
  448.6 21.9 %copy-start.15 = (f32[16,4,1,16]{3,2,1,0:T(1,128)S(1)}, f32[16,4,1,16]{3,2,1,0:T(1,128)}, u32[]{:S(2)}) copy-start(f32[16,4,1,16]{3,2,1,0:T(1,128)} %copy-done.14) | copy-start | bytes 12292
  448.7 24.3 %copy-start.4 = (f32[17,16,256]{2,1,0:T(8,128)S(1)}, f32[17,16,256]{2,1,0:T(8,128)}, u32[]{:S(2)}) copy-start(f32[17,16,256]{2,1,0:T(8,128)} %chi_ref.1) | copy-start | bytes 835588
  464.3 8.7 %collective-permute-start.5 = (f32[4,272,256]{2,1,0:T(8,128)S(1)}, f32[4,272,256]{2,1,0:T(8,128)}, u32[]{:S(2)}, u32[]{:S(2)}) collective-permute-start(f32[4,272,256]{2,1,0:T(8,128)S(1)} %all_to_all.79.refs_0_), channel_id=1, source_target_pairs={{0,64},{64,0},{128,192},{192,128},{256,320},{320,256},{384,448},{4... | collective-permute-start | bytes 3342344 | tf_op jit(solution)/shard_map/ppermute | solution.py:397
  (7 other events, 11.3 us)

commit v3 on v2

--- a/solution.py
+++ b/solution.py
@@ -19,10 +19,7 @@
 OBS = 1024
 FOOT = 4
 BLOCK = 256
-CHUNKS = 1
-HALVES = 2 // CHUNKS
-PARTS = 1
-PART = OBS // PARTS
+HALVES = 2
 GROUP_MAIN = 4 * HALVES * MAIN
 GROUP = GROUP_MAIN + 8
 PARTNER = [(t, t ^ 1) for t in range(8)]
@@ -103,7 +100,7 @@
     lasts = jnp.concatenate([s[0, GROUP_MAIN : GROUP_MAIN + 4 * HALVES, :] for s in slots], axis=0)
     values = split_rows(jnp.concatenate([mains, lasts], axis=0))
     total = 16 * MAIN + 16
-    for start in range(0, PART, BLOCK):
+    for start in range(0, OBS, BLOCK):
         lanes = slice(start, start + BLOCK)
         main = jnp.zeros((MAIN, BLOCK), F32)
         last = jnp.zeros((16, BLOCK), F32)
@@ -122,17 +119,17 @@
         mean_ref[0, MAIN:, lanes] = jnp.sum(last, axis=0, keepdims=True)
 
 
-def means(slots, place, weight, part):
+def means(slots, place, weight):
     return pl.pallas_call(
         mean_kernel,
         grid=(VIEWERS,),
         in_specs=[
-            pl.BlockSpec((1, FOOT, PART), lambda v: (v, 0, part)),
-            pl.BlockSpec((1, FOOT, PART), lambda v: (v, 0, part)),
+            pl.BlockSpec((1, FOOT, OBS), lambda v: (v, 0, 0)),
+            pl.BlockSpec((1, FOOT, OBS), lambda v: (v, 0, 0)),
         ]
         + [pl.BlockSpec((1, GROUP, BLOCK), lambda v: (v, 0, 0))] * len(slots),
-        out_specs=pl.BlockSpec((1, LEVELS, PART), lambda v: (v, 0, 0)),
-        out_shape=jax.ShapeDtypeStruct((VIEWERS, LEVELS, PART), F32),
+        out_specs=pl.BlockSpec((1, LEVELS, OBS), lambda v: (v, 0, 0)),
+        out_shape=jax.ShapeDtypeStruct((VIEWERS, LEVELS, OBS), F32),
         compiler_params=params(),
     )(place, weight, *slots)
 
@@ -147,27 +144,26 @@
         pulled_ref[m] = pulled[m * LEVELS : (m + 1) * LEVELS]
 
 
-def pull(mean, hessian, constant, part):
+def pull(mean, hessian, constant):
     size = 8 * LEVELS
     return pl.pallas_call(
         pull_kernel,
         grid=(1,),
         in_specs=[
-            pl.BlockSpec((8, LEVELS, PART), lambda i: (0, 0, 0)),
+            pl.BlockSpec((8, LEVELS, OBS), lambda i: (0, 0, 0)),
             pl.BlockSpec((size, size), lambda i: (0, 0)),
-            pl.BlockSpec((size, PART), lambda i: (0, part)),
+            pl.BlockSpec((size, OBS), lambda i: (0, 0)),
         ],
-        out_specs=pl.BlockSpec((8, LEVELS, PART), lambda i: (0, 0, 0)),
-        out_shape=jax.ShapeDtypeStruct((8, LEVELS, PART), F32),
+        out_specs=pl.BlockSpec((8, LEVELS, OBS), lambda i: (0, 0, 0)),
+        out_shape=jax.ShapeDtypeStruct((8, LEVELS, OBS), F32),
         compiler_params=params(),
     )(mean, hessian, constant)
 
 
 def spread_kernel(grad_ref, place_ref, weight_ref, *refs):
-    groups = 2 * CHUNKS
-    before, slots = refs[:-groups], refs[-groups:]
+    slots = refs
     total = jnp.zeros((2 * (16 * MAIN + 16), BLOCK), F32)
-    for start in range(0, PART, BLOCK):
+    for start in range(0, OBS, BLOCK):
         lanes = slice(start, start + BLOCK)
         grad = grad_ref[0, :, lanes]
         for member in range(FOOT):
@@ -184,33 +180,28 @@
             )
             total = total + dot_nt(rows, one_hot(low, BLOCK))
     total = total[: 16 * MAIN + 16] + total[16 * MAIN + 16 :]
-    for group in range(groups):
+    for group in range(2):
         main = total[group * GROUP_MAIN : (group + 1) * GROUP_MAIN]
         at = 16 * MAIN + group * 4 * HALVES
         last = total[at : at + 4 * HALVES]
-        if before:
-            main = main + before[group][0, :GROUP_MAIN, :]
-            last = last + before[group][0, GROUP_MAIN : GROUP_MAIN + 4 * HALVES, :]
         slots[group][0, :GROUP_MAIN, :] = main
         slots[group][0, GROUP_MAIN : GROUP_MAIN + 4 * HALVES, :] = last
 
 
-def spread(grad, place, weight, before, part):
-    groups = 2 * CHUNKS
+def spread(grad, place, weight):
     slots = pl.BlockSpec((1, GROUP, BLOCK), lambda v: (v, 0, 0))
     return pl.pallas_call(
         spread_kernel,
         grid=(VIEWERS,),
         in_specs=[
-            pl.BlockSpec((1, LEVELS, PART), lambda v: (v, 0, 0)),
-            pl.BlockSpec((1, FOOT, PART), lambda v: (v, 0, part)),
-            pl.BlockSpec((1, FOOT, PART), lambda v: (v, 0, part)),
-        ]
-        + [slots] * len(before),
-        out_specs=[slots] * groups,
-        out_shape=[jax.ShapeDtypeStruct((VIEWERS, GROUP, BLOCK), F32)] * groups,
-        compiler_params=params(),
-    )(grad, place, weight, *before)
+            pl.BlockSpec((1, LEVELS, OBS), lambda v: (v, 0, 0)),
+            pl.BlockSpec((1, FOOT, OBS), lambda v: (v, 0, 0)),
+            pl.BlockSpec((1, FOOT, OBS), lambda v: (v, 0, 0)),
+        ],
+        out_specs=[slots] * 2,
+        out_shape=[jax.ShapeDtypeStruct((VIEWERS, GROUP, BLOCK), F32)] * 2,
+        compiler_params=params(),
+    )(grad, place, weight)
 
 
 def put_kernel(slots_ref, serve_ref, field_ref):
@@ -260,8 +251,8 @@
     lasts = []
     for near_far in range(2):
         for half in range(2):
-            ref = bands[near_far * CHUNKS + half // HALVES]
-            base = (half % HALVES) * HALF
+            ref = bands[near_far]
+            base = half * HALF
             for x in range(4):
                 main = ref[x, base : base + 4 * OWNER, :].reshape(8, MAIN, CELLS)
                 mains.append(jnp.swapaxes(main, 0, 1))
@@ -286,16 +277,12 @@
     return lax.all_to_all(copies, axis, 0, 0, axis_index_groups=ALONG)
 
 
-def gather_obs(block):
-    other = lax.ppermute(block, "obs", PARTNER)
-    return to_all(block, "obs"), to_all(other, "obs")
-
-
-def times_lon(near, far, lon_near, lon_far):
-    def product(tiles, matrix):
-        return jnp.einsum("yrc,ycd->rd", tiles, matrix, precision=HIGHEST, preferred_element_type=F32)
-
-    return product(near, lon_near) + product(far, lon_far)
+def to_sum(tiles):
+    return jnp.sum(lax.all_to_all(tiles, "obs", 0, 0, axis_index_groups=ALONG), axis=0)
+
+
+def product(tiles, matrix):
+    return jnp.einsum("yrc,ycd->rd", tiles, matrix, precision=HIGHEST, preferred_element_type=F32)
 
 
 def shards(
@@ -319,11 +306,21 @@
         far = lax.dynamic_index_in_dim(x, 1 - which, axis, keepdims=False)
         return near, far
 
-    feet = jnp.concatenate([foot_slot.astype(F32), foot_weight], axis=0)
-    feet = lax.all_to_all(jnp.broadcast_to(feet[None], (8,) + feet.shape), "lev", 0, 0)
-    serve = serve_cols[0, 0].astype(F32).reshape(8, 8, CAP).transpose(1, 0, 2)
-    serve = lax.all_to_all(serve, "obs", 0, 0)
-    serve = serve.reshape(8, VIEWERS * CAP)
+    tile = (foot_slot >> 6) & 7
+    slab = foot_slot >> 9
+    group = 2 * ((tile & 1) ^ half) + (slab >> 2)
+    place = (4 * group + (tile >> 1)) * BLOCK + (slab & 3) * CAP + (foot_slot & (CAP - 1))
+
+    serve = serve_cols[0, 0].astype(F32).reshape(8, 4, 2, CAP).transpose(2, 1, 0, 3)
+    near, far = near_far(serve, 0, half)
+    piece = lax.dynamic_index_in_dim(
+        mat_lon.reshape(8, CELLS, CELLS), lax.axis_index("lat"), 0, keepdims=False
+    )
+    piece = jnp.concatenate([piece, far.reshape(8, CELLS)], axis=0)
+    piece = lax.ppermute(piece, "obs", PARTNER)
+    other_lon = lax.all_gather(piece[:CELLS], "lat", axis=0, tiled=False)
+    lon_near, lon_far = near_far(mat_lon.reshape(4, 2, CELLS, CELLS), 1, half)
+    other_near, other_far = near_far(other_lon.reshape(4, 2, CELLS, CELLS), 1, half)
 
     band_near = to_all(chi, "lat")
     band_far = lax.ppermute(band_near, "lat", PARTNER)
@@ -331,30 +328,12 @@
     field = jnp.einsum(
         "ixr,xlrk->ilk", lat_near, band_near, precision=HIGHEST, preferred_element_type=F32
     ) + jnp.einsum("ixr,xlrk->ilk", lat_far, band_far, precision=HIGHEST, preferred_element_type=F32)
-    feet, serve, field = lax.optimization_barrier((feet, serve, field))
-    chunks = []
-    for chunk in range(CHUNKS):
-        pieces = []
-        for place in range(chunk * HALVES, (chunk + 1) * HALVES):
-            rows = field[8 * place : 8 * place + 8]
-            pieces += [rows[:, :MAIN].reshape(8 * MAIN, CELLS), rows[:, MAIN]]
-        chunks.append(jnp.concatenate(pieces, axis=0))
-
-    serve = lax.all_to_all(jnp.broadcast_to(serve[None], (8,) + serve.shape), "lev", 0, 0)
-    serve = serve.reshape(8, 4, 2, VIEWERS * CAP).astype(jnp.int32)
-    serves = [s.transpose(1, 0, 2) for s in near_far(serve, 2, half)]
-    slot = feet[:, :4].astype(jnp.int32)
-    weight = feet[:, 4:]
-    tile = (slot >> 6) & 7
-    far = (tile & 1) ^ half
-    slab = slot >> 9
-    if CHUNKS == 2:
-        group = 2 * (slab >> 2) + far
-    else:
-        group = 2 * far + (slab >> 2)
-    place = (4 * group + (tile >> 1)) * BLOCK + (slab & 3) * CAP + (slot & (CAP - 1))
-
-    lons = near_far(mat_lon.reshape(4, 2, CELLS, CELLS), 1, half)
+    pieces = []
+    for part in range(HALVES):
+        rows = field[8 * part : 8 * part + 8]
+        pieces += [rows[:, :MAIN].reshape(8 * MAIN, CELLS), rows[:, MAIN]]
+    field = jnp.concatenate(pieces, axis=0)
+
     matches = (
         chan_map[:, None] == jnp.arange(chan_table.shape[0], dtype=jnp.int32)[None, :]
     ).astype(F32)
@@ -363,42 +342,48 @@
     scaled = error_weight[:, None] * selected
     hessian = jnp.dot(selected.T, scaled, precision=HIGHEST, preferred_element_type=F32)
     constant = jnp.dot(scaled.T, innovation, precision=HIGHEST, preferred_element_type=F32)
-
-    chunks = [times_lon(*gather_obs(chunk), *lons) for chunk in chunks]
-    chunks, serves, place, weight, hessian, constant = lax.optimization_barrier(
-        (chunks, serves, place, weight, hessian, constant)
-    )
-
-    def serve_of(which, chunk):
-        return serves[which][:, 4 * HALVES * chunk : 4 * HALVES * (chunk + 1)]
-
-    slots = []
-    for chunk in range(CHUNKS):
-        for which, tiles in enumerate(gather_obs(chunks[chunk])):
-            slots.append(pick(tiles, serve_of(which, chunk)))
-
-    back = []
-    for part in range(PARTS):
-        mean = lax.all_to_all(means(slots, place, weight, part), "lev", 0, 0)
-        back.append(lax.all_to_all(pull(mean, hessian, constant, part), "lev", 0, 0))
-    slots = []
-    for part in range(PARTS):
-        slots = spread(back[part], place, weight, slots, part)
-
-    bands = []
-    for chunk in range(CHUNKS):
-        tiles = put(slots[2 * chunk + 1], serve_of(1, chunk))
-        far = jnp.sum(lax.all_to_all(tiles, "obs", 0, 0, axis_index_groups=ALONG), axis=0)
-        far = lax.ppermute(far, "obs", PARTNER)
-        tiles = put(slots[2 * chunk], serve_of(0, chunk))
-        near = jnp.sum(lax.all_to_all(tiles, "obs", 0, 0, axis_index_groups=ALONG), axis=0)
-        field = times_lon(*gather_obs(near + far), *lons)
-        band_near = to_all(field, "lat")
-        bands.append((band_near, lax.ppermute(band_near, "lat", PARTNER)))
     lat = jnp.stack(
         [m.reshape(16, 4, 2, 8).transpose(0, 2, 1, 3) for m in (lat_near, lat_far)], axis=1
     ).reshape(16, 128)
-    return finish(chi, lat, [b[0] for b in bands] + [b[1] for b in bands])
+
+    other = lax.ppermute(field, "obs", PARTNER)
+    near_tiles = to_all(field, "obs")
+    serve = jnp.stack([near, piece[CELLS:].reshape(4, VIEWERS, CAP)], axis=1)
+    serve = lax.all_to_all(serve, "obs", 0, 0, axis_index_groups=ALONG)
+    far_tiles = to_all(other, "obs")
+    tile_near = product(near_tiles, lon_near) + product(far_tiles, lon_far)
+    tile_far = product(near_tiles, other_near) + product(far_tiles, other_far)
+
+    about = jnp.concatenate([serve.reshape(4, OBS), place.astype(F32), foot_weight], axis=0)
+    about, tile_near, tile_far, hessian, constant, lat = lax.optimization_barrier(
+        (about, tile_near, tile_far, hessian, constant, lat)
+    )
+    about = about[None]
+    for step in (4, 2, 1):
+        other = lax.ppermute(about, "lev", [(m, m ^ step) for m in range(8)])
+        upper = (lax.axis_index("lev") // step) % 2
+        pair = jnp.where(upper == 0, jnp.stack([about, other], 1), jnp.stack([other, about], 1))
+        about = pair.reshape((-1,) + about.shape[1:])
+    weight = about[:, 8:]
+    place = about[:, 4:8].astype(jnp.int32)
+    serve = about[:, :4].reshape(8, 4, 2, VIEWERS * CAP).astype(jnp.int32).transpose(2, 1, 0, 3)
+    near = pick(to_all(tile_near, "obs"), serve[0])
+    far = pick(to_all(tile_far, "obs"), serve[1])
+
+    mean = lax.all_to_all(means([near, far], place, weight), "lev", 0, 0)
+    pulled = lax.all_to_all(pull(mean, hessian, constant), "lev", 0, 0)
+    near, far = spread(pulled, place, weight)
+
+    far = to_sum(put(far, serve[1]))
+    near = to_sum(put(near, serve[0]))
+    far_tiles = to_all(far, "obs")
+    near_tiles = to_all(near, "obs")
+    far = product(far_tiles, other_far) + product(near_tiles, other_near)
+    far = lax.ppermute(far, "obs", PARTNER)
+    field = product(far_tiles, lon_far) + product(near_tiles, lon_near) + far
+    band_near = to_all(field, "lat")
+    band_far = lax.ppermute(band_near, "lat", PARTNER)
+    return finish(chi, lat, [band_near, band_far])
 
 
 def solution(mesh):

time: 478 us -> 443 us (0.927)
  the two profiles are of different devices: /device:TPU:33 before, /device:TPU:161 now
where the time goes in v3:
time: 443 us; the launch traced here: 441 us
  waiting for transfers between devices  111 us (25%)
  starting transfers between devices  109 us (25%)
  blocking collectives  101 us (23%)
  Pallas kernels  40.7 us (9%)
  matrix products  27.1 us (6%)
  local copies, waits for them, and re-layouts  25.6 us (6%)
  between operations  14 us (3%)
  other arithmetic  11.8 us (3%)
    all_to_all x1, blocking collectives, shards(): pulled = lax.all_to_all(pull(mean, hessian, constant), 'lev', 0, 0)  44.9 us
    all_to_all x1, blocking collectives, shards(): mean = lax.all_to_all(means([near, far], place, weight), 'lev', 0, 0)  38.9 us
    all_to_all x7, waiting for transfers between devices, to_all(): return lax.all_to_all(copies, axis, 0, 0, axis_index_groups=ALONG)  33.6 us
    all_to_all x7, starting transfers between devices, to_all(): return lax.all_to_all(copies, axis, 0, 0, axis_index_groups=ALONG)  28 us
    ppermute x3, starting transfers between devices, shards(): other = lax.ppermute(about, 'lev', [(m, m ^ step) for m in range(8)])  27.9 us
    ppermute x1, waiting for transfers between devices, shards(): far = lax.ppermute(far, 'obs', PARTNER)  23.8 us
    all_to_all x2, waiting for transfers between devices, to_sum(): lax.all_to_all(tiles, 'obs', 0, 0, axis_index_groups=ALONG)  21.6 us
    all_to_all x1, blocking collectives, to_all(): return lax.all_to_all(copies, axis, 0, 0, axis_index_groups=ALONG)  17 us
  transfers between devices with their start and end apart: 19, of which 12 were waited for; matrix products, arithmetic and copies ran while one was open for 11% of the time, Pallas kernels for 2%

profile of v3, /device:TPU:161, one launch (start us, length us, event | category | flops | bytes accessed | tf_op | source)
XLA Modules:
  0.0 440.9 jit_solution(16761950321682589578)
XLA Ops:
  8.8 4.1 all-to-all-start.1
  13.7 14.1 %all-to-all-done.1 = f32[4,17,16,256]{3,2,1,0:T(8,128)S(1)} async-done(((f32[4,17,16,256]{3,2,1,0:T(8,128)}), f32[4,17,16,256]{3,2,1,0:T(8,128)S(1)}, u32[]{:S(2)}, u32[]{:S(2)}) %all-to-all-start.1) | async-done | bytes 1114144 | tf_op jit(solution)/shard_map/all_to_all | solution.py:277
  28.9 3.9 collective-permute-start.1
  32.9 9.7 %collective-permute-start = (f32[264,256]{1,0:T(8,128)S(1)}, f32[264,256]{1,0:T(8,128)S(1)}, u32[]{:S(2)}, u32[]{:S(2)}) collective-permute-start(f32[264,256]{1,0:T(8,128)S(1)} %pad_maximum_fusion.1), channel_id=1, source_target_pairs={{0,1},{1,0},{2,3},{3,2},{4,5},{5,4},{6,7},{7,6},{8,9},{9,8},{10,11... | collective-permute-start | bytes 811016 | tf_op jit(solution)/shard_map/ppermute | solution.py:320
  42.6 16.4 %collective-permute-done = f32[264,256]{1,0:T(8,128)S(1)} collective-permute-done((f32[264,256]{1,0:T(8,128)S(1)}, f32[264,256]{1,0:T(8,128)S(1)}, u32[]{:S(2)}, u32[]{:S(2)}) %collective-permute-start) | collective-permute-done | bytes 270368 | tf_op jit(solution)/shard_map/ppermute | solution.py:320
  63.1 4.2 all-to-all-start
  74.0 4.4 all-to-all-start.2
  80.7 12.4 %collective-permute-start.2 = (f32[272,256]{1,0:T(8,128)}, f32[272,256]{1,0:T(8,128)}, u32[]{:S(2)}, u32[]{:S(2)}) collective-permute-start(f32[272,256]{1,0:T(8,128)} %pad_maximum_fusion), channel_id=1, source_target_pairs={{0,1},{1,0},{2,3},{3,2},{4,5},{5,4},{6,7},{7,6},{8,9},{9,8},{10,11... | collective-permute-start | bytes 835592 | tf_op jit(solution)/shard_map/ppermute | solution.py:349
  95.5 9.9 %collective-permute-done.2 = f32[272,256]{1,0:T(8,128)} collective-permute-done((f32[272,256]{1,0:T(8,128)}, f32[272,256]{1,0:T(8,128)}, u32[]{:S(2)}, u32[]{:S(2)}) %collective-permute-start.2) | collective-permute-done | bytes 278560 | tf_op jit(solution)/shard_map/ppermute | solution.py:349
  107.6 4.4 all-to-all-start.3
  128.8 3.5 all-to-all-start.4
  132.4 19.3 %collective-permute-start.3 = (f32[1,12,1024]{2,1,0:T(8,128)S(1)}, f32[1,12,1024]{2,1,0:T(8,128)}, u32[]{:S(2)}, u32[]{:S(2)}) collective-permute-start(f32[1,12,1024]{2,1,0:T(8,128)S(1)} %bitcast.144), channel_id=1, source_target_pairs={{0,32},{8,40},{16,48},{24,56},{32,0},{40,8},{48,16},{56,24},{1,33}... | collective-permute-start | bytes 147464 | tf_op jit(solution)/shard_map/ppermute | solution.py:363
  159.7 4.6 %all-to-all-start.5 = ((f32[4,272,256]{2,1,0:T(8,128)}), f32[4,272,256]{2,1,0:T(8,128)}, u32[]{:S(2)}, u32[]{:S(2)}) async-start(f32[4,272,256]{2,1,0:T(8,128)} %broadcast_in_dim.23), calls=%async_computation.5 | async-start | bytes 2228224 | tf_op jit(solution)/shard_map/all_to_all | solution.py:277
  166.3 6.7 %collective-permute-start.5 = (f32[4,12,1024]{2,0,1:T(4,128)}, f32[4,12,1024]{2,0,1:T(4,128)}, u32[]{:S(2)}, u32[]{:S(2)}) collective-permute-start(f32[4,12,1024]{2,0,1:T(4,128)} %select_n.130), channel_id=1, source_target_pairs={{0,8},{8,0},{16,24},{24,16},{32,40},{40,32},{48,56},{56,48},{1,9},... | collective-permute-start | bytes 589832 | tf_op jit(solution)/shard_map/ppermute | solution.py:363
  186.1 4.0 shard_map.110.refs_1_
  190.1 11.1 %shard_map.111 = f32[8,17,1024]{2,1,0:T(8,128)S(1)} custom-call(s32[8,4,1024]{2,1,0:T(4,128)S(1)} %get-tuple-element.23.place_ref, f32[8,4,1024]{2,1,0:T(4,128)S(1)} %get-tuple-element.22.weight_ref, f32[8,136,256]{2,1,0:T(8,128)S(1)} %copy-done.2, f32[8,136,256]{2,1,0:T(8,128)S(1)} %shard_map.110.refs_1_), custom_call_target="tpu_custom_call" | custom-call | tf_op jit(solution)/shard_map/pallas_call | solution.py:123
  201.3 38.9 %all_to_all.65.mean_ref = f32[8,17,1024]{2,1,0:T(8,128)S(1)} all-to-all(f32[8,17,1024]{2,1,0:T(8,128)S(1)} %shard_map.111), channel_id=1, replica_groups=mesh['lat'=8,'lev'=8,'obs'=8] {'lev'}, dimensions={0} | all-to-all | bytes 1114112 | tf_op jit(solution)/shard_map/all_to_all | solution.py:373
  240.8 44.9 %all_to_all.66.grad_ref = f32[8,17,1024]{2,1,0:T(8,128)S(1)} all-to-all(f32[8,17,1024]{2,1,0:T(8,128)S(1)} %shard_map.112), channel_id=1, replica_groups=mesh['lat'=8,'lev'=8,'obs'=8] {'lev'}, dimensions={0} | all-to-all | bytes 1114112 | tf_op jit(solution)/shard_map/all_to_all | solution.py:374
  285.7 10.9 %shard_map.113 = (f32[8,136,256]{2,1,0:T(8,128)S(1)}, f32[8,136,256]{2,1,0:T(8,128)S(1)}) custom-call(f32[8,17,1024]{2,1,0:T(8,128)S(1)} %all_to_all.66.grad_ref, s32[8,4,1024]{2,1,0:T(4,128)S(1)} %get-tuple-element.23.place_ref, f32[8,4,1024]{2,1,0:T(4,128)S(1)} %get-tuple-element.22.weight_ref), custom_call_target="tpu_custom_call" | custom-call | tf_op jit(solution)/shard_map/pallas_call | solution.py:193
  296.7 4.0 shard_map.115
  300.7 4.3 all-to-all-start.10
  304.9 4.0 shard_map.114
  308.9 10.1 %all-to-all-done.10 = f32[4,272,256]{2,1,0:T(8,128)} async-done(((f32[4,272,256]{2,1,0:T(8,128)}), f32[4,272,256]{2,1,0:T(8,128)}, u32[]{:S(2)}, u32[]{:S(2)}) %all-to-all-start.10) | async-done | bytes 1114144 | tf_op jit(solution)/shard_map/all_to_all | solution.py:281
  319.1 3.5 all-to-all-start.8
  324.0 11.5 %all-to-all-done.8 = f32[4,272,256]{2,1,0:T(8,128)S(1)} async-done(((f32[4,272,256]{2,1,0:T(8,128)}), f32[4,272,256]{2,1,0:T(8,128)S(1)}, u32[]{:S(2)}, u32[]{:S(2)}) %all-to-all-start.8) | async-done | bytes 1114144 | tf_op jit(solution)/shard_map/all_to_all | solution.py:281
  336.8 3.5 all-to-all-start.11
  341.7 10.2 %all-to-all-done.11 = f32[4,272,256]{2,1,0:T(8,128)S(1)} async-done(((f32[4,272,256]{2,1,0:T(8,128)}), f32[4,272,256]{2,1,0:T(8,128)S(1)}, u32[]{:S(2)}, u32[]{:S(2)}) %all-to-all-start.11) | async-done | bytes 1114144 | tf_op jit(solution)/shard_map/all_to_all | solution.py:277
  359.5 7.7 %all-to-all-done.9 = f32[4,272,256]{2,1,0:T(8,128)S(1)} async-done(((f32[4,272,256]{2,1,0:T(8,128)}), f32[4,272,256]{2,1,0:T(8,128)S(1)}, u32[]{:S(2)}, u32[]{:S(2)}) %all-to-all-start.9) | async-done | bytes 1114144 | tf_op jit(solution)/shard_map/all_to_all | solution.py:277
  369.6 11.4 %collective-permute-start.6 = (f32[272,256]{1,0:T(8,128)S(1)}, f32[272,256]{1,0:T(8,128)S(1)}, u32[]{:S(2)}, u32[]{:S(2)}) collective-permute-start(f32[272,256]{1,0:T(8,128)S(1)} %fusion.5), channel_id=1, source_target_pairs={{0,1},{1,0},{2,3},{3,2},{4,5},{5,4},{6,7},{7,6},{8,9},{9,8},{10,11... | collective-permute-start | bytes 835592 | tf_op jit(solution)/shard_map/ppermute | solution.py:382
  382.1 23.8 %collective-permute-done.6 = f32[272,256]{1,0:T(8,128)S(1)} collective-permute-done((f32[272,256]{1,0:T(8,128)S(1)}, f32[272,256]{1,0:T(8,128)S(1)}, u32[]{:S(2)}, u32[]{:S(2)}) %collective-permute-start.6) | collective-permute-done | bytes 278560 | tf_op jit(solution)/shard_map/ppermute | solution.py:382
  407.0 17.0 %all_to_all.67.refs_0_ = f32[4,272,256]{2,1,0:T(8,128)S(1)} all-to-all(f32[4,272,256]{2,1,0:T(8,128)S(1)} %broadcast_in_dim.26), channel_id=1, replica_groups={{0,128,256,384},{64,192,320,448},{1,129,257,385},{65,193,321,449},{2,13..., dimensions={0} | all-to-all | bytes 2228224 | tf_op jit(solution)/shard_map/all_to_all | solution.py:277
  424.0 4.2 collective-permute-start.7
  (130 shorter events, 84.3 us)
Async XLA Ops:
  6.5 7.2 %copy-start = (f32[2048,256]{1,0:T(8,128)S(1)}, f32[2048,256]{1,0:T(8,128)}, u32[]{:S(2)}) copy-start(f32[2048,256]{1,0:T(8,128)} %param.12) | copy-start | bytes 6291460
  8.8 19.0 %all-to-all-start.1 = ((f32[4,17,16,256]{3,2,1,0:T(8,128)}), f32[4,17,16,256]{3,2,1,0:T(8,128)S(1)}, u32[]{:S(2)}, u32[]{:S(2)}) async-start(f32[4,17,16,256]{3,2,1,0:T(8,128)} %broadcast_in_dim.18), calls=%async_computation.1 | async-start | bytes 2228224 | tf_op jit(solution)/shard_map/all_to_all | solution.py:277
  13.0 110.9 %all-gather.3.cloned.1.call-start = ((), (), s32[]{:S(2)}) async-start(), calls=%async_computation.13 | async-start | bytes 2359296 | tf_op jit(solution)/shard_map/all_gather | solution.py:321
  28.9 30.9 %copy-start.20 = (f32[16,128]{1,0:T(8,128)S(1)}, f32[16,128]{1,0:T(8,128)}, u32[]{:S(2)}) copy-start(f32[16,128]{1,0:T(8,128)} %param.13) | copy-start | bytes 24580
  28.9 39.6 %collective-permute-start.1 = (f32[4,17,16,256]{3,2,0,1:T(8,128)}, f32[4,17,16,256]{3,2,0,1:T(8,128)}, u32[]{:S(2)}, u32[]{:S(2)}) collective-permute-start(f32[4,17,16,256]{3,2,0,1:T(8,128)} %copy.72), channel_id=1, source_target_pairs={{0,64},{64,0},{128,192},{192,128},{256,320},{320,256},{384,448},{4... | collective-permute-start | bytes 3342344 | tf_op jit(solution)/shard_map/ppermute | solution.py:326
  32.9 26.2 %collective-permute-start = (f32[264,256]{1,0:T(8,128)S(1)}, f32[264,256]{1,0:T(8,128)S(1)}, u32[]{:S(2)}, u32[]{:S(2)}) collective-permute-start(f32[264,256]{1,0:T(8,128)S(1)} %pad_maximum_fusion.1), channel_id=1, source_target_pairs={{0,1},{1,0},{2,3},{3,2},{4,5},{5,4},{6,7},{7,6},{8,9},{9,8},{10,11... | collective-permute-start | bytes 811016 | tf_op jit(solution)/shard_map/ppermute | solution.py:320
  63.1 8.9 %all-to-all-start = ((f32[4,1,1024]{2,1,0:T(1,128)}), f32[4,1,1024]{2,1,0:T(1,128)S(1)}, u32[]{:S(2)}, u32[]{:S(2)}) async-start(f32[4,1,1024]{2,1,0:T(1,128)} %reshape.188), calls=%async_computation | async-start | bytes 32768 | tf_op jit(solution)/shard_map/all_to_all | solution.py:352
  74.0 4.4 copy-start.21
  74.0 19.1 %copy-start.18 = (s32[4,1024]{1,0:T(4,128)S(1)}, s32[4,1024]{1,0:T(4,128)}, u32[]{:S(2)}) copy-start(s32[4,1024]{1,0:T(4,128)} %param.20) | copy-start | bytes 49156
  74.0 31.4 %all-to-all-start.2 = ((f32[4,272,256]{2,1,0:T(8,128)}), f32[4,272,256]{2,1,0:T(8,128)S(1)}, u32[]{:S(2)}, u32[]{:S(2)}) async-start(f32[4,272,256]{2,1,0:T(8,128)} %broadcast_in_dim.19), calls=%async_computation.2 | async-start | bytes 2228224 | tf_op jit(solution)/shard_map/all_to_all | solution.py:277
  80.7 24.6 %collective-permute-start.2 = (f32[272,256]{1,0:T(8,128)}, f32[272,256]{1,0:T(8,128)}, u32[]{:S(2)}, u32[]{:S(2)}) collective-permute-start(f32[272,256]{1,0:T(8,128)} %pad_maximum_fusion), channel_id=1, source_target_pairs={{0,1},{1,0},{2,3},{3,2},{4,5},{5,4},{6,7},{7,6},{8,9},{9,8},{10,11... | collective-permute-start | bytes 835592 | tf_op jit(solution)/shard_map/ppermute | solution.py:349
  107.6 5.0 %copy-start.19 = (f32[300]{0:T(512)S(1)}, f32[300]{0:T(512)}, u32[]{:S(2)}) copy-start(f32[300]{0:T(512)} %param.17) | copy-start | bytes 3604
  107.6 14.5 %all-to-all-start.3 = ((f32[4,272,256]{2,1,0:T(8,128)}), f32[4,272,256]{2,1,0:T(8,128)S(1)}, u32[]{:S(2)}, u32[]{:S(2)}) async-start(f32[4,272,256]{2,1,0:T(8,128)} %broadcast_in_dim.20), calls=%async_computation.3 | async-start | bytes 2228224 | tf_op jit(solution)/shard_map/all_to_all | solution.py:277
  113.6 4.6 %copy-start.15 = (f32[4,1024]{1,0:T(4,128)S(1)}, f32[4,1024]{1,0:T(4,128)}, u32[]{:S(2)}) copy-start(f32[4,1024]{1,0:T(4,128)} %add_convert_fusion) | copy-start | bytes 49156
  113.6 4.6 %copy-start.17 = (f32[4,1024]{1,0:T(4,128)S(1)}, f32[4,1024]{1,0:T(4,128)}, u32[]{:S(2)}) copy-start(f32[4,1024]{1,0:T(4,128)} %param.19) | copy-start | bytes 49156
  128.8 29.8 %all-to-all-start.4 = ((f32[4,272,256]{2,1,0:T(8,128)}), f32[4,272,256]{2,1,0:T(8,128)S(1)}, u32[]{:S(2)}, u32[]{:S(2)}) async-start(f32[4,272,256]{2,1,0:T(8,128)} %broadcast_in_dim.22), calls=%async_computation.4 | async-start | bytes 2228224 | tf_op jit(solution)/shard_map/all_to_all | solution.py:277
  132.4 21.2 %collective-permute-start.3 = (f32[1,12,1024]{2,1,0:T(8,128)S(1)}, f32[1,12,1024]{2,1,0:T(8,128)}, u32[]{:S(2)}, u32[]{:S(2)}) collective-permute-start(f32[1,12,1024]{2,1,0:T(8,128)S(1)} %bitcast.144), channel_id=1, source_target_pairs={{0,32},{8,40},{16,48},{24,56},{32,0},{40,8},{48,16},{56,24},{1,33}... | collective-permute-start | bytes 147464 | tf_op jit(solution)/shard_map/ppermute | solution.py:363
  155.1 9.2 %collective-permute-start.4 = (f32[2,12,1024]{2,1,0:T(8,128)}, f32[2,12,1024]{2,1,0:T(8,128)}, u32[]{:S(2)}, u32[]{:S(2)}) collective-permute-start(f32[2,12,1024]{2,1,0:T(8,128)} %maximum_select_fusion.3), channel_id=1, source_target_pairs={{0,16},{8,24},{16,0},{24,8},{32,48},{40,56},{48,32},{56,40},{1,17}... | collective-permute-start | bytes 294920 | tf_op jit(solution)/shard_map/ppermute | solution.py:363
  159.7 4.6 %copy-start.14 = (f32[2,1,12,1024]{3,2,0,1:T(8,128)S(1)}, f32[2,1,12,1024]{3,2,0,1:T(8,128)}, u32[]{:S(2)}) copy-start(f32[2,1,12,1024]{3,2,0,1:T(8,128)} %maximum_select_fusion.2) | copy-start | bytes 294916
  159.7 26.4 %all-to-all-start.5 = ((f32[4,272,256]{2,1,0:T(8,128)}), f32[4,272,256]{2,1,0:T(8,128)}, u32[]{:S(2)}, u32[]{:S(2)}) async-start(f32[4,272,256]{2,1,0:T(8,128)} %broadcast_in_dim.23), calls=%async_computation.5 | async-start | bytes 2228224 | tf_op jit(solution)/shard_map/all_to_all | solution.py:277
  166.3 10.4 %collective-permute-start.5 = (f32[4,12,1024]{2,0,1:T(4,128)}, f32[4,12,1024]{2,0,1:T(4,128)}, u32[]{:S(2)}, u32[]{:S(2)}) collective-permute-start(f32[4,12,1024]{2,0,1:T(4,128)} %select_n.130), channel_id=1, source_target_pairs={{0,8},{8,0},{16,24},{24,16},{32,40},{40,32},{48,56},{56,48},{1,9},... | collective-permute-start | bytes 589832 | tf_op jit(solution)/shard_map/ppermute | solution.py:363
  201.3 38.9 %copy-start.3 = (f32[136,1024]{1,0:T(8,128)S(1)}, f32[136,1024]{1,0:T(8,128)}, u32[]{:S(2)}) copy-start(f32[136,1024]{1,0:T(8,128)} %fusion.24.constant_ref) | copy-start | bytes 1671172
  201.3 38.9 %copy-start.7 = (f32[136,136]{1,0:T(8,128)S(1)}, f32[136,136]{1,0:T(8,128)}, u32[]{:S(2)}) copy-start(f32[136,136]{1,0:T(8,128)} %fusion.26.hessian_ref) | copy-start | bytes 221956
  240.8 55.9 %copy-start.6 = (s32[4,8,512]{2,1,0:T(8,128)S(1)}, s32[4,8,512]{2,1,0:T(8,128)}, u32[]{:S(2)}) copy-start(s32[4,8,512]{2,1,0:T(8,128)} %copy-done.5) | copy-start | bytes 196612
  300.7 18.4 %all-to-all-start.10 = ((f32[4,272,256]{2,1,0:T(8,128)}), f32[4,272,256]{2,1,0:T(8,128)}, u32[]{:S(2)}, u32[]{:S(2)}) async-start(f32[4,272,256]{2,1,0:T(8,128)} %shard_map.115), calls=%async_computation.10 | async-start | bytes 2228224 | tf_op jit(solution)/shard_map/all_to_all | solution.py:281
  319.1 16.3 %all-to-all-start.8 = ((f32[4,272,256]{2,1,0:T(8,128)}), f32[4,272,256]{2,1,0:T(8,128)S(1)}, u32[]{:S(2)}, u32[]{:S(2)}) async-start(f32[4,272,256]{2,1,0:T(8,128)} %shard_map.114), calls=%async_computation.8 | async-start | bytes 2228224 | tf_op jit(solution)/shard_map/all_to_all | solution.py:281
  336.8 15.1 %all-to-all-start.11 = ((f32[4,272,256]{2,1,0:T(8,128)}), f32[4,272,256]{2,1,0:T(8,128)S(1)}, u32[]{:S(2)}, u32[]{:S(2)}) async-start(f32[4,272,256]{2,1,0:T(8,128)} %broadcast_in_dim.25), calls=%async_computation.11 | async-start | bytes 2228224 | tf_op jit(solution)/shard_map/all_to_all | solution.py:277
  353.3 13.9 %all-to-all-start.9 = ((f32[4,272,256]{2,1,0:T(8,128)}), f32[4,272,256]{2,1,0:T(8,128)S(1)}, u32[]{:S(2)}, u32[]{:S(2)}) async-start(f32[4,272,256]{2,1,0:T(8,128)} %broadcast_in_dim.24), calls=%async_computation.9 | async-start | bytes 2228224 | tf_op jit(solution)/shard_map/all_to_all | solution.py:277
  367.2 13.8 %copy-start.10 = (f32[4,272,256]{2,1,0:T(8,128)S(1)}, f32[4,272,256]{2,1,0:T(8,128)}, u32[]{:S(2)}) copy-start(f32[4,272,256]{2,1,0:T(8,128)} %copy-done.9) | copy-start | bytes 3342340
  369.6 36.2 %collective-permute-start.6 = (f32[272,256]{1,0:T(8,128)S(1)}, f32[272,256]{1,0:T(8,128)S(1)}, u32[]{:S(2)}, u32[]{:S(2)}) collective-permute-start(f32[272,256]{1,0:T(8,128)S(1)} %fusion.5), channel_id=1, source_target_pairs={{0,1},{1,0},{2,3},{3,2},{4,5},{5,4},{6,7},{7,6},{8,9},{9,8},{10,11... | collective-permute-start | bytes 835592 | tf_op jit(solution)/shard_map/ppermute | solution.py:382
  407.0 23.7 %copy-start.4 = (f32[17,16,256]{2,1,0:T(8,128)S(1)}, f32[17,16,256]{2,1,0:T(8,128)}, u32[]{:S(2)}) copy-start(f32[17,16,256]{2,1,0:T(8,128)} %chi_ref.1) | copy-start | bytes 835588
  424.0 6.7 %collective-permute-start.7 = (f32[4,272,256]{2,1,0:T(8,128)S(1)}, f32[4,272,256]{2,1,0:T(8,128)}, u32[]{:S(2)}, u32[]{:S(2)}) collective-permute-start(f32[4,272,256]{2,1,0:T(8,128)S(1)} %all_to_all.67.refs_0_), channel_id=1, source_target_pairs={{0,64},{64,0},{128,192},{192,128},{256,320},{320,256},{384,448},{4... | collective-permute-start | bytes 3342344 | tf_op jit(solution)/shard_map/ppermute | solution.py:385
  (9 other events, 18.7 us)
Sparse Core Ops, SparseCore 0:
  59.9 43.6 all-gather.2

commit v4 on v3

v4 whole, which is shorter than its diff:
```python
import functools

import jax
import jax.numpy as jnp
from jax import lax
from jax.experimental import pallas as pl
from jax.experimental.pallas import tpu as pltpu
from jax.sharding import PartitionSpec as P

HIGHEST = lax.Precision.HIGHEST
F32 = jnp.float32
BF16 = jnp.bfloat16

LEVELS = 17
MAIN = 16
CELLS = 256
OWNER = 2 * MAIN
HALF = 4 * OWNER + 8
CAP = 64
VIEWERS = 8
OBS = 1024
FOOT = 4
BLOCK = 256
HALVES = 2
GROUP_MAIN = 4 * HALVES * MAIN
GROUP = GROUP_MAIN + 8
LANES = 128
LISTS = 32
COLUMN = MAIN * 8 + 8
PARTNER = [(t, t ^ 1) for t in range(8)]
ALONG = [[0, 2, 4, 6], [1, 3, 5, 7]]
VMEM = 48 * 1024 * 1024


def params():
    return pltpu.CompilerParams(vmem_limit_bytes=VMEM)


def split(x):
    high = x.astype(BF16)
    return high, (x - high.astype(F32)).astype(BF16)


def split_rows(x):
    return jnp.concatenate(split(x), axis=0)


def one_hot(index, rows):
    place = lax.broadcasted_iota(jnp.int32, (rows, index.shape[1]), 0)
    return jnp.where(place == index, 1.0, 0.0).astype(BF16)


def dot(a, b):
    return lax.dot_general(a, b, (((1,), (0,)), ((), ())), preferred_element_type=F32)


def dot_nt(a, b):
    return lax.dot_general(a, b, (((1,), (1,)), ((), ())), preferred_element_type=F32)


def lists_of(about_ref, tile, which):
    lists = []
    for slab in range(8):
        rows = about_ref[slab, pl.ds(pl.multiple_of(8 * tile, 8), 8), :]
        rows = [rows[4 * which + i : 4 * which + i + 1] for i in range(4)]
        lists.append(jnp.concatenate(rows, axis=1).astype(jnp.int32))
    return lists


def feet_of(about_ref, member, start):
    def row(first):
        at = first + 8 * member + start // LANES
        return jnp.concatenate([about_ref[0, at : at + 1, :], about_ref[0, at + 1 : at + 2, :]], axis=1)

    place = row(LISTS).astype(jnp.int32)
    return jnp.bitwise_and(place, BLOCK - 1), lax.shift_right_logical(place, 8), row(2 * LISTS)


def pick_kernel(which, field_ref, about_ref, slots_ref):
    tile = pl.program_id(0)
    lists = lists_of(about_ref, tile, which)
    for half in range(HALVES):
        base = half * HALF
        last = field_ref[0, base + 4 * OWNER : base + HALF, :]
        mains = []
        lasts = []
        for quarter in range(4):
            index = lists[4 * half + quarter]
            cell = jnp.bitwise_and(index, CELLS - 1)
            second = index >= CELLS
            start = base + quarter * OWNER
            rows = jnp.concatenate([field_ref[0, start : start + OWNER, :], last], axis=0)
            count = OWNER + 8
            both = dot(split_rows(rows), one_hot(cell, CELLS))
            picked = both[:count] + both[count:]
            mains.append(jnp.where(second, picked[MAIN:OWNER], picked[:MAIN]))
            at = OWNER + 2 * quarter
            lasts.append(jnp.where(second, picked[at + 1 : at + 2], picked[at : at + 1]))
        place = 4 * half + tile
        start = pl.multiple_of(place * MAIN, MAIN)
        for viewer in range(VIEWERS):
            lanes = slice(viewer * CAP, (viewer + 1) * CAP)
            slots_ref[viewer, pl.ds(start, MAIN), :] = jnp.concatenate([m[:, lanes] for m in mains], axis=1)
            slots_ref[viewer, pl.ds(GROUP_MAIN + place, 1), :] = jnp.concatenate([m[:, lanes] for m in lasts], axis=1)


ABOUT = (8, 3 * LISTS, LANES)


def pick(field, about, which):
    return pl.pallas_call(
        functools.partial(pick_kernel, which),
        grid=(4,),
        in_specs=[
            pl.BlockSpec((1, HALVES * HALF, CELLS), lambda y: (y, 0, 0)),
            pl.BlockSpec(ABOUT, lambda y: (0, 0, 0)),
        ],
        out_specs=pl.BlockSpec((VIEWERS, GROUP, BLOCK), lambda y: (0, 0, 0)),
        out_shape=jax.ShapeDtypeStruct((VIEWERS, GROUP, BLOCK), F32),
        compiler_params=params(),
    )(field, about)


def mean_kernel(about_ref, near_ref, far_ref, mean_ref):
    slots = near_ref, far_ref
    mains = jnp.concatenate([s[0, :GROUP_MAIN, :] for s in slots], axis=0)
    lasts = jnp.concatenate([s[0, GROUP_MAIN : GROUP_MAIN + 4 * HALVES, :] for s in slots], axis=0)
    values = split_rows(jnp.concatenate([mains, lasts], axis=0))
    total = 16 * MAIN + 16
    for start in range(0, OBS, BLOCK):
        main = jnp.zeros((MAIN, BLOCK), F32)
        last = jnp.zeros((16, BLOCK), F32)
        for member in range(FOOT):
            low, high, weight = feet_of(about_ref, member, start)
            both = dot(values, one_hot(low, BLOCK))
            picked = both[:total] + both[total:]
            masked = jnp.where(lax.broadcasted_iota(jnp.int32, (16, BLOCK), 0) == high, weight, 0.0)
            for part in range(16):
                main = main + picked[part * MAIN : (part + 1) * MAIN] * masked[part : part + 1]
            last = last + picked[16 * MAIN :] * masked
        last = jnp.sum(last, axis=0, keepdims=True)
        for piece in range(BLOCK // LANES):
            lanes = slice(piece * LANES, (piece + 1) * LANES)
            at = start // LANES + piece
            mean_ref[0, at * MAIN : (at + 1) * MAIN, :] = main[:, lanes]
            mean_ref[0, 8 * MAIN + at : 8 * MAIN + at + 1, :] = last[:, lanes]


def means(near, far, about):
    slots = pl.BlockSpec((1, GROUP, BLOCK), lambda v: (v, 0, 0))
    return pl.pallas_call(
        mean_kernel,
        grid=(VIEWERS,),
        in_specs=[pl.BlockSpec((1,) + ABOUT[1:], lambda v: (v, 0, 0)), slots, slots],
        out_specs=pl.BlockSpec((1, COLUMN, LANES), lambda v: (v, 0, 0)),
        out_shape=jax.ShapeDtypeStruct((VIEWERS, COLUMN, LANES), F32),
        compiler_params=params(),
    )(about, near, far)


def pull_kernel(mean_ref, hessian_ref, constant_ref, pulled_ref):
    columns = []
    for at in range(8):
        pieces = [mean_ref[m, at * MAIN : (at + 1) * MAIN, :] for m in range(8)]
        pieces += [mean_ref[m, 8 * MAIN + at : 8 * MAIN + at + 1, :] for m in range(8)]
        columns.append(jnp.concatenate(pieces, axis=0))
    pulled = lax.dot_general(
        hessian_ref[...],
        jnp.concatenate(columns, axis=1),
        (((1,), (0,)), ((), ())),
        precision=HIGHEST,
        preferred_element_type=F32,
    )
    pulled = pulled - constant_ref[...]
    for at in range(8):
        lanes = slice(at * LANES, (at + 1) * LANES)
        for m in range(8):
            pulled_ref[m, at * MAIN : (at + 1) * MAIN, :] = pulled[m * MAIN : (m + 1) * MAIN, lanes]
            pulled_ref[m, 8 * MAIN + at : 8 * MAIN + at + 1, :] = pulled[8 * MAIN + m : 8 * MAIN + m + 1, lanes]


def pull(mean, hessian, constant):
    return pl.pallas_call(
        pull_kernel,
        out_shape=jax.ShapeDtypeStruct((8, COLUMN, LANES), F32),
        compiler_params=params(),
    )(mean, hessian, constant)


def spread_kernel(grad_ref, about_ref, near_ref, far_ref):
    count = 16 * MAIN + 16
    total = jnp.zeros((2 * count, BLOCK), F32)
    for start in range(0, OBS, BLOCK):
        main = []
        last = []
        for at in range(start // LANES, (start + BLOCK) // LANES):
            main.append(grad_ref[0, at * MAIN : (at + 1) * MAIN, :])
            last.append(grad_ref[0, 8 * MAIN + at : 8 * MAIN + at + 1, :])
        main = jnp.concatenate(main, axis=1)
        last = jnp.concatenate(last, axis=1)
        for member in range(FOOT):
            low, high, weight = feet_of(about_ref, member, start)
            hit = jnp.where(lax.broadcasted_iota(jnp.int32, (16, BLOCK), 0) == high, 1.0, 0.0)
            main_high, main_low = split(main * weight)
            last_high, last_low = split(last * weight * hit)
            hits = [jnp.broadcast_to(hit[part : part + 1], (MAIN, BLOCK)).astype(BF16) for part in range(16)]
            rows = jnp.concatenate(
                [main_high * h for h in hits] + [last_high] + [main_low * h for h in hits] + [last_low], axis=0
            )
            total = total + dot_nt(rows, one_hot(low, BLOCK))
    total = total[:count] + total[count:]
    for group, slots_ref in enumerate((near_ref, far_ref)):
        slots_ref[0, :GROUP_MAIN, :] = total[group * GROUP_MAIN : (group + 1) * GROUP_MAIN]
        at = 16 * MAIN + group * 4 * HALVES
        slots_ref[0, GROUP_MAIN : GROUP_MAIN + 4 * HALVES, :] = total[at : at + 4 * HALVES]


def spread(grad, about):
    slots = pl.BlockSpec((1, GROUP, BLOCK), lambda v: (v, 0, 0))
    return pl.pallas_call(
        spread_kernel,
        grid=(VIEWERS,),
        in_specs=[
            pl.BlockSpec((1, COLUMN, LANES), lambda v: (v, 0, 0)),
            pl.BlockSpec((1,) + ABOUT[1:], lambda v: (v, 0, 0)),
        ],
        out_specs=[slots] * 2,
        out_shape=[jax.ShapeDtypeStruct((VIEWERS, GROUP, BLOCK), F32)] * 2,
        compiler_params=params(),
    )(grad, about)


def put_kernel(which, slots_ref, about_ref, field_ref):
    tile = pl.program_id(0)
    lists = lists_of(about_ref, tile, which)
    for half in range(HALVES):
        base = half * HALF
        place = 4 * half + tile
        start = pl.multiple_of(place * MAIN, MAIN)
        mains = [slots_ref[viewer, pl.ds(start, MAIN), :] for viewer in range(VIEWERS)]
        lasts = [slots_ref[viewer, pl.ds(GROUP_MAIN + place, 1), :] for viewer in range(VIEWERS)]
        tails = []
        for quarter in range(4):
            index = lists[4 * half + quarter]
            cell = jnp.bitwise_and(index, CELLS - 1)
            second = index >= CELLS
            lanes = slice(quarter * CAP, (quarter + 1) * CAP)
            main = jnp.concatenate([m[:, lanes] for m in mains], axis=1)
            last = jnp.concatenate([m[:, lanes] for m in lasts], axis=1)
            row = lax.broadcasted_iota(jnp.int32, (8, VIEWERS * CAP), 0)
            tail = jnp.where(row == jnp.where(second, 1, 0), last, 0.0)
            rows = jnp.concatenate([jnp.where(second, 0.0, main), jnp.where(second, main, 0.0), tail], axis=0)
            count = OWNER + 8
            both = dot_nt(split_rows(rows), one_hot(cell, CELLS))
            back = both[:count] + both[count:]
            field_ref[0, base + quarter * OWNER : base + (quarter + 1) * OWNER, :] = back[:OWNER]
            tails.append(back[OWNER : OWNER + 2])
        field_ref[0, base + 4 * OWNER : base + HALF, :] = jnp.concatenate(tails, axis=0)


def put(slots, about, which):
    return pl.pallas_call(
        functools.partial(put_kernel, which),
        grid=(4,),
        in_specs=[
            pl.BlockSpec((VIEWERS, GROUP, BLOCK), lambda y: (0, 0, 0)),
            pl.BlockSpec(ABOUT, lambda y: (0, 0, 0)),
        ],
        out_specs=pl.BlockSpec((1, HALVES * HALF, CELLS), lambda y: (y, 0, 0)),
        out_shape=jax.ShapeDtypeStruct((4, HALVES * HALF, CELLS), F32),
        compiler_params=params(),
    )(slots, about)


def add_kernel(parts_ref, sums_ref):
    total = parts_ref[0] + parts_ref[1] + parts_ref[2] + parts_ref[3]
    for copy in range(4):
        sums_ref[copy] = total


def add(parts):
    return pl.pallas_call(
        add_kernel, out_shape=jax.ShapeDtypeStruct(parts.shape, F32), compiler_params=params()
    )(parts)


def start_kernel(lat_ref, near_ref, far_ref, serve_ref, field_ref, copies_ref):
    size = HALVES * HALF
    copies_ref[:, size:, :LANES] = serve_ref[...]
    copies_ref[:, size:, LANES:] = jnp.zeros_like(serve_ref)
    levels = []
    for level in range(LEVELS):
        rows = jnp.concatenate([ref[x, level] for ref in (near_ref, far_ref) for x in range(4)], axis=0)
        levels.append(
            lax.dot_general(
                lat_ref[...], rows, (((1,), (0,)), ((), ())), precision=HIGHEST, preferred_element_type=F32
            )
        )
    main = jnp.swapaxes(jnp.stack(levels[:MAIN], axis=0), 0, 1)
    main = main.reshape(16 * MAIN, CELLS)
    for half in range(HALVES):
        rows = main[half * 8 * MAIN : (half + 1) * 8 * MAIN]
        last = levels[MAIN][8 * half : 8 * half + 8]
        base = half * HALF
        field_ref[base : base + 8 * MAIN, :] = rows
        field_ref[base + 8 * MAIN : base + HALF, :] = last
        for copy in range(4):
            copies_ref[copy, base : base + 8 * MAIN, :] = rows
            copies_ref[copy, base + 8 * MAIN : base + HALF, :] = last


def start(lat, near, far, serve):
    size = HALVES * HALF
    return pl.pallas_call(
        start_kernel,
        out_shape=[
            jax.ShapeDtypeStruct((size, CELLS), F32),
            jax.ShapeDtypeStruct((4, size + 8, CELLS), F32),
        ],
        compiler_params=params(),
    )(lat, near, far, serve)


def finish_kernel(chi_ref, lat_ref, *refs):
    bands, out_ref = refs[:-1], refs[-1]
    mains = []
    lasts = []
    for near_far in range(2):
        for half in range(2):
            ref = bands[near_far]
            base = half * HALF
            for x in range(4):
                main = ref[x, base : base + 4 * OWNER, :].reshape(8, MAIN, CELLS)
                mains.append(jnp.swapaxes(main, 0, 1))
                lasts.append(ref[x, base + 4 * OWNER : base + HALF, :])
    for level in range(LEVELS):
        rows = jnp.concatenate([m[level] for m in mains] if level < MAIN else lasts, axis=0)
        out_ref[level] = chi_ref[level] + lax.dot_general(
            lat_ref[...], rows, (((1,), (0,)), ((), ())), precision=HIGHEST, preferred_element_type=F32
        )


def finish(chi, lat, bands):
    return pl.pallas_call(
        finish_kernel,
        out_shape=jax.ShapeDtypeStruct(chi.shape, F32),
        compiler_params=params(),
    )(chi, lat, *bands)


def exchange(blocks, axis):
    return lax.all_to_all(blocks, axis, 0, 0, axis_index_groups=ALONG)


def to_all(block, axis):
    return exchange(jnp.broadcast_to(block[None], (4,) + block.shape), axis)


def both_of(x, step, axis):
    other = lax.ppermute(x, "lev", [(m, m ^ step) for m in range(8)])
    upper = (lax.axis_index("lev") // step) % 2
    return jnp.where(upper == 0, jnp.stack([x, other], axis), jnp.stack([other, x], axis))


def product(tiles, matrix):
    return jnp.einsum("yrc,ycd->rd", tiles, matrix, precision=HIGHEST, preferred_element_type=F32)


def shards(
    chi,
    mat_lon,
    mat_lat,
    mat_vert,
    chan_table,
    chan_map,
    error_weight,
    innovation,
    foot_weight,
    foot_slot,
    serve_cols,
):
    half = lax.axis_index("obs") % 2
    core = lax.axis_index("lat") % 2

    def near_far(x, axis, which):
        near = lax.dynamic_index_in_dim(x, which, axis, keepdims=False)
        far = lax.dynamic_index_in_dim(x, 1 - which, axis, keepdims=False)
        return near, far

    tile = (foot_slot >> 6) & 7
    slab = foot_slot >> 9
    group = 2 * ((tile & 1) ^ half) + (slab >> 2)
    place = (4 * group + (tile >> 1)) * BLOCK + (slab & 3) * CAP + (foot_slot & (CAP - 1))

    serve = serve_cols[0, 0].astype(F32).reshape(8, 4, 2, CAP).transpose(2, 1, 0, 3)
    near, far = near_far(serve, 0, half)
    half_piece = 2 * lax.axis_index("lat") + lax.axis_index("lev") % 2
    piece = lax.dynamic_index_in_dim(mat_lon.reshape(16, LANES, CELLS), half_piece, 0, keepdims=False)
    piece = jnp.concatenate([piece, far.reshape(8, CELLS)], axis=0)
    piece = lax.ppermute(piece, "obs", PARTNER)
    serve = jnp.stack([near, piece[LANES:].reshape(4, VIEWERS, CAP)], axis=1)
    serve = serve.reshape(4, 8, LANES)
    piece = both_of(piece[:LANES], 1, 0).reshape(CELLS, CELLS)
    band_near = to_all(chi, "lat")

    vertical = mat_vert.reshape(8 * LEVELS, 8, LEVELS)
    vertical = jnp.concatenate([vertical[:, :, :MAIN].reshape(8 * LEVELS, 8 * MAIN), vertical[:, :, MAIN]], axis=1)
    matches = (
        chan_map[:, None] == jnp.arange(chan_table.shape[0], dtype=jnp.int32)[None, :]
    ).astype(F32)
    selected = jnp.dot(matches, chan_table, precision=HIGHEST, preferred_element_type=F32)
    selected = jnp.dot(selected, vertical, precision=HIGHEST, preferred_element_type=F32)
    scaled = error_weight[:, None] * selected
    hessian = jnp.dot(selected.T, scaled, precision=HIGHEST, preferred_element_type=F32)
    constant = jnp.dot(scaled.T, innovation, precision=HIGHEST, preferred_element_type=F32)
    lats = near_far(mat_lat.reshape(16, 4, 2, 16), 2, core)
    lat_start = jnp.stack(lats, axis=1).reshape(16, 128)
    lat_finish = jnp.stack([m.reshape(16, 4, 2, 8).transpose(0, 2, 1, 3) for m in lats], axis=1).reshape(16, 128)
    band_near, serve, hessian, constant, lat_start, lat_finish = lax.optimization_barrier(
        (band_near, serve, hessian, constant, lat_start, lat_finish)
    )
    other_lon = lax.all_gather(piece, "lat", axis=0, tiled=False)
    lon_near, lon_far = near_far(mat_lon.reshape(4, 2, CELLS, CELLS), 1, half)
    other_near, other_far = near_far(other_lon.reshape(4, 2, CELLS, CELLS), 1, half)

    band_far = lax.ppermute(band_near, "lat", PARTNER)
    field, copies = start(lat_start, band_near, band_far, serve)
    other = lax.ppermute(field, "obs", PARTNER)
    near_tiles = exchange(copies, "obs")
    serve = near_tiles[:, HALVES * HALF :, :LANES]
    near_tiles = near_tiles[:, : HALVES * HALF]
    about = [x.reshape(LISTS, LANES) for x in (serve, place.astype(F32), foot_weight)]
    about = jnp.concatenate(about, axis=0)
    about, other = lax.optimization_barrier((about, other))
    far_tiles = to_all(other, "obs")
    about = both_of(about, 4, 0)
    about, far_tiles = lax.optimization_barrier((about, far_tiles))
    tile_near = product(near_tiles, lon_near) + product(far_tiles, lon_far)
    tile_far = product(near_tiles, other_near) + product(far_tiles, other_far)
    near_tiles = to_all(tile_near, "obs")
    about = both_of(about, 2, 1)
    about, near_tiles = lax.optimization_barrier((about, near_tiles))
    about = both_of(about, 1, 2).reshape(ABOUT)
    near = pick(near_tiles, about, 0)
    far = pick(to_all(tile_far, "obs"), about, 1)

    mean = lax.all_to_all(means(near, far, about), "lev", 0, 0)
    pulled = lax.all_to_all(pull(mean, hessian, constant), "lev", 0, 0)
    near, far = spread(pulled, about)

    far_tiles = exchange(add(exchange(put(far, about, 1), "obs")), "obs")
    near_tiles = exchange(add(exchange(put(near, about, 0), "obs")), "obs")
    far = product(far_tiles, other_far) + product(near_tiles, other_near)
    far = lax.ppermute(far, "obs", PARTNER)
    field = product(far_tiles, lon_far) + product(near_tiles, lon_near) + far
    band_near = to_all(field, "lat")
    band_far = lax.ppermute(band_near, "lat", PARTNER)
    return finish(chi, lat_finish, [band_near, band_far])


def solution(mesh):
    in_specs = (
        P("lev", "lat", "obs"),
        P(None, "obs"),
        P("lat", None),
        P(),
        P(),
        P(),
        P(),
        P(None, ("lat", "lev", "obs")),
        P(None, ("lat", "lev", "obs")),
        P(None, ("lat", "lev", "obs")),
        P("lat", ("lev", "obs"), None, None),
    )
    out_specs = P("lev", "lat", "obs")
    return jax.shard_map(shards, mesh=mesh, in_specs=in_specs, out_specs=out_specs, check_vma=False)
```

time: 443 us -> 400 us (0.903)
  the two profiles are of different devices: /device:TPU:161 before, /device:TPU:1 now
where the time goes in v4:
time: 400 us; the launch traced here: 393 us
  starting transfers between devices  108 us (27%)
  waiting for transfers between devices  90.5 us (23%)
  blocking collectives  83.7 us (21%)
  Pallas kernels  43.2 us (11%)
  local copies, waits for them, and re-layouts  25.1 us (6%)
  matrix products  23.2 us (6%)
  between operations  14.1 us (4%)
  other arithmetic  4.94 us (1%)
    all_to_all x9, waiting for transfers between devices, exchange(): return lax.all_to_all(blocks, axis, 0, 0, axis_index_groups=ALONG)  59.2 us
    all_to_all x9, starting transfers between devices, exchange(): return lax.all_to_all(blocks, axis, 0, 0, axis_index_groups=ALONG)  35.7 us
    all_to_all x1, blocking collectives, shards(): pulled = lax.all_to_all(pull(mean, hessian, constant), 'lev', 0, 0)  33.9 us
    all_to_all x1, blocking collectives, shards(): mean = lax.all_to_all(means(near, far, about), 'lev', 0, 0)  33.4 us
    ppermute x4, starting transfers between devices, both_of(): other = lax.ppermute(x, 'lev', [(m, m ^ step) for m in range(8)])  23.4 us
    ppermute x2, starting transfers between devices, shards(): band_far = lax.ppermute(band_near, 'lat', PARTNER)  21.6 us
    dot_general x8, matrix products, product(): jnp.einsum('yrc,ycd->rd', tiles, matrix, precision=HIGHEST, preferred_ele...  17.5 us
    all_to_all x1, blocking collectives, exchange(): return lax.all_to_all(blocks, axis, 0, 0, axis_index_groups=ALONG)  16.4 us
  transfers between devices with their start and end apart: 19, of which 15 were waited for; matrix products, arithmetic and copies ran while one was open for 9% of the time, Pallas kernels for 2%

profile of v4, /device:TPU:1, one launch (start us, length us, event | category | flops | bytes accessed | tf_op | source)
XLA Modules:
  0.0 393.2 jit_solution(12019428713501541673)
XLA Ops:
  8.8 16.3 %collective-permute-start = (f32[136,256]{1,0:T(8,128)}, f32[136,256]{1,0:T(8,128)}, u32[]{:S(2)}, u32[]{:S(2)}) collective-permute-start(f32[136,256]{1,0:T(8,128)} %pad_maximum_fusion), channel_id=1, source_target_pairs={{0,1},{1,0},{2,3},{3,2},{4,5},{5,4},{6,7},{7,6},{8,9},{9,8},{10,11... | collective-permute-start | bytes 417800 | tf_op jit(solution)/shard_map/ppermute | solution.py:400
  27.3 4.1 %all-to-all-start = ((f32[4,17,16,256]{3,2,1,0:T(8,128)}), f32[4,17,16,256]{3,2,1,0:T(8,128)S(1)}, u32[]{:S(2)}, u32[]{:S(2)}) async-start(f32[4,17,16,256]{3,2,1,0:T(8,128)} %broadcast_in_dim.10), calls=%async_computation | async-start | bytes 2228224 | tf_op jit(solution)/shard_map/all_to_all | solution.py:352
  46.0 4.1 %collective-permute-start.1 = (f32[4,17,16,256]{3,2,1,0:T(8,128)S(1)}, f32[4,17,16,256]{3,2,1,0:T(8,128)}, u32[]{:S(2)}, u32[]{:S(2)}) collective-permute-start(f32[4,17,16,256]{3,2,1,0:T(8,128)S(1)} %all-to-all-done.near_ref), channel_id=1, source_target_pairs={{0,64},{64,0},{128,192},{192,128},{256,320},{320,256},{384,448},{4... | collective-permute-start | bytes 3342344 | tf_op jit(solution)/shard_map/ppermute | solution.py:426
  54.3 4.7 %collective-permute-done.6 = f32[128,256]{1,0:T(8,128)} collective-permute-done((f32[128,256]{1,0:T(8,128)}, f32[128,256]{1,0:T(8,128)}, u32[]{:S(2)}, u32[]{:S(2)}) %collective-permute-start.6) | collective-permute-done | bytes 131104 | tf_op jit(solution)/shard_map/ppermute | solution.py:360
  64.8 4.4 %all-to-all-start.1 = ((f32[4,280,256]{2,1,0:T(8,128)}), f32[4,280,256]{2,1,0:T(8,128)}, u32[]{:S(2)}, u32[]{:S(2)}) async-start(f32[4,280,256]{2,1,0:T(8,128)} %copy-done.10), calls=%async_computation.1 | async-start | bytes 2293760 | tf_op jit(solution)/shard_map/all_to_all | solution.py:352
  72.4 12.0 %all-to-all-done.1 = f32[4,280,256]{2,1,0:T(8,128)} async-done(((f32[4,280,256]{2,1,0:T(8,128)}), f32[4,280,256]{2,1,0:T(8,128)}, u32[]{:S(2)}, u32[]{:S(2)}) %all-to-all-start.1) | async-done | bytes 1146912 | tf_op jit(solution)/shard_map/all_to_all | solution.py:352
  85.2 9.4 %collective-permute-done.2 = f32[272,256]{1,0:T(8,128)S(1)} collective-permute-done((f32[272,256]{1,0:T(8,128)S(1)}, f32[272,256]{1,0:T(8,128)S(1)}, u32[]{:S(2)}, u32[]{:S(2)}) %collective-permute-start.2) | collective-permute-done | bytes 278560 | tf_op jit(solution)/shard_map/ppermute | solution.py:428
  95.7 3.8 all-to-all-start.2
  99.5 3.8 collective-permute-start.3
  103.3 4.9 %collective-permute-done.3 = f32[96,128]{1,0:T(8,128)S(1)} collective-permute-done((f32[96,128]{1,0:T(8,128)S(1)}, f32[96,128]{1,0:T(8,128)S(1)}, u32[]{:S(2)}, u32[]{:S(2)}) %collective-permute-start.3) | collective-permute-done | bytes 49184 | tf_op jit(solution)/shard_map/ppermute | solution.py:360
  108.2 5.6 %all-to-all-done.2 = f32[4,272,256]{2,1,0:T(8,128)S(1)} async-done(((f32[4,272,256]{2,1,0:T(8,128)}), f32[4,272,256]{2,1,0:T(8,128)S(1)}, u32[]{:S(2)}, u32[]{:S(2)}) %all-to-all-start.2) | async-done | bytes 1114144 | tf_op jit(solution)/shard_map/all_to_all | solution.py:352
  127.7 7.2 %all-to-all-done.3.field_ref = f32[4,272,256]{2,1,0:T(8,128)S(1)} async-done(((f32[4,272,256]{2,1,0:T(8,128)}), f32[4,272,256]{2,1,0:T(8,128)S(1)}, u32[]{:S(2)}, u32[]{:S(2)}) %all-to-all-start.3) | async-done | bytes 1114144 | tf_op jit(solution)/shard_map/all_to_all | solution.py:352
  137.1 4.3 %all-to-all-start.4 = ((f32[4,272,256]{2,1,0:T(8,128)}), f32[4,272,256]{2,1,0:T(8,128)}, u32[]{:S(2)}, u32[]{:S(2)}) async-start(f32[4,272,256]{2,1,0:T(8,128)} %broadcast_in_dim.13), calls=%async_computation.4 | async-start | bytes 2228224 | tf_op jit(solution)/shard_map/all_to_all | solution.py:352
  141.3 7.8 %collective-permute-start.4 = (f32[2,96,128]{2,1,0:T(8,128)S(1)}, f32[2,96,128]{2,1,0:T(8,128)S(1)}, u32[]{:S(2)}, u32[]{:S(2)}) collective-permute-start(f32[2,96,128]{2,1,0:T(8,128)S(1)} %maximum_select_fusion.3), channel_id=1, source_target_pairs={{0,16},{8,24},{16,0},{24,8},{32,48},{40,56},{48,32},{56,40},{1,17}... | collective-permute-start | bytes 294920 | tf_op jit(solution)/shard_map/ppermute | solution.py:360
  151.6 9.2 %collective-permute-start.5 = (f32[2,2,96,128]{3,2,1,0:T(8,128)S(1)}, f32[2,2,96,128]{3,2,1,0:T(8,128)S(1)}, u32[]{:S(2)}, u32[]{:S(2)}) collective-permute-start(f32[2,2,96,128]{3,2,1,0:T(8,128)S(1)} %maximum_select_fusion.2), channel_id=1, source_target_pairs={{0,8},{8,0},{16,24},{24,16},{32,40},{40,32},{48,56},{56,48},{1,9},... | collective-permute-start | bytes 589832 | tf_op jit(solution)/shard_map/ppermute | solution.py:360
  167.5 4.1 %shard_map.111.far_ref = f32[8,136,256]{2,1,0:T(8,128)S(1)} custom-call(f32[4,272,256]{2,1,0:T(8,128)} %all-to-all-done.4.field_ref, f32[8,96,128]{2,1,0:T(8,128)S(1)} %bitcast.118), custom_call_target="tpu_custom_call" | custom-call | tf_op jit(solution)/shard_map/pallas_call | solution.py:111
  171.7 11.1 %shard_map.112 = f32[8,136,128]{2,1,0:T(8,128)S(1)} custom-call(f32[8,96,128]{2,1,0:T(8,128)S(1)} %bitcast.119, f32[8,136,256]{2,1,0:T(8,128)S(1)} %copy-done.6, f32[8,136,256]{2,1,0:T(8,128)S(1)} %shard_map.111.far_ref), custom_call_target="tpu_custom_call" | custom-call | tf_op jit(solution)/shard_map/pallas_call | solution.py:151
  182.8 33.4 %all_to_all.60.mean_ref = f32[8,136,128]{2,1,0:T(8,128)S(1)} all-to-all(f32[8,136,128]{2,1,0:T(8,128)S(1)} %shard_map.112), channel_id=1, replica_groups=mesh['lat'=8,'lev'=8,'obs'=8] {'lev'}, dimensions={0} | all-to-all | bytes 1114112 | tf_op jit(solution)/shard_map/all_to_all | solution.py:447
  216.8 33.9 %all_to_all.61.grad_ref = f32[8,136,128]{2,1,0:T(8,128)S(1)} all-to-all(f32[8,136,128]{2,1,0:T(8,128)S(1)} %shard_map.113), channel_id=1, replica_groups=mesh['lat'=8,'lev'=8,'obs'=8] {'lev'}, dimensions={0} | all-to-all | bytes 1114112 | tf_op jit(solution)/shard_map/all_to_all | solution.py:448
  250.7 10.9 %shard_map.114 = (f32[8,136,256]{2,1,0:T(8,128)S(1)}, f32[8,136,256]{2,1,0:T(8,128)S(1)}) custom-call(f32[8,136,128]{2,1,0:T(8,128)S(1)} %all_to_all.61.grad_ref, f32[8,96,128]{2,1,0:T(8,128)S(1)} %bitcast.120), custom_call_target="tpu_custom_call" | custom-call | tf_op jit(solution)/shard_map/pallas_call | solution.py:220
  266.9 4.3 %all-to-all-start.9 = ((f32[4,272,256]{2,1,0:T(8,128)}), f32[4,272,256]{2,1,0:T(8,128)}, u32[]{:S(2)}, u32[]{:S(2)}) async-start(f32[4,272,256]{2,1,0:T(8,128)} %copy-done.4), calls=%async_computation.9 | async-start | bytes 2228224 | tf_op jit(solution)/shard_map/all_to_all | solution.py:352
  276.7 7.2 %all-to-all-done.9.parts_ref = f32[4,272,256]{2,1,0:T(8,128)} async-done(((f32[4,272,256]{2,1,0:T(8,128)}), f32[4,272,256]{2,1,0:T(8,128)}, u32[]{:S(2)}, u32[]{:S(2)}) %all-to-all-start.9) | async-done | bytes 1114144 | tf_op jit(solution)/shard_map/all_to_all | solution.py:352
  283.9 3.5 all-to-all-start.7
  289.7 9.0 %all-to-all-done.7.parts_ref = f32[4,272,256]{2,1,0:T(8,128)S(1)} async-done(((f32[4,272,256]{2,1,0:T(8,128)}), f32[4,272,256]{2,1,0:T(8,128)S(1)}, u32[]{:S(2)}, u32[]{:S(2)}) %all-to-all-start.7) | async-done | bytes 1114144 | tf_op jit(solution)/shard_map/all_to_all | solution.py:352
  298.8 4.3 %all-to-all-start.10 = ((f32[4,272,256]{2,1,0:T(8,128)}), f32[4,272,256]{2,1,0:T(8,128)}, u32[]{:S(2)}, u32[]{:S(2)}) async-start(f32[4,272,256]{2,1,0:T(8,128)} %copy-done.7), calls=%async_computation.10 | async-start | bytes 2228224 | tf_op jit(solution)/shard_map/all_to_all | solution.py:352
  304.2 9.1 %all-to-all-done.10 = f32[4,272,256]{2,1,0:T(8,128)} async-done(((f32[4,272,256]{2,1,0:T(8,128)}), f32[4,272,256]{2,1,0:T(8,128)}, u32[]{:S(2)}, u32[]{:S(2)}) %all-to-all-start.10) | async-done | bytes 1114144 | tf_op jit(solution)/shard_map/all_to_all | solution.py:352
  313.3 3.5 all-to-all-start.8
  319.5 7.4 %all-to-all-done.8 = f32[4,272,256]{2,1,0:T(8,128)S(1)} async-done(((f32[4,272,256]{2,1,0:T(8,128)}), f32[4,272,256]{2,1,0:T(8,128)S(1)}, u32[]{:S(2)}, u32[]{:S(2)}) %all-to-all-start.8) | async-done | bytes 1114144 | tf_op jit(solution)/shard_map/all_to_all | solution.py:352
  329.2 8.4 %collective-permute-start.7 = (f32[272,256]{1,0:T(8,128)S(1)}, f32[272,256]{1,0:T(8,128)S(1)}, u32[]{:S(2)}, u32[]{:S(2)}) collective-permute-start(f32[272,256]{1,0:T(8,128)S(1)} %fusion.4), channel_id=1, source_target_pairs={{0,1},{1,0},{2,3},{3,2},{4,5},{5,4},{6,7},{7,6},{8,9},{9,8},{10,11... | collective-permute-start | bytes 835592 | tf_op jit(solution)/shard_map/ppermute | solution.py:454
  339.9 5.5 %collective-permute-done.7 = f32[272,256]{1,0:T(8,128)S(1)} collective-permute-done((f32[272,256]{1,0:T(8,128)S(1)}, f32[272,256]{1,0:T(8,128)S(1)}, u32[]{:S(2)}, u32[]{:S(2)}) %collective-permute-start.7) | collective-permute-done | bytes 278560 | tf_op jit(solution)/shard_map/ppermute | solution.py:454
  346.6 16.4 %all_to_all.62.refs_0_ = f32[4,272,256]{2,1,0:T(8,128)S(1)} all-to-all(f32[4,272,256]{2,1,0:T(8,128)S(1)} %broadcast_in_dim.14), channel_id=1, replica_groups={{0,128,256,384},{64,192,320,448},{1,129,257,385},{65,193,321,449},{2,13..., dimensions={0} | all-to-all | bytes 2228224 | tf_op jit(solution)/shard_map/all_to_all | solution.py:352
  363.0 17.5 %collective-permute-start.8 = (f32[4,272,256]{2,1,0:T(8,128)S(1)}, f32[4,272,256]{2,1,0:T(8,128)}, u32[]{:S(2)}, u32[]{:S(2)}) collective-permute-start(f32[4,272,256]{2,1,0:T(8,128)S(1)} %all_to_all.62.refs_0_), channel_id=1, source_target_pairs={{0,64},{64,0},{128,192},{192,128},{256,320},{320,256},{384,448},{4... | collective-permute-start | bytes 3342344 | tf_op jit(solution)/shard_map/ppermute | solution.py:457
  (121 shorter events, 88.0 us)
Async XLA Ops:
  6.5 1.6 copy-start
  8.8 34.7 %collective-permute-start = (f32[136,256]{1,0:T(8,128)}, f32[136,256]{1,0:T(8,128)}, u32[]{:S(2)}, u32[]{:S(2)}) collective-permute-start(f32[136,256]{1,0:T(8,128)} %pad_maximum_fusion), channel_id=1, source_target_pairs={{0,1},{1,0},{2,3},{3,2},{4,5},{5,4},{6,7},{7,6},{8,9},{9,8},{10,11... | collective-permute-start | bytes 417800 | tf_op jit(solution)/shard_map/ppermute | solution.py:400
  27.3 4.2 %copy-start.21 = (f32[16,128]{1,0:T(8,128)S(1)}, f32[16,128]{1,0:T(8,128)}, u32[]{:S(2)}) copy-start(f32[16,128]{1,0:T(8,128)} %param.13) | copy-start | bytes 24580
  27.3 18.7 %all-to-all-start = ((f32[4,17,16,256]{3,2,1,0:T(8,128)}), f32[4,17,16,256]{3,2,1,0:T(8,128)S(1)}, u32[]{:S(2)}, u32[]{:S(2)}) async-start(f32[4,17,16,256]{3,2,1,0:T(8,128)} %broadcast_in_dim.10), calls=%async_computation | async-start | bytes 2228224 | tf_op jit(solution)/shard_map/all_to_all | solution.py:352
  31.4 6.4 %copy-start.22 = (s32[300]{0:T(512)S(1)}, s32[300]{0:T(512)}, u32[]{:S(2)}) copy-start(s32[300]{0:T(512)} %param.16) | copy-start | bytes 3604
  31.4 90.4 %all-gather.2.cloned.1.call-start = ((), (), s32[]{:S(2)}) async-start(), calls=%async_computation.12 | async-start | bytes 2359296 | tf_op jit(solution)/shard_map/all_gather | solution.py:422
  34.6 5.2 %copy-start.20 = (f32[300]{0:T(512)S(1)}, f32[300]{0:T(512)}, u32[]{:S(2)}) copy-start(f32[300]{0:T(512)} %param.17) | copy-start | bytes 3604
  46.0 14.7 %collective-permute-start.1 = (f32[4,17,16,256]{3,2,1,0:T(8,128)S(1)}, f32[4,17,16,256]{3,2,1,0:T(8,128)}, u32[]{:S(2)}, u32[]{:S(2)}) collective-permute-start(f32[4,17,16,256]{3,2,1,0:T(8,128)S(1)} %all-to-all-done.near_ref), channel_id=1, source_target_pairs={{0,64},{64,0},{128,192},{192,128},{256,320},{320,256},{384,448},{4... | collective-permute-start | bytes 3342344 | tf_op jit(solution)/shard_map/ppermute | solution.py:426
  51.7 7.3 %collective-permute-start.6 = (f32[128,256]{1,0:T(8,128)}, f32[128,256]{1,0:T(8,128)}, u32[]{:S(2)}, u32[]{:S(2)}) collective-permute-start(f32[128,256]{1,0:T(8,128)} %get-tuple-element.38), channel_id=1, source_target_pairs={{0,8},{8,0},{16,24},{24,16},{32,40},{40,32},{48,56},{56,48},{1,9},... | collective-permute-start | bytes 393224 | tf_op jit(solution)/shard_map/ppermute | solution.py:360
  64.8 4.4 %copy-start.18 = (s32[4,1024]{1,0:T(4,128)S(1)}, s32[4,1024]{1,0:T(4,128)}, u32[]{:S(2)}) copy-start(s32[4,1024]{1,0:T(4,128)} %param.20) | copy-start | bytes 49156
  64.8 4.5 %copy-start.19 = (f32[4,1024]{1,0:T(4,128)S(1)}, f32[4,1024]{1,0:T(4,128)}, u32[]{:S(2)}) copy-start(f32[4,1024]{1,0:T(4,128)} %param.19) | copy-start | bytes 49156
  64.8 4.5 %copy-start.15 = (f32[272,256]{1,0:T(8,128)S(1)}, f32[272,256]{1,0:T(8,128)}, u32[]{:S(2)}) copy-start(f32[272,256]{1,0:T(8,128)} %copy-done.14) | copy-start | bytes 835588
  64.8 19.6 %all-to-all-start.1 = ((f32[4,280,256]{2,1,0:T(8,128)}), f32[4,280,256]{2,1,0:T(8,128)}, u32[]{:S(2)}, u32[]{:S(2)}) async-start(f32[4,280,256]{2,1,0:T(8,128)} %copy-done.10), calls=%async_computation.1 | async-start | bytes 2293760 | tf_op jit(solution)/shard_map/all_to_all | solution.py:352
  69.3 25.3 %collective-permute-start.2 = (f32[272,256]{1,0:T(8,128)S(1)}, f32[272,256]{1,0:T(8,128)S(1)}, u32[]{:S(2)}, u32[]{:S(2)}) collective-permute-start(f32[272,256]{1,0:T(8,128)S(1)} %copy-done.15), channel_id=1, source_target_pairs={{0,1},{1,0},{2,3},{3,2},{4,5},{5,4},{6,7},{7,6},{8,9},{9,8},{10,11... | collective-permute-start | bytes 835592 | tf_op jit(solution)/shard_map/ppermute | solution.py:428
  95.7 18.1 %all-to-all-start.2 = ((f32[4,272,256]{2,1,0:T(8,128)}), f32[4,272,256]{2,1,0:T(8,128)S(1)}, u32[]{:S(2)}, u32[]{:S(2)}) async-start(f32[4,272,256]{2,1,0:T(8,128)} %broadcast_in_dim.11), calls=%async_computation.2 | async-start | bytes 2228224 | tf_op jit(solution)/shard_map/all_to_all | solution.py:352
  99.5 8.7 %collective-permute-start.3 = (f32[96,128]{1,0:T(8,128)S(1)}, f32[96,128]{1,0:T(8,128)S(1)}, u32[]{:S(2)}, u32[]{:S(2)}) collective-permute-start(f32[96,128]{1,0:T(8,128)S(1)} %pad_maximum_fusion.3), channel_id=1, source_target_pairs={{0,32},{8,40},{16,48},{24,56},{32,0},{40,8},{48,16},{56,24},{1,33}... | collective-permute-start | bytes 147464 | tf_op jit(solution)/shard_map/ppermute | solution.py:360
  118.3 16.6 %all-to-all-start.3 = ((f32[4,272,256]{2,1,0:T(8,128)}), f32[4,272,256]{2,1,0:T(8,128)S(1)}, u32[]{:S(2)}, u32[]{:S(2)}) async-start(f32[4,272,256]{2,1,0:T(8,128)} %broadcast_in_dim.12), calls=%async_computation.3 | async-start | bytes 2228224 | tf_op jit(solution)/shard_map/all_to_all | solution.py:352
  121.8 2.8 copy-start.17
  134.8 2.2 copy-start.1
  137.1 30.5 %all-to-all-start.4 = ((f32[4,272,256]{2,1,0:T(8,128)}), f32[4,272,256]{2,1,0:T(8,128)}, u32[]{:S(2)}, u32[]{:S(2)}) async-start(f32[4,272,256]{2,1,0:T(8,128)} %broadcast_in_dim.13), calls=%async_computation.4 | async-start | bytes 2228224 | tf_op jit(solution)/shard_map/all_to_all | solution.py:352
  141.3 10.2 %collective-permute-start.4 = (f32[2,96,128]{2,1,0:T(8,128)S(1)}, f32[2,96,128]{2,1,0:T(8,128)S(1)}, u32[]{:S(2)}, u32[]{:S(2)}) collective-permute-start(f32[2,96,128]{2,1,0:T(8,128)S(1)} %maximum_select_fusion.3), channel_id=1, source_target_pairs={{0,16},{8,24},{16,0},{24,8},{32,48},{40,56},{48,32},{56,40},{1,17}... | collective-permute-start | bytes 294920 | tf_op jit(solution)/shard_map/ppermute | solution.py:360
  149.2 14.4 %copy-start.2 = (f32[4,272,256]{2,1,0:T(8,128)S(1)}, f32[4,272,256]{2,1,0:T(8,128)}, u32[]{:S(2)}) copy-start(f32[4,272,256]{2,1,0:T(8,128)} %copy-done.1) | copy-start | bytes 3342340
  151.6 12.0 %collective-permute-start.5 = (f32[2,2,96,128]{3,2,1,0:T(8,128)S(1)}, f32[2,2,96,128]{3,2,1,0:T(8,128)S(1)}, u32[]{:S(2)}, u32[]{:S(2)}) collective-permute-start(f32[2,2,96,128]{3,2,1,0:T(8,128)S(1)} %maximum_select_fusion.2), channel_id=1, source_target_pairs={{0,8},{8,0},{16,24},{24,16},{32,40},{40,32},{48,56},{56,48},{1,9},... | collective-permute-start | bytes 589832 | tf_op jit(solution)/shard_map/ppermute | solution.py:360
  167.5 4.2 %copy-start.6 = (f32[8,136,256]{2,1,0:T(8,128)S(1)}, f32[8,136,256]{2,1,0:T(8,128)}, u32[]{:S(2)}) copy-start(f32[8,136,256]{2,1,0:T(8,128)} %copy-done.5) | copy-start | bytes 3342340
  182.8 33.4 %copy-start.9 = (f32[136,1024]{1,0:T(8,128)S(1)}, f32[136,1024]{1,0:T(8,128)}, u32[]{:S(2)}) copy-start(f32[136,1024]{1,0:T(8,128)} %fusion.25.constant_ref) | copy-start | bytes 1671172
  266.9 17.0 %all-to-all-start.9 = ((f32[4,272,256]{2,1,0:T(8,128)}), f32[4,272,256]{2,1,0:T(8,128)}, u32[]{:S(2)}, u32[]{:S(2)}) async-start(f32[4,272,256]{2,1,0:T(8,128)} %copy-done.4), calls=%async_computation.9 | async-start | bytes 2228224 | tf_op jit(solution)/shard_map/all_to_all | solution.py:352
  283.9 14.9 %all-to-all-start.7 = ((f32[4,272,256]{2,1,0:T(8,128)}), f32[4,272,256]{2,1,0:T(8,128)S(1)}, u32[]{:S(2)}, u32[]{:S(2)}) async-start(f32[4,272,256]{2,1,0:T(8,128)} %copy-done.3), calls=%async_computation.7 | async-start | bytes 2228224 | tf_op jit(solution)/shard_map/all_to_all | solution.py:352
  298.8 14.5 %all-to-all-start.10 = ((f32[4,272,256]{2,1,0:T(8,128)}), f32[4,272,256]{2,1,0:T(8,128)}, u32[]{:S(2)}, u32[]{:S(2)}) async-start(f32[4,272,256]{2,1,0:T(8,128)} %copy-done.7), calls=%async_computation.10 | async-start | bytes 2228224 | tf_op jit(solution)/shard_map/all_to_all | solution.py:352
  313.3 13.6 %all-to-all-start.8 = ((f32[4,272,256]{2,1,0:T(8,128)}), f32[4,272,256]{2,1,0:T(8,128)S(1)}, u32[]{:S(2)}, u32[]{:S(2)}) async-start(f32[4,272,256]{2,1,0:T(8,128)} %copy-done.8), calls=%async_computation.8 | async-start | bytes 2228224 | tf_op jit(solution)/shard_map/all_to_all | solution.py:352
  329.2 16.2 %collective-permute-start.7 = (f32[272,256]{1,0:T(8,128)S(1)}, f32[272,256]{1,0:T(8,128)S(1)}, u32[]{:S(2)}, u32[]{:S(2)}) collective-permute-start(f32[272,256]{1,0:T(8,128)S(1)} %fusion.4), channel_id=1, source_target_pairs={{0,1},{1,0},{2,3},{3,2},{4,5},{5,4},{6,7},{7,6},{8,9},{9,8},{10,11... | collective-permute-start | bytes 835592 | tf_op jit(solution)/shard_map/ppermute | solution.py:454
  346.6 36.4 %copy-start.13 = (f32[17,16,256]{2,1,0:T(8,128)S(1)}, f32[17,16,256]{2,1,0:T(8,128)}, u32[]{:S(2)}) copy-start(f32[17,16,256]{2,1,0:T(8,128)} %chi_ref.1) | copy-start | bytes 835588
  363.0 20.0 %collective-permute-start.8 = (f32[4,272,256]{2,1,0:T(8,128)S(1)}, f32[4,272,256]{2,1,0:T(8,128)}, u32[]{:S(2)}, u32[]{:S(2)}) collective-permute-start(f32[4,272,256]{2,1,0:T(8,128)S(1)} %all_to_all.62.refs_0_), channel_id=1, source_target_pairs={{0,64},{64,0},{128,192},{192,128},{256,320},{320,256},{384,448},{4... | collective-permute-start | bytes 3342344 | tf_op jit(solution)/shard_map/ppermute | solution.py:457
  (10 other events, 10.1 us)
Sparse Core Ops, SparseCore 0:
  60.8 25.8 all-gather.1

commit v5 on v4

--- a/solution.py
+++ b/solution.py
@@ -363,7 +363,7 @@
 
 
 def product(tiles, matrix):
-    return jnp.einsum("yrc,ycd->rd", tiles, matrix, precision=HIGHEST, preferred_element_type=F32)
+    return jnp.einsum("yrc,ycd->rd", tiles, matrix, precision=lax.Precision.HIGH, preferred_element_type=F32)
 
 
 def shards(
@@ -400,7 +400,6 @@
     piece = lax.ppermute(piece, "obs", PARTNER)
     serve = jnp.stack([near, piece[LANES:].reshape(4, VIEWERS, CAP)], axis=1)
     serve = serve.reshape(4, 8, LANES)
-    piece = both_of(piece[:LANES], 1, 0).reshape(CELLS, CELLS)
     band_near = to_all(chi, "lat")
 
     vertical = mat_vert.reshape(8 * LEVELS, 8, LEVELS)
@@ -419,14 +418,17 @@
     band_near, serve, hessian, constant, lat_start, lat_finish = lax.optimization_barrier(
         (band_near, serve, hessian, constant, lat_start, lat_finish)
     )
-    other_lon = lax.all_gather(piece, "lat", axis=0, tiled=False)
     lon_near, lon_far = near_far(mat_lon.reshape(4, 2, CELLS, CELLS), 1, half)
-    other_near, other_far = near_far(other_lon.reshape(4, 2, CELLS, CELLS), 1, half)
 
     band_far = lax.ppermute(band_near, "lat", PARTNER)
     field, copies = start(lat_start, band_near, band_far, serve)
     other = lax.ppermute(field, "obs", PARTNER)
     near_tiles = exchange(copies, "obs")
+    piece, near_tiles = lax.optimization_barrier((piece, near_tiles))
+    piece = both_of(piece[:LANES], 1, 0).reshape(CELLS, CELLS)
+    piece, other = lax.optimization_barrier((piece, other))
+    other_lon = lax.all_gather(piece, "lat", axis=0, tiled=False)
+    other_near, other_far = near_far(other_lon.reshape(4, 2, CELLS, CELLS), 1, half)
     serve = near_tiles[:, HALVES * HALF :, :LANES]
     near_tiles = near_tiles[:, : HALVES * HALF]
     about = [x.reshape(LISTS, LANES) for x in (serve, place.astype(F32), foot_weight)]
@@ -439,10 +441,11 @@
     tile_far = product(near_tiles, other_near) + product(far_tiles, other_far)
     near_tiles = to_all(tile_near, "obs")
     about = both_of(about, 2, 1)
-    about, near_tiles = lax.optimization_barrier((about, near_tiles))
     about = both_of(about, 1, 2).reshape(ABOUT)
+    copies = jnp.broadcast_to(tile_far[None], (4,) + tile_far.shape)
+    about, copies = lax.optimization_barrier((about, copies))
     near = pick(near_tiles, about, 0)
-    far = pick(to_all(tile_far, "obs"), about, 1)
+    far = pick(exchange(copies, "obs"), about, 1)
 
     mean = lax.all_to_all(means(near, far, about), "lev", 0, 0)
     pulled = lax.all_to_all(pull(mean, hessian, constant), "lev", 0, 0)

time: 400 us -> 391 us (0.978); the launches traced: 393 us -> 389 us
  waiting for transfers between devices: 90.5 us -> 103 us
  starting transfers between devices: 108 us -> 101 us
  matrix products: 23.2 us -> 19 us
    ppermute x4, starting transfers between devices: 23.4 us -> 9.59 us  [both_of(): other = lax.ppermute(x, 'lev', [(m, m ^ step) for m in range(8)])]
    ppermute x4, waiting for transfers between devices: 14.8 us -> 26.2 us  [both_of(): other = lax.ppermute(x, 'lev', [(m, m ^ step) for m in range(8)])]
    ppermute x1, waiting for transfers between devices: 9.44 us -> 0.01 us  [shards(): other = lax.ppermute(field, 'obs', PARTNER)]
    ppermute x2, starting transfers between devices: 21.6 us -> 29.4 us  [shards(): band_far = lax.ppermute(band_near, 'lat', PARTNER)]
    all_to_all x9, waiting for transfers between devices: 59.2 us -> 66 us  [exchange(): return lax.all_to_all(blocks, axis, 0, 0, axis_index_groups=ALONG)]
    dot_general x8, matrix products: 17.5 us -> 13.3 us  [product(): jnp.einsum('yrc,ycd->rd', tiles, matrix, precision=lax.Precision.HIGH, pr...]
    unnamed x50 -> x46, local copies, waits for them, and re-layouts: 10.8 us -> 10.8 us
  transfers between devices with their start and end apart: 19 -> 19, of which waited for: 15 -> 15; matrix products, arithmetic and copies ran while one was open for 9% -> 8% of each run, Pallas kernels for 2% -> 2%
where the time goes in v5:
time: 391 us; the launch traced here: 389 us
  waiting for transfers between devices  103 us (26%)
  starting transfers between devices  101 us (26%)
  blocking collectives  81.2 us (21%)
  Pallas kernels  43.2 us (11%)
  local copies, waits for them, and re-layouts  23.4 us (6%)
  matrix products  19 us (5%)
  between operations  14.1 us (4%)
  other arithmetic  4.03 us (1%)
    all_to_all x9, waiting for transfers between devices, exchange(): return lax.all_to_all(blocks, axis, 0, 0, axis_index_groups=ALONG)  66 us
    all_to_all x9, starting transfers between devices, exchange(): return lax.all_to_all(blocks, axis, 0, 0, axis_index_groups=ALONG)  36.1 us
    all_to_all x1, blocking collectives, shards(): pulled = lax.all_to_all(pull(mean, hessian, constant), 'lev', 0, 0)  33.9 us
    all_to_all x1, blocking collectives, shards(): mean = lax.all_to_all(means(near, far, about), 'lev', 0, 0)  32.7 us
    ppermute x2, starting transfers between devices, shards(): band_far = lax.ppermute(band_near, 'lat', PARTNER)  29.4 us
    ppermute x4, waiting for transfers between devices, both_of(): other = lax.ppermute(x, 'lev', [(m, m ^ step) for m in range(8)])  26.2 us
    ppermute x1, starting transfers between devices, shards(): piece = lax.ppermute(piece, 'obs', PARTNER)  16.3 us
    all_to_all x1, blocking collectives, exchange(): return lax.all_to_all(blocks, axis, 0, 0, axis_index_groups=ALONG)  14.5 us
  transfers between devices with their start and end apart: 19, of which 15 were waited for; matrix products, arithmetic and copies ran while one was open for 8% of the time, Pallas kernels for 2%

profile of v5, /device:TPU:1, one launch (start us, length us, event | category | flops | bytes accessed | tf_op | source)
XLA Modules:
  0.0 388.6 jit_solution(9036094173360990708)
XLA Ops:
  8.8 16.3 %collective-permute-start = (f32[136,256]{1,0:T(8,128)}, f32[136,256]{1,0:T(8,128)}, u32[]{:S(2)}, u32[]{:S(2)}) collective-permute-start(f32[136,256]{1,0:T(8,128)} %pad_maximum_fusion.2), channel_id=1, source_target_pairs={{0,1},{1,0},{2,3},{3,2},{4,5},{5,4},{6,7},{7,6},{8,9},{9,8},{10,11... | collective-permute-start | bytes 417800 | tf_op jit(solution)/shard_map/ppermute | solution.py:400
  27.3 4.1 %all-to-all-start = ((f32[4,17,16,256]{3,2,1,0:T(8,128)}), f32[4,17,16,256]{3,2,1,0:T(8,128)S(1)}, u32[]{:S(2)}, u32[]{:S(2)}) async-start(f32[4,17,16,256]{3,2,1,0:T(8,128)} %broadcast_in_dim.10), calls=%async_computation | async-start | bytes 2228224 | tf_op jit(solution)/shard_map/all_to_all | solution.py:352
  46.0 4.1 %collective-permute-start.1 = (f32[4,17,16,256]{3,2,1,0:T(8,128)S(1)}, f32[4,17,16,256]{3,2,1,0:T(8,128)S(1)}, u32[]{:S(2)}, u32[]{:S(2)}) collective-permute-start(f32[4,17,16,256]{3,2,1,0:T(8,128)S(1)} %all-to-all-done.near_ref), channel_id=1, source_target_pairs={{0,64},{64,0},{128,192},{192,128},{256,320},{320,256},{384,448},{4... | collective-permute-start | bytes 3342344 | tf_op jit(solution)/shard_map/ppermute | solution.py:423
  55.3 4.4 %all-to-all-start.1 = ((f32[4,280,256]{2,1,0:T(8,128)}), f32[4,280,256]{2,1,0:T(8,128)}, u32[]{:S(2)}, u32[]{:S(2)}) async-start(f32[4,280,256]{2,1,0:T(8,128)} %copy-done.8), calls=%async_computation.1 | async-start | bytes 2293760 | tf_op jit(solution)/shard_map/all_to_all | solution.py:352
  61.8 13.7 %all-to-all-done.1 = f32[4,280,256]{2,1,0:T(8,128)} async-done(((f32[4,280,256]{2,1,0:T(8,128)}), f32[4,280,256]{2,1,0:T(8,128)}, u32[]{:S(2)}, u32[]{:S(2)}) %all-to-all-start.1) | async-done | bytes 1146912 | tf_op jit(solution)/shard_map/all_to_all | solution.py:352
  79.0 15.8 %collective-permute-done.2 = f32[128,256]{1,0:T(8,128)S(1)} collective-permute-done((f32[128,256]{1,0:T(8,128)S(1)}, f32[128,256]{1,0:T(8,128)S(1)}, u32[]{:S(2)}, u32[]{:S(2)}) %collective-permute-start.2) | collective-permute-done | bytes 131104 | tf_op jit(solution)/shard_map/ppermute | solution.py:360
  97.5 3.5 all-to-all-start.2
  103.0 6.8 %collective-permute-done.4 = f32[96,128]{1,0:T(8,128)S(1)} collective-permute-done((f32[96,128]{1,0:T(8,128)S(1)}, f32[96,128]{1,0:T(8,128)S(1)}, u32[]{:S(2)}, u32[]{:S(2)}) %collective-permute-start.4) | collective-permute-done | bytes 49184 | tf_op jit(solution)/shard_map/ppermute | solution.py:360
  109.8 6.4 %all-to-all-done.2 = f32[4,272,256]{2,1,0:T(8,128)S(1)} async-done(((f32[4,272,256]{2,1,0:T(8,128)}), f32[4,272,256]{2,1,0:T(8,128)S(1)}, u32[]{:S(2)}, u32[]{:S(2)}) %all-to-all-start.2) | async-done | bytes 1114144 | tf_op jit(solution)/shard_map/all_to_all | solution.py:352
  121.8 4.3 %all-to-all-start.3 = ((f32[4,272,256]{2,1,0:T(8,128)}), f32[4,272,256]{2,1,0:T(8,128)}, u32[]{:S(2)}, u32[]{:S(2)}) async-start(f32[4,272,256]{2,1,0:T(8,128)} %broadcast_in_dim.13), calls=%async_computation.3 | async-start | bytes 2228224 | tf_op jit(solution)/shard_map/all_to_all | solution.py:352
  129.2 3.6 collective-permute-done.6
  140.4 4.2 %all-to-all-start.4 = ((f32[4,272,256]{2,1,0:T(8,128)}), f32[4,272,256]{2,1,0:T(8,128)}, u32[]{:S(2)}, u32[]{:S(2)}) async-start(f32[4,272,256]{2,1,0:T(8,128)} %broadcast_in_dim.12), calls=%async_computation.4 | async-start | bytes 2228224 | tf_op jit(solution)/shard_map/all_to_all | solution.py:352
  144.6 4.1 %shard_map.110.near_ref = f32[8,136,256]{2,1,0:T(8,128)S(1)} custom-call(f32[4,272,256]{2,1,0:T(8,128)} %all-to-all-done.3.field_ref, f32[8,96,128]{2,1,0:T(8,128)S(1)} %bitcast.118), custom_call_target="tpu_custom_call" | custom-call | tf_op jit(solution)/shard_map/pallas_call | solution.py:111
  149.7 8.1 %all-to-all-done.4.field_ref = f32[4,272,256]{2,1,0:T(8,128)} async-done(((f32[4,272,256]{2,1,0:T(8,128)}), f32[4,272,256]{2,1,0:T(8,128)}, u32[]{:S(2)}, u32[]{:S(2)}) %all-to-all-start.4) | async-done | bytes 1114144 | tf_op jit(solution)/shard_map/all_to_all | solution.py:352
  157.7 4.1 %shard_map.111.far_ref = f32[8,136,256]{2,1,0:T(8,128)S(1)} custom-call(f32[4,272,256]{2,1,0:T(8,128)} %all-to-all-done.4.field_ref, f32[8,96,128]{2,1,0:T(8,128)S(1)} %bitcast.119), custom_call_target="tpu_custom_call" | custom-call | tf_op jit(solution)/shard_map/pallas_call | solution.py:111
  161.9 11.1 %shard_map.112 = f32[8,136,128]{2,1,0:T(8,128)S(1)} custom-call(f32[8,96,128]{2,1,0:T(8,128)S(1)} %bitcast.120, f32[8,136,256]{2,1,0:T(8,128)S(1)} %copy-done.4, f32[8,136,256]{2,1,0:T(8,128)S(1)} %shard_map.111.far_ref), custom_call_target="tpu_custom_call" | custom-call | tf_op jit(solution)/shard_map/pallas_call | solution.py:151
  173.0 32.7 %all_to_all.60.mean_ref = f32[8,136,128]{2,1,0:T(8,128)S(1)} all-to-all(f32[8,136,128]{2,1,0:T(8,128)S(1)} %shard_map.112), channel_id=1, replica_groups=mesh['lat'=8,'lev'=8,'obs'=8] {'lev'}, dimensions={0} | all-to-all | bytes 1114112 | tf_op jit(solution)/shard_map/all_to_all | solution.py:450
  206.4 33.9 %all_to_all.61.grad_ref = f32[8,136,128]{2,1,0:T(8,128)S(1)} all-to-all(f32[8,136,128]{2,1,0:T(8,128)S(1)} %shard_map.113), channel_id=1, replica_groups=mesh['lat'=8,'lev'=8,'obs'=8] {'lev'}, dimensions={0} | all-to-all | bytes 1114112 | tf_op jit(solution)/shard_map/all_to_all | solution.py:451
  240.3 10.9 %shard_map.114 = (f32[8,136,256]{2,1,0:T(8,128)S(1)}, f32[8,136,256]{2,1,0:T(8,128)S(1)}) custom-call(f32[8,136,128]{2,1,0:T(8,128)S(1)} %all_to_all.61.grad_ref, f32[8,96,128]{2,1,0:T(8,128)S(1)} %bitcast.121), custom_call_target="tpu_custom_call" | custom-call | tf_op jit(solution)/shard_map/pallas_call | solution.py:220
  256.5 4.3 %all-to-all-start.9 = ((f32[4,272,256]{2,1,0:T(8,128)}), f32[4,272,256]{2,1,0:T(8,128)}, u32[]{:S(2)}, u32[]{:S(2)}) async-start(f32[4,272,256]{2,1,0:T(8,128)} %copy-done.2), calls=%async_computation.9 | async-start | bytes 2228224 | tf_op jit(solution)/shard_map/all_to_all | solution.py:352
  266.2 7.5 %all-to-all-done.9.parts_ref = f32[4,272,256]{2,1,0:T(8,128)} async-done(((f32[4,272,256]{2,1,0:T(8,128)}), f32[4,272,256]{2,1,0:T(8,128)}, u32[]{:S(2)}, u32[]{:S(2)}) %all-to-all-start.9) | async-done | bytes 1114144 | tf_op jit(solution)/shard_map/all_to_all | solution.py:352
  273.7 3.5 all-to-all-start.7
  279.6 9.3 %all-to-all-done.7.parts_ref = f32[4,272,256]{2,1,0:T(8,128)S(1)} async-done(((f32[4,272,256]{2,1,0:T(8,128)}), f32[4,272,256]{2,1,0:T(8,128)S(1)}, u32[]{:S(2)}, u32[]{:S(2)}) %all-to-all-start.7) | async-done | bytes 1114144 | tf_op jit(solution)/shard_map/all_to_all | solution.py:352
  288.9 4.3 %all-to-all-start.10 = ((f32[4,272,256]{2,1,0:T(8,128)}), f32[4,272,256]{2,1,0:T(8,128)}, u32[]{:S(2)}, u32[]{:S(2)}) async-start(f32[4,272,256]{2,1,0:T(8,128)} %copy-done.5), calls=%async_computation.10 | async-start | bytes 2228224 | tf_op jit(solution)/shard_map/all_to_all | solution.py:352
  294.3 9.4 %all-to-all-done.10 = f32[4,272,256]{2,1,0:T(8,128)} async-done(((f32[4,272,256]{2,1,0:T(8,128)}), f32[4,272,256]{2,1,0:T(8,128)}, u32[]{:S(2)}, u32[]{:S(2)}) %all-to-all-start.10) | async-done | bytes 1114144 | tf_op jit(solution)/shard_map/all_to_all | solution.py:352
  303.7 3.5 all-to-all-start.8
  309.4 7.9 %all-to-all-done.8 = f32[4,272,256]{2,1,0:T(8,128)S(1)} async-done(((f32[4,272,256]{2,1,0:T(8,128)}), f32[4,272,256]{2,1,0:T(8,128)S(1)}, u32[]{:S(2)}, u32[]{:S(2)}) %all-to-all-start.8) | async-done | bytes 1114144 | tf_op jit(solution)/shard_map/all_to_all | solution.py:352
  319.2 7.6 %collective-permute-start.7 = (f32[272,256]{1,0:T(8,128)S(1)}, f32[272,256]{1,0:T(8,128)S(1)}, u32[]{:S(2)}, u32[]{:S(2)}) collective-permute-start(f32[272,256]{1,0:T(8,128)S(1)} %fusion.4), channel_id=1, source_target_pairs={{0,1},{1,0},{2,3},{3,2},{4,5},{5,4},{6,7},{7,6},{8,9},{9,8},{10,11... | collective-permute-start | bytes 835592 | tf_op jit(solution)/shard_map/ppermute | solution.py:457
  328.6 6.6 %collective-permute-done.7 = f32[272,256]{1,0:T(8,128)S(1)} collective-permute-done((f32[272,256]{1,0:T(8,128)S(1)}, f32[272,256]{1,0:T(8,128)S(1)}, u32[]{:S(2)}, u32[]{:S(2)}) %collective-permute-start.7) | collective-permute-done | bytes 278560 | tf_op jit(solution)/shard_map/ppermute | solution.py:457
  336.0 14.5 %all_to_all.62.refs_0_ = f32[4,272,256]{2,1,0:T(8,128)S(1)} all-to-all(f32[4,272,256]{2,1,0:T(8,128)S(1)} %broadcast_in_dim.14), channel_id=1, replica_groups={{0,128,256,384},{64,192,320,448},{1,129,257,385},{65,193,321,449},{2,13..., dimensions={0} | all-to-all | bytes 2228224 | tf_op jit(solution)/shard_map/all_to_all | solution.py:352
  350.6 25.4 %collective-permute-start.8 = (f32[4,272,256]{2,1,0:T(8,128)S(1)}, f32[4,272,256]{2,1,0:T(8,128)}, u32[]{:S(2)}, u32[]{:S(2)}) collective-permute-start(f32[4,272,256]{2,1,0:T(8,128)S(1)} %all_to_all.62.refs_0_), channel_id=1, source_target_pairs={{0,64},{64,0},{128,192},{192,128},{256,320},{320,256},{384,448},{4... | collective-permute-start | bytes 3342344 | tf_op jit(solution)/shard_map/ppermute | solution.py:460
  378.4 3.3 shard_map.119
  (119 shorter events, 75.2 us)
Async XLA Ops:
  6.5 1.6 copy-start
  8.8 34.6 %collective-permute-start = (f32[136,256]{1,0:T(8,128)}, f32[136,256]{1,0:T(8,128)}, u32[]{:S(2)}, u32[]{:S(2)}) collective-permute-start(f32[136,256]{1,0:T(8,128)} %pad_maximum_fusion.2), channel_id=1, source_target_pairs={{0,1},{1,0},{2,3},{3,2},{4,5},{5,4},{6,7},{7,6},{8,9},{9,8},{10,11... | collective-permute-start | bytes 417800 | tf_op jit(solution)/shard_map/ppermute | solution.py:400
  27.3 4.2 %copy-start.19 = (f32[16,128]{1,0:T(8,128)S(1)}, f32[16,128]{1,0:T(8,128)}, u32[]{:S(2)}) copy-start(f32[16,128]{1,0:T(8,128)} %param.13) | copy-start | bytes 24580
  27.3 18.7 %all-to-all-start = ((f32[4,17,16,256]{3,2,1,0:T(8,128)}), f32[4,17,16,256]{3,2,1,0:T(8,128)S(1)}, u32[]{:S(2)}, u32[]{:S(2)}) async-start(f32[4,17,16,256]{3,2,1,0:T(8,128)} %broadcast_in_dim.10), calls=%async_computation | async-start | bytes 2228224 | tf_op jit(solution)/shard_map/all_to_all | solution.py:352
  31.4 6.4 %copy-start.20 = (s32[300]{0:T(512)S(1)}, s32[300]{0:T(512)}, u32[]{:S(2)}) copy-start(s32[300]{0:T(512)} %param.16) | copy-start | bytes 3604
  34.7 5.2 %copy-start.18 = (f32[300]{0:T(512)S(1)}, f32[300]{0:T(512)}, u32[]{:S(2)}) copy-start(f32[300]{0:T(512)} %param.17) | copy-start | bytes 3604
  46.0 6.4 %collective-permute-start.1 = (f32[4,17,16,256]{3,2,1,0:T(8,128)S(1)}, f32[4,17,16,256]{3,2,1,0:T(8,128)S(1)}, u32[]{:S(2)}, u32[]{:S(2)}) collective-permute-start(f32[4,17,16,256]{3,2,1,0:T(8,128)S(1)} %all-to-all-done.near_ref), channel_id=1, source_target_pairs={{0,64},{64,0},{128,192},{192,128},{256,320},{320,256},{384,448},{4... | collective-permute-start | bytes 3342344 | tf_op jit(solution)/shard_map/ppermute | solution.py:423
  55.3 4.5 %copy-start.13 = (f32[272,256]{1,0:T(8,128)S(1)}, f32[272,256]{1,0:T(8,128)}, u32[]{:S(2)}) copy-start(f32[272,256]{1,0:T(8,128)} %copy-done.12) | copy-start | bytes 835588
  55.3 20.1 %all-to-all-start.1 = ((f32[4,280,256]{2,1,0:T(8,128)}), f32[4,280,256]{2,1,0:T(8,128)}, u32[]{:S(2)}, u32[]{:S(2)}) async-start(f32[4,280,256]{2,1,0:T(8,128)} %copy-done.8), calls=%async_computation.1 | async-start | bytes 2293760 | tf_op jit(solution)/shard_map/all_to_all | solution.py:352
  59.7 35.8 %copy-start.16 = (s32[4,1024]{1,0:T(4,128)S(1)}, s32[4,1024]{1,0:T(4,128)}, u32[]{:S(2)}) copy-start(s32[4,1024]{1,0:T(4,128)} %param.20) | copy-start | bytes 49156
  59.8 35.9 %copy-start.17 = (f32[4,1024]{1,0:T(4,128)S(1)}, f32[4,1024]{1,0:T(4,128)}, u32[]{:S(2)}) copy-start(f32[4,1024]{1,0:T(4,128)} %param.19) | copy-start | bytes 49156
  59.8 73.2 %all-gather.3.cloned.1.call-start = ((), (), s32[]{:S(2)}) async-start(), calls=%async_computation.12 | async-start | bytes 2359296 | tf_op jit(solution)/shard_map/all_gather | solution.py:430
  59.8 35.7 %collective-permute-start.3 = (f32[272,256]{1,0:T(8,128)S(1)}, f32[272,256]{1,0:T(8,128)S(1)}, u32[]{:S(2)}, u32[]{:S(2)}) collective-permute-start(f32[272,256]{1,0:T(8,128)S(1)} %copy-done.13), channel_id=1, source_target_pairs={{0,1},{1,0},{2,3},{3,2},{4,5},{5,4},{6,7},{7,6},{8,9},{9,8},{10,11... | collective-permute-start | bytes 835592 | tf_op jit(solution)/shard_map/ppermute | solution.py:425
  76.4 18.5 %collective-permute-start.2 = (f32[128,256]{1,0:T(8,128)S(1)}, f32[128,256]{1,0:T(8,128)S(1)}, u32[]{:S(2)}, u32[]{:S(2)}) collective-permute-start(f32[128,256]{1,0:T(8,128)S(1)} %get-tuple-element.48), channel_id=1, source_target_pairs={{0,8},{8,0},{16,24},{24,16},{32,40},{40,32},{48,56},{56,48},{1,9},... | collective-permute-start | bytes 393224 | tf_op jit(solution)/shard_map/ppermute | solution.py:360
  97.5 18.7 %all-to-all-start.2 = ((f32[4,272,256]{2,1,0:T(8,128)}), f32[4,272,256]{2,1,0:T(8,128)S(1)}, u32[]{:S(2)}, u32[]{:S(2)}) async-start(f32[4,272,256]{2,1,0:T(8,128)} %broadcast_in_dim.11), calls=%async_computation.2 | async-start | bytes 2228224 | tf_op jit(solution)/shard_map/all_to_all | solution.py:352
  101.0 8.7 %collective-permute-start.4 = (f32[96,128]{1,0:T(8,128)S(1)}, f32[96,128]{1,0:T(8,128)S(1)}, u32[]{:S(2)}, u32[]{:S(2)}) collective-permute-start(f32[96,128]{1,0:T(8,128)S(1)} %pad_maximum_fusion.5), channel_id=1, source_target_pairs={{0,32},{8,40},{16,48},{24,56},{32,0},{40,8},{48,16},{56,24},{1,33}... | collective-permute-start | bytes 147464 | tf_op jit(solution)/shard_map/ppermute | solution.py:360
  116.2 2.6 copy-start.14
  116.2 9.9 %collective-permute-start.5 = (f32[2,96,128]{2,1,0:T(8,128)S(1)}, f32[2,96,128]{2,1,0:T(8,128)S(1)}, u32[]{:S(2)}, u32[]{:S(2)}) collective-permute-start(f32[2,96,128]{2,1,0:T(8,128)S(1)} %maximum_select_fusion.3), channel_id=1, source_target_pairs={{0,16},{8,24},{16,0},{24,8},{32,48},{40,56},{48,32},{56,40},{1,17}... | collective-permute-start | bytes 294920 | tf_op jit(solution)/shard_map/ppermute | solution.py:360
  121.8 18.6 %all-to-all-start.3 = ((f32[4,272,256]{2,1,0:T(8,128)}), f32[4,272,256]{2,1,0:T(8,128)}, u32[]{:S(2)}, u32[]{:S(2)}) async-start(f32[4,272,256]{2,1,0:T(8,128)} %broadcast_in_dim.13), calls=%async_computation.3 | async-start | bytes 2228224 | tf_op jit(solution)/shard_map/all_to_all | solution.py:352
  126.1 6.8 %collective-permute-start.6 = (f32[2,2,96,128]{3,2,1,0:T(8,128)S(1)}, f32[2,2,96,128]{3,2,1,0:T(8,128)S(1)}, u32[]{:S(2)}, u32[]{:S(2)}) collective-permute-start(f32[2,2,96,128]{3,2,1,0:T(8,128)S(1)} %maximum_select_fusion.2), channel_id=1, source_target_pairs={{0,8},{8,0},{16,24},{24,16},{32,40},{40,32},{48,56},{56,48},{1,9},... | collective-permute-start | bytes 589832 | tf_op jit(solution)/shard_map/ppermute | solution.py:360
  132.9 2.4 copy-start.15
  140.4 17.4 %all-to-all-start.4 = ((f32[4,272,256]{2,1,0:T(8,128)}), f32[4,272,256]{2,1,0:T(8,128)}, u32[]{:S(2)}, u32[]{:S(2)}) async-start(f32[4,272,256]{2,1,0:T(8,128)} %broadcast_in_dim.12), calls=%async_computation.4 | async-start | bytes 2228224 | tf_op jit(solution)/shard_map/all_to_all | solution.py:352
  157.7 4.2 %copy-start.4 = (f32[8,136,256]{2,1,0:T(8,128)S(1)}, f32[8,136,256]{2,1,0:T(8,128)}, u32[]{:S(2)}) copy-start(f32[8,136,256]{2,1,0:T(8,128)} %copy-done.3) | copy-start | bytes 3342340
  173.0 32.7 %copy-start.7 = (f32[136,1024]{1,0:T(8,128)S(1)}, f32[136,1024]{1,0:T(8,128)}, u32[]{:S(2)}) copy-start(f32[136,1024]{1,0:T(8,128)} %fusion.25.constant_ref) | copy-start | bytes 1671172
  256.5 17.2 %all-to-all-start.9 = ((f32[4,272,256]{2,1,0:T(8,128)}), f32[4,272,256]{2,1,0:T(8,128)}, u32[]{:S(2)}, u32[]{:S(2)}) async-start(f32[4,272,256]{2,1,0:T(8,128)} %copy-done.2), calls=%async_computation.9 | async-start | bytes 2228224 | tf_op jit(solution)/shard_map/all_to_all | solution.py:352
  260.7 1.2 copy-start.10
  273.7 15.2 %all-to-all-start.7 = ((f32[4,272,256]{2,1,0:T(8,128)}), f32[4,272,256]{2,1,0:T(8,128)S(1)}, u32[]{:S(2)}, u32[]{:S(2)}) async-start(f32[4,272,256]{2,1,0:T(8,128)} %copy-done.1), calls=%async_computation.7 | async-start | bytes 2228224 | tf_op jit(solution)/shard_map/all_to_all | solution.py:352
  288.9 14.8 %all-to-all-start.10 = ((f32[4,272,256]{2,1,0:T(8,128)}), f32[4,272,256]{2,1,0:T(8,128)}, u32[]{:S(2)}, u32[]{:S(2)}) async-start(f32[4,272,256]{2,1,0:T(8,128)} %copy-done.5), calls=%async_computation.10 | async-start | bytes 2228224 | tf_op jit(solution)/shard_map/all_to_all | solution.py:352
  303.7 13.6 %all-to-all-start.8 = ((f32[4,272,256]{2,1,0:T(8,128)}), f32[4,272,256]{2,1,0:T(8,128)S(1)}, u32[]{:S(2)}, u32[]{:S(2)}) async-start(f32[4,272,256]{2,1,0:T(8,128)} %copy-done.6), calls=%async_computation.8 | async-start | bytes 2228224 | tf_op jit(solution)/shard_map/all_to_all | solution.py:352
  319.2 16.1 %collective-permute-start.7 = (f32[272,256]{1,0:T(8,128)S(1)}, f32[272,256]{1,0:T(8,128)S(1)}, u32[]{:S(2)}, u32[]{:S(2)}) collective-permute-start(f32[272,256]{1,0:T(8,128)S(1)} %fusion.4), channel_id=1, source_target_pairs={{0,1},{1,0},{2,3},{3,2},{4,5},{5,4},{6,7},{7,6},{8,9},{9,8},{10,11... | collective-permute-start | bytes 835592 | tf_op jit(solution)/shard_map/ppermute | solution.py:457
  336.0 42.4 %copy-start.11 = (f32[17,16,256]{2,1,0:T(8,128)S(1)}, f32[17,16,256]{2,1,0:T(8,128)}, u32[]{:S(2)}) copy-start(f32[17,16,256]{2,1,0:T(8,128)} %chi_ref.1) | copy-start | bytes 835588
  350.6 27.9 %collective-permute-start.8 = (f32[4,272,256]{2,1,0:T(8,128)S(1)}, f32[4,272,256]{2,1,0:T(8,128)}, u32[]{:S(2)}, u32[]{:S(2)}) collective-permute-start(f32[4,272,256]{2,1,0:T(8,128)S(1)} %all_to_all.62.refs_0_), channel_id=1, source_target_pairs={{0,64},{64,0},{128,192},{192,128},{256,320},{320,256},{384,448},{4... | collective-permute-start | bytes 3342344 | tf_op jit(solution)/shard_map/ppermute | solution.py:460
  (8 other events, 7.8 us)
Sparse Core Ops, SparseCore 0:
  95.7 27.7 all-gather.2

commit v6 on v5

--- a/solution.py
+++ b/solution.py
@@ -46,8 +46,9 @@
 
 
 def one_hot(index, rows):
-    place = lax.broadcasted_iota(jnp.int32, (rows, index.shape[1]), 0)
-    return jnp.where(place == index, 1.0, 0.0).astype(BF16)
+    place = lax.broadcasted_iota(jnp.int32, (rows, index.shape[1]), 0).astype(BF16)
+    index = jnp.broadcast_to(index.astype(F32), place.shape).astype(BF16)
+    return jnp.where(place == index, jnp.ones_like(place), jnp.zeros_like(place))
 
 
 def dot(a, b):
@@ -121,41 +122,49 @@
     )(field, about)
 
 
-def mean_kernel(about_ref, near_ref, far_ref, mean_ref):
-    slots = near_ref, far_ref
-    mains = jnp.concatenate([s[0, :GROUP_MAIN, :] for s in slots], axis=0)
-    lasts = jnp.concatenate([s[0, GROUP_MAIN : GROUP_MAIN + 4 * HALVES, :] for s in slots], axis=0)
-    values = split_rows(jnp.concatenate([mains, lasts], axis=0))
-    total = 16 * MAIN + 16
+def mean_kernel(which, about_ref, slots_ref, *refs):
+    before_ref, mean_ref = (None,) * (2 - len(refs)) + refs
+    values = split_rows(slots_ref[0])
     for start in range(0, OBS, BLOCK):
         main = jnp.zeros((MAIN, BLOCK), F32)
-        last = jnp.zeros((16, BLOCK), F32)
+        last = jnp.zeros((8, BLOCK), F32)
         for member in range(FOOT):
             low, high, weight = feet_of(about_ref, member, start)
             both = dot(values, one_hot(low, BLOCK))
-            picked = both[:total] + both[total:]
-            masked = jnp.where(lax.broadcasted_iota(jnp.int32, (16, BLOCK), 0) == high, weight, 0.0)
-            for part in range(16):
+            picked = both[:GROUP] + both[GROUP:]
+            place = lax.broadcasted_iota(jnp.int32, (8, BLOCK), 0) + 8 * which
+            masked = jnp.where(place == high, weight, 0.0)
+            for part in range(8):
                 main = main + picked[part * MAIN : (part + 1) * MAIN] * masked[part : part + 1]
-            last = last + picked[16 * MAIN :] * masked
+            last = last + picked[GROUP_MAIN:] * masked
         last = jnp.sum(last, axis=0, keepdims=True)
         for piece in range(BLOCK // LANES):
             lanes = slice(piece * LANES, (piece + 1) * LANES)
             at = start // LANES + piece
-            mean_ref[0, at * MAIN : (at + 1) * MAIN, :] = main[:, lanes]
-            mean_ref[0, 8 * MAIN + at : 8 * MAIN + at + 1, :] = last[:, lanes]
-
-
-def means(near, far, about):
-    slots = pl.BlockSpec((1, GROUP, BLOCK), lambda v: (v, 0, 0))
-    return pl.pallas_call(
-        mean_kernel,
+            rows = slice(at * MAIN, (at + 1) * MAIN)
+            row = slice(8 * MAIN + at, 8 * MAIN + at + 1)
+            if before_ref is None:
+                mean_ref[0, rows, :] = main[:, lanes]
+                mean_ref[0, row, :] = last[:, lanes]
+            else:
+                mean_ref[0, rows, :] = before_ref[0, rows, :] + main[:, lanes]
+                mean_ref[0, row, :] = before_ref[0, row, :] + last[:, lanes]
+
+
+def means(slots, about, which, *before):
+    column = pl.BlockSpec((1, COLUMN, LANES), lambda v: (v, 0, 0))
+    return pl.pallas_call(
+        functools.partial(mean_kernel, which),
         grid=(VIEWERS,),
-        in_specs=[pl.BlockSpec((1,) + ABOUT[1:], lambda v: (v, 0, 0)), slots, slots],
-        out_specs=pl.BlockSpec((1, COLUMN, LANES), lambda v: (v, 0, 0)),
+        in_specs=[
+            pl.BlockSpec((1,) + ABOUT[1:], lambda v: (v, 0, 0)),
+            pl.BlockSpec((1, GROUP, BLOCK), lambda v: (v, 0, 0)),
+        ]
+        + [column] * len(before),
+        out_specs=column,
         out_shape=jax.ShapeDtypeStruct((VIEWERS, COLUMN, LANES), F32),
         compiler_params=params(),
-    )(about, near, far)
+    )(about, slots, *before)
 
 
 def pull_kernel(mean_ref, hessian_ref, constant_ref, pulled_ref):
@@ -187,9 +196,8 @@
     )(mean, hessian, constant)
 
 
-def spread_kernel(grad_ref, about_ref, near_ref, far_ref):
-    count = 16 * MAIN + 16
-    total = jnp.zeros((2 * count, BLOCK), F32)
+def spread_kernel(which, grad_ref, about_ref, slots_ref):
+    total = jnp.zeros((2 * GROUP, BLOCK), F32)
     for start in range(0, OBS, BLOCK):
         main = []
         last = []
@@ -200,32 +208,29 @@
         last = jnp.concatenate(last, axis=1)
         for member in range(FOOT):
             low, high, weight = feet_of(about_ref, member, start)
-            hit = jnp.where(lax.broadcasted_iota(jnp.int32, (16, BLOCK), 0) == high, 1.0, 0.0)
+            place = lax.broadcasted_iota(jnp.int32, (8, BLOCK), 0) + 8 * which
+            hit = jnp.where(place == high, 1.0, 0.0)
             main_high, main_low = split(main * weight)
-            last_high, last_low = split(last * weight * hit)
-            hits = [jnp.broadcast_to(hit[part : part + 1], (MAIN, BLOCK)).astype(BF16) for part in range(16)]
-            rows = jnp.concatenate(
-                [main_high * h for h in hits] + [last_high] + [main_low * h for h in hits] + [last_low], axis=0
-            )
+            last_rows = last * weight * hit
+            last_high = last_rows.astype(BF16).astype(F32)
+            lasts = jnp.concatenate([last_high, last_rows - last_high], axis=0).astype(BF16)
+            hits = [jnp.broadcast_to(hit[part : part + 1], (MAIN, BLOCK)).astype(BF16) for part in range(8)]
+            rows = jnp.concatenate([main_high * h for h in hits] + [main_low * h for h in hits] + [lasts], axis=0)
             total = total + dot_nt(rows, one_hot(low, BLOCK))
-    total = total[:count] + total[count:]
-    for group, slots_ref in enumerate((near_ref, far_ref)):
-        slots_ref[0, :GROUP_MAIN, :] = total[group * GROUP_MAIN : (group + 1) * GROUP_MAIN]
-        at = 16 * MAIN + group * 4 * HALVES
-        slots_ref[0, GROUP_MAIN : GROUP_MAIN + 4 * HALVES, :] = total[at : at + 4 * HALVES]
-
-
-def spread(grad, about):
-    slots = pl.BlockSpec((1, GROUP, BLOCK), lambda v: (v, 0, 0))
-    return pl.pallas_call(
-        spread_kernel,
+    slots_ref[0, :GROUP_MAIN, :] = total[:GROUP_MAIN] + total[GROUP_MAIN : 2 * GROUP_MAIN]
+    slots_ref[0, GROUP_MAIN:, :] = total[2 * GROUP_MAIN : 2 * GROUP_MAIN + 8] + total[2 * GROUP_MAIN + 8 :]
+
+
+def spread(grad, about, which):
+    return pl.pallas_call(
+        functools.partial(spread_kernel, which),
         grid=(VIEWERS,),
         in_specs=[
             pl.BlockSpec((1, COLUMN, LANES), lambda v: (v, 0, 0)),
             pl.BlockSpec((1,) + ABOUT[1:], lambda v: (v, 0, 0)),
         ],
-        out_specs=[slots] * 2,
-        out_shape=[jax.ShapeDtypeStruct((VIEWERS, GROUP, BLOCK), F32)] * 2,
+        out_specs=pl.BlockSpec((1, GROUP, BLOCK), lambda v: (v, 0, 0)),
+        out_shape=jax.ShapeDtypeStruct((VIEWERS, GROUP, BLOCK), F32),
         compiler_params=params(),
     )(grad, about)
 
@@ -444,15 +449,14 @@
     about = both_of(about, 1, 2).reshape(ABOUT)
     copies = jnp.broadcast_to(tile_far[None], (4,) + tile_far.shape)
     about, copies = lax.optimization_barrier((about, copies))
-    near = pick(near_tiles, about, 0)
-    far = pick(exchange(copies, "obs"), about, 1)
-
-    mean = lax.all_to_all(means(near, far, about), "lev", 0, 0)
+    mean = means(pick(near_tiles, about, 0), about, 0)
+    mean = means(pick(exchange(copies, "obs"), about, 1), about, 1, mean)
+
+    mean = lax.all_to_all(mean, "lev", 0, 0)
     pulled = lax.all_to_all(pull(mean, hessian, constant), "lev", 0, 0)
-    near, far = spread(pulled, about)
-
-    far_tiles = exchange(add(exchange(put(far, about, 1), "obs")), "obs")
-    near_tiles = exchange(add(exchange(put(near, about, 0), "obs")), "obs")
+
+    far_tiles = exchange(add(exchange(put(spread(pulled, about, 1), about, 1), "obs")), "obs")
+    near_tiles = exchange(add(exchange(put(spread(pulled, about, 0), about, 0), "obs")), "obs")
     far = product(far_tiles, other_far) + product(near_tiles, other_near)
     far = lax.ppermute(far, "obs", PARTNER)
     field = product(far_tiles, lon_far) + product(near_tiles, lon_near) + far

time: 391 us -> 380 us (0.972)
  waiting for transfers between devices: 103 us -> 92.4 us
    all_to_all x9, waiting for transfers between devices: 66 us -> 55.7 us  [exchange(): return lax.all_to_all(blocks, axis, 0, 0, axis_index_groups=ALONG)]
    pallas_call x2 -> x4, Pallas kernels: 22.1 us -> 25.5 us  [the longest x2 12.7 us: means(): pl.pallas_call(functools.partial(mean_kernel, which), grid=(VIEWERS,), in...]
    unnamed x46 -> x38, local copies, waits for them, and re-layouts: 10.8 us -> 7.58 us
  transfers between devices with their start and end apart: 19 -> 19, of which waited for: 15 -> 15; matrix products, arithmetic and copies ran while one was open for 8% -> 9% of each run, Pallas kernels for 2% -> 6%
where the time goes in v6:
time: 380 us; the launch traced here: 378 us
  starting transfers between devices  101 us (27%)
  waiting for transfers between devices  92.4 us (24%)
  blocking collectives  81.2 us (21%)
  Pallas kernels  45.8 us (12%)
  local copies, waits for them, and re-layouts  20.2 us (5%)
  matrix products  19 us (5%)
  between operations  14.1 us (4%)
  other arithmetic  4.03 us (1%)
    all_to_all x9, waiting for transfers between devices, exchange(): return lax.all_to_all(blocks, axis, 0, 0, axis_index_groups=ALONG)  55.7 us
    all_to_all x9, starting transfers between devices, exchange(): return lax.all_to_all(blocks, axis, 0, 0, axis_index_groups=ALONG)  36.2 us
    all_to_all x1, blocking collectives, shards(): pulled = lax.all_to_all(pull(mean, hessian, constant), 'lev', 0, 0)  33.9 us
    all_to_all x1, blocking collectives, shards(): mean = lax.all_to_all(mean, 'lev', 0, 0)  32.7 us
    ppermute x2, starting transfers between devices, shards(): band_far = lax.ppermute(band_near, 'lat', PARTNER)  29.5 us
    ppermute x4, waiting for transfers between devices, both_of(): other = lax.ppermute(x, 'lev', [(m, m ^ step) for m in range(8)])  26.1 us
    ppermute x1, starting transfers between devices, shards(): piece = lax.ppermute(piece, 'obs', PARTNER)  16.3 us
    all_to_all x1, blocking collectives, exchange(): return lax.all_to_all(blocks, axis, 0, 0, axis_index_groups=ALONG)  14.5 us
  transfers between devices with their start and end apart: 19, of which 15 were waited for; matrix products, arithmetic and copies ran while one was open for 9% of the time, Pallas kernels for 6%

profile of v6, /device:TPU:1, one launch (start us, length us, event | category | flops | bytes accessed | tf_op | source)
XLA Modules:
  0.0 377.8 jit_solution(8336848034329281568)
XLA Ops:
  8.8 16.3 %collective-permute-start = (f32[136,256]{1,0:T(8,128)}, f32[136,256]{1,0:T(8,128)}, u32[]{:S(2)}, u32[]{:S(2)}) collective-permute-start(f32[136,256]{1,0:T(8,128)} %pad_maximum_fusion.2), channel_id=1, source_target_pairs={{0,1},{1,0},{2,3},{3,2},{4,5},{5,4},{6,7},{7,6},{8,9},{9,8},{10,11... | collective-permute-start | bytes 417800 | tf_op jit(solution)/shard_map/ppermute | solution.py:405
  27.2 4.1 %all-to-all-start = ((f32[4,17,16,256]{3,2,1,0:T(8,128)}), f32[4,17,16,256]{3,2,1,0:T(8,128)S(1)}, u32[]{:S(2)}, u32[]{:S(2)}) async-start(f32[4,17,16,256]{3,2,1,0:T(8,128)} %broadcast_in_dim.10), calls=%async_computation | async-start | bytes 2228224 | tf_op jit(solution)/shard_map/all_to_all | solution.py:357
  46.0 4.1 %collective-permute-start.1 = (f32[4,17,16,256]{3,2,1,0:T(8,128)S(1)}, f32[4,17,16,256]{3,2,1,0:T(8,128)S(1)}, u32[]{:S(2)}, u32[]{:S(2)}) collective-permute-start(f32[4,17,16,256]{3,2,1,0:T(8,128)S(1)} %all-to-all-done.near_ref), channel_id=1, source_target_pairs={{0,64},{64,0},{128,192},{192,128},{256,320},{320,256},{384,448},{4... | collective-permute-start | bytes 3342344 | tf_op jit(solution)/shard_map/ppermute | solution.py:428
  55.3 4.4 %all-to-all-start.1 = ((f32[4,280,256]{2,1,0:T(8,128)}), f32[4,280,256]{2,1,0:T(8,128)}, u32[]{:S(2)}, u32[]{:S(2)}) async-start(f32[4,280,256]{2,1,0:T(8,128)} %copy-done.6), calls=%async_computation.1 | async-start | bytes 2293760 | tf_op jit(solution)/shard_map/all_to_all | solution.py:357
  61.7 13.7 %all-to-all-done.1 = f32[4,280,256]{2,1,0:T(8,128)} async-done(((f32[4,280,256]{2,1,0:T(8,128)}), f32[4,280,256]{2,1,0:T(8,128)}, u32[]{:S(2)}, u32[]{:S(2)}) %all-to-all-start.1) | async-done | bytes 1146912 | tf_op jit(solution)/shard_map/all_to_all | solution.py:357
  79.0 15.8 %collective-permute-done.2 = f32[128,256]{1,0:T(8,128)S(1)} collective-permute-done((f32[128,256]{1,0:T(8,128)S(1)}, f32[128,256]{1,0:T(8,128)S(1)}, u32[]{:S(2)}, u32[]{:S(2)}) %collective-permute-start.2) | collective-permute-done | bytes 131104 | tf_op jit(solution)/shard_map/ppermute | solution.py:365
  97.5 3.5 all-to-all-start.2
  103.0 6.8 %collective-permute-done.4 = f32[96,128]{1,0:T(8,128)S(1)} collective-permute-done((f32[96,128]{1,0:T(8,128)S(1)}, f32[96,128]{1,0:T(8,128)S(1)}, u32[]{:S(2)}, u32[]{:S(2)}) %collective-permute-start.4) | collective-permute-done | bytes 49184 | tf_op jit(solution)/shard_map/ppermute | solution.py:365
  109.7 6.4 %all-to-all-done.2 = f32[4,272,256]{2,1,0:T(8,128)S(1)} async-done(((f32[4,272,256]{2,1,0:T(8,128)}), f32[4,272,256]{2,1,0:T(8,128)S(1)}, u32[]{:S(2)}, u32[]{:S(2)}) %all-to-all-start.2) | async-done | bytes 1114144 | tf_op jit(solution)/shard_map/all_to_all | solution.py:357
  121.7 4.2 %all-to-all-start.4 = ((f32[4,272,256]{2,1,0:T(8,128)}), f32[4,272,256]{2,1,0:T(8,128)}, u32[]{:S(2)}, u32[]{:S(2)}) async-start(f32[4,272,256]{2,1,0:T(8,128)} %broadcast_in_dim.13), calls=%async_computation.4 | async-start | bytes 2228224 | tf_op jit(solution)/shard_map/all_to_all | solution.py:357
  129.2 3.6 collective-permute-done.6
  140.3 4.3 %all-to-all-start.3 = ((f32[4,272,256]{2,1,0:T(8,128)}), f32[4,272,256]{2,1,0:T(8,128)}, u32[]{:S(2)}, u32[]{:S(2)}) async-start(f32[4,272,256]{2,1,0:T(8,128)} %broadcast_in_dim.12), calls=%async_computation.3 | async-start | bytes 2228224 | tf_op jit(solution)/shard_map/all_to_all | solution.py:357
  144.6 3.8 shard_map.111.slots_ref
  148.3 6.4 %shard_map.112.refs_0_ = f32[8,136,128]{2,1,0:T(8,128)S(1)} custom-call(f32[8,96,128]{2,1,0:T(8,128)S(1)} %bitcast.119, f32[8,136,256]{2,1,0:T(8,128)S(1)} %shard_map.111.slots_ref), custom_call_target="tpu_custom_call" | custom-call | tf_op jit(solution)/shard_map/pallas_call | solution.py:156
  157.7 3.7 shard_map.110.slots_ref
  161.4 6.4 %shard_map.113 = f32[8,136,128]{2,1,0:T(8,128)S(1)} custom-call(f32[8,96,128]{2,1,0:T(8,128)S(1)} %bitcast.121, f32[8,136,256]{2,1,0:T(8,128)S(1)} %shard_map.110.slots_ref, f32[8,136,128]{2,1,0:T(8,128)S(1)} %shard_map.112.refs_0_), custom_call_target="tpu_custom_call" | custom-call | tf_op jit(solution)/shard_map/pallas_call | solution.py:156
  167.8 32.7 %all_to_all.60.mean_ref = f32[8,136,128]{2,1,0:T(8,128)S(1)} all-to-all(f32[8,136,128]{2,1,0:T(8,128)S(1)} %shard_map.113), channel_id=1, replica_groups=mesh['lat'=8,'lev'=8,'obs'=8] {'lev'}, dimensions={0} | all-to-all | bytes 1114112 | tf_op jit(solution)/shard_map/all_to_all | solution.py:455
  201.2 33.9 %all_to_all.61.grad_ref = f32[8,136,128]{2,1,0:T(8,128)S(1)} all-to-all(f32[8,136,128]{2,1,0:T(8,128)S(1)} %shard_map.114), channel_id=1, replica_groups=mesh['lat'=8,'lev'=8,'obs'=8] {'lev'}, dimensions={0} | all-to-all | bytes 1114112 | tf_op jit(solution)/shard_map/all_to_all | solution.py:456
  235.1 6.3 %shard_map.118.slots_ref = f32[8,136,256]{2,1,0:T(8,128)S(1)} custom-call(f32[8,136,128]{2,1,0:T(8,128)S(1)} %all_to_all.61.grad_ref, f32[8,96,128]{2,1,0:T(8,128)S(1)} %bitcast.122), custom_call_target="tpu_custom_call" | custom-call | tf_op jit(solution)/shard_map/pallas_call | solution.py:225
  245.6 4.2 %all-to-all-start.9 = ((f32[4,272,256]{2,1,0:T(8,128)}), f32[4,272,256]{2,1,0:T(8,128)}, u32[]{:S(2)}, u32[]{:S(2)}) async-start(f32[4,272,256]{2,1,0:T(8,128)} %copy-done.2), calls=%async_computation.9 | async-start | bytes 2228224 | tf_op jit(solution)/shard_map/all_to_all | solution.py:357
  249.9 6.4 %shard_map.115.slots_ref = f32[8,136,256]{2,1,0:T(8,128)S(1)} custom-call(f32[8,136,128]{2,1,0:T(8,128)S(1)} %all_to_all.61.grad_ref, f32[8,96,128]{2,1,0:T(8,128)S(1)} %bitcast.124), custom_call_target="tpu_custom_call" | custom-call | tf_op jit(solution)/shard_map/pallas_call | solution.py:225
  262.9 3.5 all-to-all-start.7
  268.7 9.3 %all-to-all-done.7.parts_ref = f32[4,272,256]{2,1,0:T(8,128)S(1)} async-done(((f32[4,272,256]{2,1,0:T(8,128)}), f32[4,272,256]{2,1,0:T(8,128)S(1)}, u32[]{:S(2)}, u32[]{:S(2)}) %all-to-all-start.7) | async-done | bytes 1114144 | tf_op jit(solution)/shard_map/all_to_all | solution.py:357
  278.0 4.3 %all-to-all-start.10 = ((f32[4,272,256]{2,1,0:T(8,128)}), f32[4,272,256]{2,1,0:T(8,128)}, u32[]{:S(2)}, u32[]{:S(2)}) async-start(f32[4,272,256]{2,1,0:T(8,128)} %copy-done.3), calls=%async_computation.10 | async-start | bytes 2228224 | tf_op jit(solution)/shard_map/all_to_all | solution.py:357
  283.4 9.4 %all-to-all-done.10 = f32[4,272,256]{2,1,0:T(8,128)} async-done(((f32[4,272,256]{2,1,0:T(8,128)}), f32[4,272,256]{2,1,0:T(8,128)}, u32[]{:S(2)}, u32[]{:S(2)}) %all-to-all-start.10) | async-done | bytes 1114144 | tf_op jit(solution)/shard_map/all_to_all | solution.py:357
  292.8 3.5 all-to-all-start.8
  298.6 7.9 %all-to-all-done.8 = f32[4,272,256]{2,1,0:T(8,128)S(1)} async-done(((f32[4,272,256]{2,1,0:T(8,128)}), f32[4,272,256]{2,1,0:T(8,128)S(1)}, u32[]{:S(2)}, u32[]{:S(2)}) %all-to-all-start.8) | async-done | bytes 1114144 | tf_op jit(solution)/shard_map/all_to_all | solution.py:357
  308.3 7.7 %collective-permute-start.7 = (f32[272,256]{1,0:T(8,128)S(1)}, f32[272,256]{1,0:T(8,128)S(1)}, u32[]{:S(2)}, u32[]{:S(2)}) collective-permute-start(f32[272,256]{1,0:T(8,128)S(1)} %fusion.4), channel_id=1, source_target_pairs={{0,1},{1,0},{2,3},{3,2},{4,5},{5,4},{6,7},{7,6},{8,9},{9,8},{10,11... | collective-permute-start | bytes 835592 | tf_op jit(solution)/shard_map/ppermute | solution.py:461
  317.9 6.5 %collective-permute-done.7 = f32[272,256]{1,0:T(8,128)S(1)} collective-permute-done((f32[272,256]{1,0:T(8,128)S(1)}, f32[272,256]{1,0:T(8,128)S(1)}, u32[]{:S(2)}, u32[]{:S(2)}) %collective-permute-start.7) | collective-permute-done | bytes 278560 | tf_op jit(solution)/shard_map/ppermute | solution.py:461
  325.1 14.5 %all_to_all.62.refs_0_ = f32[4,272,256]{2,1,0:T(8,128)S(1)} all-to-all(f32[4,272,256]{2,1,0:T(8,128)S(1)} %broadcast_in_dim.14), channel_id=1, replica_groups={{0,128,256,384},{64,192,320,448},{1,129,257,385},{65,193,321,449},{2,13..., dimensions={0} | all-to-all | bytes 2228224 | tf_op jit(solution)/shard_map/all_to_all | solution.py:357
  339.7 25.5 %collective-permute-start.8 = (f32[4,272,256]{2,1,0:T(8,128)S(1)}, f32[4,272,256]{2,1,0:T(8,128)}, u32[]{:S(2)}, u32[]{:S(2)}) collective-permute-start(f32[4,272,256]{2,1,0:T(8,128)S(1)} %all_to_all.62.refs_0_), channel_id=1, source_target_pairs={{0,64},{64,0},{128,192},{192,128},{256,320},{320,256},{384,448},{4... | collective-permute-start | bytes 3342344 | tf_op jit(solution)/shard_map/ppermute | solution.py:464
  367.6 3.3 shard_map.121
  (113 shorter events, 77.3 us)
Async XLA Ops:
  6.5 1.6 copy-start
  8.8 34.6 %collective-permute-start = (f32[136,256]{1,0:T(8,128)}, f32[136,256]{1,0:T(8,128)}, u32[]{:S(2)}, u32[]{:S(2)}) collective-permute-start(f32[136,256]{1,0:T(8,128)} %pad_maximum_fusion.2), channel_id=1, source_target_pairs={{0,1},{1,0},{2,3},{3,2},{4,5},{5,4},{6,7},{7,6},{8,9},{9,8},{10,11... | collective-permute-start | bytes 417800 | tf_op jit(solution)/shard_map/ppermute | solution.py:405
  27.2 4.2 %copy-start.15 = (f32[16,128]{1,0:T(8,128)S(1)}, f32[16,128]{1,0:T(8,128)}, u32[]{:S(2)}) copy-start(f32[16,128]{1,0:T(8,128)} %param.13) | copy-start | bytes 24580
  27.2 18.7 %all-to-all-start = ((f32[4,17,16,256]{3,2,1,0:T(8,128)}), f32[4,17,16,256]{3,2,1,0:T(8,128)S(1)}, u32[]{:S(2)}, u32[]{:S(2)}) async-start(f32[4,17,16,256]{3,2,1,0:T(8,128)} %broadcast_in_dim.10), calls=%async_computation | async-start | bytes 2228224 | tf_op jit(solution)/shard_map/all_to_all | solution.py:357
  31.4 6.4 %copy-start.16 = (s32[300]{0:T(512)S(1)}, s32[300]{0:T(512)}, u32[]{:S(2)}) copy-start(s32[300]{0:T(512)} %param.16) | copy-start | bytes 3604
  34.6 5.2 %copy-start.14 = (f32[300]{0:T(512)S(1)}, f32[300]{0:T(512)}, u32[]{:S(2)}) copy-start(f32[300]{0:T(512)} %param.17) | copy-start | bytes 3604
  46.0 6.4 %collective-permute-start.1 = (f32[4,17,16,256]{3,2,1,0:T(8,128)S(1)}, f32[4,17,16,256]{3,2,1,0:T(8,128)S(1)}, u32[]{:S(2)}, u32[]{:S(2)}) collective-permute-start(f32[4,17,16,256]{3,2,1,0:T(8,128)S(1)} %all-to-all-done.near_ref), channel_id=1, source_target_pairs={{0,64},{64,0},{128,192},{192,128},{256,320},{320,256},{384,448},{4... | collective-permute-start | bytes 3342344 | tf_op jit(solution)/shard_map/ppermute | solution.py:428
  53.5 1.1 copy-start.6
  55.3 4.5 %copy-start.9 = (f32[272,256]{1,0:T(8,128)S(1)}, f32[272,256]{1,0:T(8,128)}, u32[]{:S(2)}) copy-start(f32[272,256]{1,0:T(8,128)} %copy-done.8) | copy-start | bytes 835588
  55.3 20.1 %all-to-all-start.1 = ((f32[4,280,256]{2,1,0:T(8,128)}), f32[4,280,256]{2,1,0:T(8,128)}, u32[]{:S(2)}, u32[]{:S(2)}) async-start(f32[4,280,256]{2,1,0:T(8,128)} %copy-done.6), calls=%async_computation.1 | async-start | bytes 2293760 | tf_op jit(solution)/shard_map/all_to_all | solution.py:357
  59.7 35.8 %copy-start.12 = (s32[4,1024]{1,0:T(4,128)S(1)}, s32[4,1024]{1,0:T(4,128)}, u32[]{:S(2)}) copy-start(s32[4,1024]{1,0:T(4,128)} %param.20) | copy-start | bytes 49156
  59.7 35.9 %copy-start.13 = (f32[4,1024]{1,0:T(4,128)S(1)}, f32[4,1024]{1,0:T(4,128)}, u32[]{:S(2)}) copy-start(f32[4,1024]{1,0:T(4,128)} %param.19) | copy-start | bytes 49156
  59.7 73.1 %all-gather.3.cloned.1.call-start = ((), (), s32[]{:S(2)}) async-start(), calls=%async_computation.12 | async-start | bytes 2359296 | tf_op jit(solution)/shard_map/all_gather | solution.py:435
  59.8 35.7 %collective-permute-start.3 = (f32[272,256]{1,0:T(8,128)S(1)}, f32[272,256]{1,0:T(8,128)S(1)}, u32[]{:S(2)}, u32[]{:S(2)}) collective-permute-start(f32[272,256]{1,0:T(8,128)S(1)} %copy-done.9), channel_id=1, source_target_pairs={{0,1},{1,0},{2,3},{3,2},{4,5},{5,4},{6,7},{7,6},{8,9},{9,8},{10,11... | collective-permute-start | bytes 835592 | tf_op jit(solution)/shard_map/ppermute | solution.py:430
  76.4 18.5 %collective-permute-start.2 = (f32[128,256]{1,0:T(8,128)S(1)}, f32[128,256]{1,0:T(8,128)S(1)}, u32[]{:S(2)}, u32[]{:S(2)}) collective-permute-start(f32[128,256]{1,0:T(8,128)S(1)} %get-tuple-element.44), channel_id=1, source_target_pairs={{0,8},{8,0},{16,24},{24,16},{32,40},{40,32},{48,56},{56,48},{1,9},... | collective-permute-start | bytes 393224 | tf_op jit(solution)/shard_map/ppermute | solution.py:365
  97.5 18.7 %all-to-all-start.2 = ((f32[4,272,256]{2,1,0:T(8,128)}), f32[4,272,256]{2,1,0:T(8,128)S(1)}, u32[]{:S(2)}, u32[]{:S(2)}) async-start(f32[4,272,256]{2,1,0:T(8,128)} %broadcast_in_dim.11), calls=%async_computation.2 | async-start | bytes 2228224 | tf_op jit(solution)/shard_map/all_to_all | solution.py:357
  101.0 8.7 %collective-permute-start.4 = (f32[96,128]{1,0:T(8,128)S(1)}, f32[96,128]{1,0:T(8,128)S(1)}, u32[]{:S(2)}, u32[]{:S(2)}) collective-permute-start(f32[96,128]{1,0:T(8,128)S(1)} %pad_maximum_fusion.5), channel_id=1, source_target_pairs={{0,32},{8,40},{16,48},{24,56},{32,0},{40,8},{48,16},{56,24},{1,33}... | collective-permute-start | bytes 147464 | tf_op jit(solution)/shard_map/ppermute | solution.py:365
  116.1 2.6 copy-start.10
  116.1 9.8 %collective-permute-start.5 = (f32[2,96,128]{2,1,0:T(8,128)S(1)}, f32[2,96,128]{2,1,0:T(8,128)S(1)}, u32[]{:S(2)}, u32[]{:S(2)}) collective-permute-start(f32[2,96,128]{2,1,0:T(8,128)S(1)} %maximum_select_fusion.3), channel_id=1, source_target_pairs={{0,16},{8,24},{16,0},{24,8},{32,48},{40,56},{48,32},{56,40},{1,17}... | collective-permute-start | bytes 294920 | tf_op jit(solution)/shard_map/ppermute | solution.py:365
  121.7 18.6 %all-to-all-start.4 = ((f32[4,272,256]{2,1,0:T(8,128)}), f32[4,272,256]{2,1,0:T(8,128)}, u32[]{:S(2)}, u32[]{:S(2)}) async-start(f32[4,272,256]{2,1,0:T(8,128)} %broadcast_in_dim.13), calls=%async_computation.4 | async-start | bytes 2228224 | tf_op jit(solution)/shard_map/all_to_all | solution.py:357
  126.0 6.8 %collective-permute-start.6 = (f32[2,2,96,128]{3,2,1,0:T(8,128)S(1)}, f32[2,2,96,128]{3,2,1,0:T(8,128)S(1)}, u32[]{:S(2)}, u32[]{:S(2)}) collective-permute-start(f32[2,2,96,128]{3,2,1,0:T(8,128)S(1)} %maximum_select_fusion.2), channel_id=1, source_target_pairs={{0,8},{8,0},{16,24},{24,16},{32,40},{40,32},{48,56},{56,48},{1,9},... | collective-permute-start | bytes 589832 | tf_op jit(solution)/shard_map/ppermute | solution.py:365
  132.9 2.4 copy-start.11
  140.3 17.4 %all-to-all-start.3 = ((f32[4,272,256]{2,1,0:T(8,128)}), f32[4,272,256]{2,1,0:T(8,128)}, u32[]{:S(2)}, u32[]{:S(2)}) async-start(f32[4,272,256]{2,1,0:T(8,128)} %broadcast_in_dim.12), calls=%async_computation.3 | async-start | bytes 2228224 | tf_op jit(solution)/shard_map/all_to_all | solution.py:357
  167.8 32.7 %copy-start.5 = (f32[136,1024]{1,0:T(8,128)S(1)}, f32[136,1024]{1,0:T(8,128)}, u32[]{:S(2)}) copy-start(f32[136,1024]{1,0:T(8,128)} %fusion.25.constant_ref) | copy-start | bytes 1671172
  244.6 1.0 copy-start.2
  245.6 17.2 %all-to-all-start.9 = ((f32[4,272,256]{2,1,0:T(8,128)}), f32[4,272,256]{2,1,0:T(8,128)}, u32[]{:S(2)}, u32[]{:S(2)}) async-start(f32[4,272,256]{2,1,0:T(8,128)} %copy-done.2), calls=%async_computation.9 | async-start | bytes 2228224 | tf_op jit(solution)/shard_map/all_to_all | solution.py:357
  262.9 15.2 %all-to-all-start.7 = ((f32[4,272,256]{2,1,0:T(8,128)}), f32[4,272,256]{2,1,0:T(8,128)S(1)}, u32[]{:S(2)}, u32[]{:S(2)}) async-start(f32[4,272,256]{2,1,0:T(8,128)} %copy-done.1), calls=%async_computation.7 | async-start | bytes 2228224 | tf_op jit(solution)/shard_map/all_to_all | solution.py:357
  278.0 14.8 %all-to-all-start.10 = ((f32[4,272,256]{2,1,0:T(8,128)}), f32[4,272,256]{2,1,0:T(8,128)}, u32[]{:S(2)}, u32[]{:S(2)}) async-start(f32[4,272,256]{2,1,0:T(8,128)} %copy-done.3), calls=%async_computation.10 | async-start | bytes 2228224 | tf_op jit(solution)/shard_map/all_to_all | solution.py:357
  292.8 13.6 %all-to-all-start.8 = ((f32[4,272,256]{2,1,0:T(8,128)}), f32[4,272,256]{2,1,0:T(8,128)S(1)}, u32[]{:S(2)}, u32[]{:S(2)}) async-start(f32[4,272,256]{2,1,0:T(8,128)} %copy-done.4), calls=%async_computation.8 | async-start | bytes 2228224 | tf_op jit(solution)/shard_map/all_to_all | solution.py:357
  308.3 16.1 %collective-permute-start.7 = (f32[272,256]{1,0:T(8,128)S(1)}, f32[272,256]{1,0:T(8,128)S(1)}, u32[]{:S(2)}, u32[]{:S(2)}) collective-permute-start(f32[272,256]{1,0:T(8,128)S(1)} %fusion.4), channel_id=1, source_target_pairs={{0,1},{1,0},{2,3},{3,2},{4,5},{5,4},{6,7},{7,6},{8,9},{9,8},{10,11... | collective-permute-start | bytes 835592 | tf_op jit(solution)/shard_map/ppermute | solution.py:461
  325.1 42.5 %copy-start.7 = (f32[17,16,256]{2,1,0:T(8,128)S(1)}, f32[17,16,256]{2,1,0:T(8,128)}, u32[]{:S(2)}) copy-start(f32[17,16,256]{2,1,0:T(8,128)} %chi_ref.1) | copy-start | bytes 835588
  339.7 28.0 %collective-permute-start.8 = (f32[4,272,256]{2,1,0:T(8,128)S(1)}, f32[4,272,256]{2,1,0:T(8,128)}, u32[]{:S(2)}, u32[]{:S(2)}) collective-permute-start(f32[4,272,256]{2,1,0:T(8,128)S(1)} %all_to_all.62.refs_0_), channel_id=1, source_target_pairs={{0,64},{64,0},{128,192},{192,128},{256,320},{320,256},{384,448},{4... | collective-permute-start | bytes 3342344 | tf_op jit(solution)/shard_map/ppermute | solution.py:464
  (4 other events, 3.8 us)
Sparse Core Ops, SparseCore 0:
  95.7 27.7 all-gather.2

commit v7 on v6

--- a/solution.py
+++ b/solution.py
@@ -326,31 +326,28 @@
     )(lat, near, far, serve)
 
 
-def finish_kernel(chi_ref, lat_ref, *refs):
-    bands, out_ref = refs[:-1], refs[-1]
+def finish_kernel(before_ref, lat_ref, band_ref, out_ref):
     mains = []
     lasts = []
-    for near_far in range(2):
-        for half in range(2):
-            ref = bands[near_far]
-            base = half * HALF
-            for x in range(4):
-                main = ref[x, base : base + 4 * OWNER, :].reshape(8, MAIN, CELLS)
-                mains.append(jnp.swapaxes(main, 0, 1))
-                lasts.append(ref[x, base + 4 * OWNER : base + HALF, :])
+    for half in range(2):
+        base = half * HALF
+        for x in range(4):
+            main = band_ref[x, base : base + 4 * OWNER, :].reshape(8, MAIN, CELLS)
+            mains.append(jnp.swapaxes(main, 0, 1))
+            lasts.append(band_ref[x, base + 4 * OWNER : base + HALF, :])
     for level in range(LEVELS):
         rows = jnp.concatenate([m[level] for m in mains] if level < MAIN else lasts, axis=0)
-        out_ref[level] = chi_ref[level] + lax.dot_general(
+        out_ref[level] = before_ref[level] + lax.dot_general(
             lat_ref[...], rows, (((1,), (0,)), ((), ())), precision=HIGHEST, preferred_element_type=F32
         )
 
 
-def finish(chi, lat, bands):
+def finish(before, lat, band):
     return pl.pallas_call(
         finish_kernel,
-        out_shape=jax.ShapeDtypeStruct(chi.shape, F32),
-        compiler_params=params(),
-    )(chi, lat, *bands)
+        out_shape=jax.ShapeDtypeStruct(before.shape, F32),
+        compiler_params=params(),
+    )(before, lat, band)
 
 
 def exchange(blocks, axis):
@@ -419,7 +416,7 @@
     constant = jnp.dot(scaled.T, innovation, precision=HIGHEST, preferred_element_type=F32)
     lats = near_far(mat_lat.reshape(16, 4, 2, 16), 2, core)
     lat_start = jnp.stack(lats, axis=1).reshape(16, 128)
-    lat_finish = jnp.stack([m.reshape(16, 4, 2, 8).transpose(0, 2, 1, 3) for m in lats], axis=1).reshape(16, 128)
+    lat_finish = [m.reshape(16, 4, 2, 8).transpose(0, 2, 1, 3).reshape(16, 64) for m in lats]
     band_near, serve, hessian, constant, lat_start, lat_finish = lax.optimization_barrier(
         (band_near, serve, hessian, constant, lat_start, lat_finish)
     )
@@ -443,14 +440,14 @@
     about = both_of(about, 4, 0)
     about, far_tiles = lax.optimization_barrier((about, far_tiles))
     tile_near = product(near_tiles, lon_near) + product(far_tiles, lon_far)
-    tile_far = product(near_tiles, other_near) + product(far_tiles, other_far)
+    tile_far = product(near_tiles, other_near)
     near_tiles = to_all(tile_near, "obs")
     about = both_of(about, 2, 1)
     about = both_of(about, 1, 2).reshape(ABOUT)
-    copies = jnp.broadcast_to(tile_far[None], (4,) + tile_far.shape)
-    about, copies = lax.optimization_barrier((about, copies))
+    about, tile_far = lax.optimization_barrier((about, tile_far))
+    tile_far = tile_far + product(far_tiles, other_far)
     mean = means(pick(near_tiles, about, 0), about, 0)
-    mean = means(pick(exchange(copies, "obs"), about, 1), about, 1, mean)
+    mean = means(pick(to_all(tile_far, "obs"), about, 1), about, 1, mean)
 
     mean = lax.all_to_all(mean, "lev", 0, 0)
     pulled = lax.all_to_all(pull(mean, hessian, constant), "lev", 0, 0)
@@ -462,7 +459,7 @@
     field = product(far_tiles, lon_far) + product(near_tiles, lon_near) + far
     band_near = to_all(field, "lat")
     band_far = lax.ppermute(band_near, "lat", PARTNER)
-    return finish(chi, lat_finish, [band_near, band_far])
+    return finish(finish(chi, lat_finish[0], band_near), lat_finish[1], band_far)
 
 
 def solution(mesh):

time: 380 us -> 381 us (level)
  no operation moved by 1% of the time
where the time goes in v7:
time: 381 us; the launch traced here: 379 us
  starting transfers between devices  99.9 us (26%)
  waiting for transfers between devices  91.7 us (24%)
  blocking collectives  82.8 us (22%)
  Pallas kernels  45.9 us (12%)
  local copies, waits for them, and re-layouts  22.3 us (6%)
  matrix products  18.9 us (5%)
  between operations  14.1 us (4%)
    all_to_all x9, waiting for transfers between devices, exchange(): return lax.all_to_all(blocks, axis, 0, 0, axis_index_groups=ALONG)  55.6 us
    all_to_all x9, starting transfers between devices, exchange(): return lax.all_to_all(blocks, axis, 0, 0, axis_index_groups=ALONG)  36.2 us
    all_to_all x1, blocking collectives, shards(): pulled = lax.all_to_all(pull(mean, hessian, constant), 'lev', 0, 0)  33.9 us
    all_to_all x1, blocking collectives, shards(): mean = lax.all_to_all(mean, 'lev', 0, 0)  32.7 us
    ppermute x2, starting transfers between devices, shards(): band_far = lax.ppermute(band_near, 'lat', PARTNER)  28.3 us
    ppermute x4, waiting for transfers between devices, both_of(): other = lax.ppermute(x, 'lev', [(m, m ^ step) for m in range(8)])  26.2 us
    ppermute x1, starting transfers between devices, shards(): piece = lax.ppermute(piece, 'obs', PARTNER)  16.3 us
    all_to_all x1, blocking collectives, exchange(): return lax.all_to_all(blocks, axis, 0, 0, axis_index_groups=ALONG)  16.2 us
  transfers between devices with their start and end apart: 19, of which 15 were waited for; matrix products, arithmetic and copies ran while one was open for 9% of the time, Pallas kernels for 6%

profile of v7, /device:TPU:1, one launch (start us, length us, event | category | flops | bytes accessed | tf_op | source)
XLA Modules:
  0.0 378.8 jit_solution(7201248407950786527)
XLA Ops:
  8.8 16.3 %collective-permute-start = (f32[136,256]{1,0:T(8,128)}, f32[136,256]{1,0:T(8,128)}, u32[]{:S(2)}, u32[]{:S(2)}) collective-permute-start(f32[136,256]{1,0:T(8,128)} %pad_maximum_fusion.2), channel_id=1, source_target_pairs={{0,1},{1,0},{2,3},{3,2},{4,5},{5,4},{6,7},{7,6},{8,9},{9,8},{10,11... | collective-permute-start | bytes 417800 | tf_op jit(solution)/shard_map/ppermute | solution.py:402
  27.2 4.1 %all-to-all-start = ((f32[4,17,16,256]{3,2,1,0:T(8,128)}), f32[4,17,16,256]{3,2,1,0:T(8,128)S(1)}, u32[]{:S(2)}, u32[]{:S(2)}) async-start(f32[4,17,16,256]{3,2,1,0:T(8,128)} %broadcast_in_dim.10), calls=%async_computation | async-start | bytes 2228224 | tf_op jit(solution)/shard_map/all_to_all | solution.py:354
  46.0 4.1 %collective-permute-start.1 = (f32[4,17,16,256]{3,2,1,0:T(8,128)S(1)}, f32[4,17,16,256]{3,2,1,0:T(8,128)S(1)}, u32[]{:S(2)}, u32[]{:S(2)}) collective-permute-start(f32[4,17,16,256]{3,2,1,0:T(8,128)S(1)} %all-to-all-done.near_ref), channel_id=1, source_target_pairs={{0,64},{64,0},{128,192},{192,128},{256,320},{320,256},{384,448},{4... | collective-permute-start | bytes 3342344 | tf_op jit(solution)/shard_map/ppermute | solution.py:425
  55.3 4.4 %all-to-all-start.1 = ((f32[4,280,256]{2,1,0:T(8,128)}), f32[4,280,256]{2,1,0:T(8,128)}, u32[]{:S(2)}, u32[]{:S(2)}) async-start(f32[4,280,256]{2,1,0:T(8,128)} %copy-done.6), calls=%async_computation.1 | async-start | bytes 2293760 | tf_op jit(solution)/shard_map/all_to_all | solution.py:354
  61.8 13.7 %all-to-all-done.1 = f32[4,280,256]{2,1,0:T(8,128)} async-done(((f32[4,280,256]{2,1,0:T(8,128)}), f32[4,280,256]{2,1,0:T(8,128)}, u32[]{:S(2)}, u32[]{:S(2)}) %all-to-all-start.1) | async-done | bytes 1146912 | tf_op jit(solution)/shard_map/all_to_all | solution.py:354
  79.0 15.8 %collective-permute-done.2 = f32[128,256]{1,0:T(8,128)S(1)} collective-permute-done((f32[128,256]{1,0:T(8,128)S(1)}, f32[128,256]{1,0:T(8,128)S(1)}, u32[]{:S(2)}, u32[]{:S(2)}) %collective-permute-start.2) | collective-permute-done | bytes 131104 | tf_op jit(solution)/shard_map/ppermute | solution.py:362
  97.5 3.5 all-to-all-start.2
  103.0 6.8 %collective-permute-done.4 = f32[96,128]{1,0:T(8,128)S(1)} collective-permute-done((f32[96,128]{1,0:T(8,128)S(1)}, f32[96,128]{1,0:T(8,128)S(1)}, u32[]{:S(2)}, u32[]{:S(2)}) %collective-permute-start.4) | collective-permute-done | bytes 49184 | tf_op jit(solution)/shard_map/ppermute | solution.py:362
  109.8 6.4 %all-to-all-done.2 = f32[4,272,256]{2,1,0:T(8,128)S(1)} async-done(((f32[4,272,256]{2,1,0:T(8,128)}), f32[4,272,256]{2,1,0:T(8,128)S(1)}, u32[]{:S(2)}, u32[]{:S(2)}) %all-to-all-start.2) | async-done | bytes 1114144 | tf_op jit(solution)/shard_map/all_to_all | solution.py:354
  121.7 4.2 %all-to-all-start.4 = ((f32[4,272,256]{2,1,0:T(8,128)}), f32[4,272,256]{2,1,0:T(8,128)}, u32[]{:S(2)}, u32[]{:S(2)}) async-start(f32[4,272,256]{2,1,0:T(8,128)} %broadcast_in_dim.13), calls=%async_computation.4 | async-start | bytes 2228224 | tf_op jit(solution)/shard_map/all_to_all | solution.py:354
  129.2 3.6 collective-permute-done.6
  137.1 3.2 all-to-all-done.4.field_ref
  141.4 4.3 %all-to-all-start.3 = ((f32[4,272,256]{2,1,0:T(8,128)}), f32[4,272,256]{2,1,0:T(8,128)}, u32[]{:S(2)}, u32[]{:S(2)}) async-start(f32[4,272,256]{2,1,0:T(8,128)} %broadcast_in_dim.12), calls=%async_computation.3 | async-start | bytes 2228224 | tf_op jit(solution)/shard_map/all_to_all | solution.py:354
  145.7 3.8 shard_map.111.slots_ref
  149.5 6.4 %shard_map.112.refs_0_ = f32[8,136,128]{2,1,0:T(8,128)S(1)} custom-call(f32[8,96,128]{2,1,0:T(8,128)S(1)} %bitcast.116, f32[8,136,256]{2,1,0:T(8,128)S(1)} %shard_map.111.slots_ref), custom_call_target="tpu_custom_call" | custom-call | tf_op jit(solution)/shard_map/pallas_call | solution.py:156
  158.8 3.7 shard_map.110.slots_ref
  162.6 6.4 %shard_map.113 = f32[8,136,128]{2,1,0:T(8,128)S(1)} custom-call(f32[8,96,128]{2,1,0:T(8,128)S(1)} %bitcast.118, f32[8,136,256]{2,1,0:T(8,128)S(1)} %shard_map.110.slots_ref, f32[8,136,128]{2,1,0:T(8,128)S(1)} %shard_map.112.refs_0_), custom_call_target="tpu_custom_call" | custom-call | tf_op jit(solution)/shard_map/pallas_call | solution.py:156
  169.0 32.7 %all_to_all.60.mean_ref = f32[8,136,128]{2,1,0:T(8,128)S(1)} all-to-all(f32[8,136,128]{2,1,0:T(8,128)S(1)} %shard_map.113), channel_id=1, replica_groups=mesh['lat'=8,'lev'=8,'obs'=8] {'lev'}, dimensions={0} | all-to-all | bytes 1114112 | tf_op jit(solution)/shard_map/all_to_all | solution.py:452
  202.3 33.9 %all_to_all.61.grad_ref = f32[8,136,128]{2,1,0:T(8,128)S(1)} all-to-all(f32[8,136,128]{2,1,0:T(8,128)S(1)} %shard_map.114), channel_id=1, replica_groups=mesh['lat'=8,'lev'=8,'obs'=8] {'lev'}, dimensions={0} | all-to-all | bytes 1114112 | tf_op jit(solution)/shard_map/all_to_all | solution.py:453
  236.2 6.4 %shard_map.118.slots_ref = f32[8,136,256]{2,1,0:T(8,128)S(1)} custom-call(f32[8,136,128]{2,1,0:T(8,128)S(1)} %all_to_all.61.grad_ref, f32[8,96,128]{2,1,0:T(8,128)S(1)} %bitcast.119), custom_call_target="tpu_custom_call" | custom-call | tf_op jit(solution)/shard_map/pallas_call | solution.py:225
  246.8 4.2 %all-to-all-start.9 = ((f32[4,272,256]{2,1,0:T(8,128)}), f32[4,272,256]{2,1,0:T(8,128)}, u32[]{:S(2)}, u32[]{:S(2)}) async-start(f32[4,272,256]{2,1,0:T(8,128)} %copy-done.2), calls=%async_computation.9 | async-start | bytes 2228224 | tf_op jit(solution)/shard_map/all_to_all | solution.py:354
  251.0 6.4 %shard_map.115.slots_ref = f32[8,136,256]{2,1,0:T(8,128)S(1)} custom-call(f32[8,136,128]{2,1,0:T(8,128)S(1)} %all_to_all.61.grad_ref, f32[8,96,128]{2,1,0:T(8,128)S(1)} %bitcast.121), custom_call_target="tpu_custom_call" | custom-call | tf_op jit(solution)/shard_map/pallas_call | solution.py:225
  264.0 3.5 all-to-all-start.7
  269.8 9.3 %all-to-all-done.7.parts_ref = f32[4,272,256]{2,1,0:T(8,128)S(1)} async-done(((f32[4,272,256]{2,1,0:T(8,128)}), f32[4,272,256]{2,1,0:T(8,128)S(1)}, u32[]{:S(2)}, u32[]{:S(2)}) %all-to-all-start.7) | async-done | bytes 1114144 | tf_op jit(solution)/shard_map/all_to_all | solution.py:354
  279.2 4.3 %all-to-all-start.10 = ((f32[4,272,256]{2,1,0:T(8,128)}), f32[4,272,256]{2,1,0:T(8,128)}, u32[]{:S(2)}, u32[]{:S(2)}) async-start(f32[4,272,256]{2,1,0:T(8,128)} %copy-done.3), calls=%async_computation.10 | async-start | bytes 2228224 | tf_op jit(solution)/shard_map/all_to_all | solution.py:354
  284.5 9.4 %all-to-all-done.10 = f32[4,272,256]{2,1,0:T(8,128)} async-done(((f32[4,272,256]{2,1,0:T(8,128)}), f32[4,272,256]{2,1,0:T(8,128)}, u32[]{:S(2)}, u32[]{:S(2)}) %all-to-all-start.10) | async-done | bytes 1114144 | tf_op jit(solution)/shard_map/all_to_all | solution.py:354
  294.0 3.5 all-to-all-start.8
  299.7 7.9 %all-to-all-done.8 = f32[4,272,256]{2,1,0:T(8,128)S(1)} async-done(((f32[4,272,256]{2,1,0:T(8,128)}), f32[4,272,256]{2,1,0:T(8,128)S(1)}, u32[]{:S(2)}, u32[]{:S(2)}) %all-to-all-start.8) | async-done | bytes 1114144 | tf_op jit(solution)/shard_map/all_to_all | solution.py:354
  309.4 7.6 %collective-permute-start.7 = (f32[272,256]{1,0:T(8,128)S(1)}, f32[272,256]{1,0:T(8,128)S(1)}, u32[]{:S(2)}, u32[]{:S(2)}) collective-permute-start(f32[272,256]{1,0:T(8,128)S(1)} %fusion.4), channel_id=1, source_target_pairs={{0,1},{1,0},{2,3},{3,2},{4,5},{5,4},{6,7},{7,6},{8,9},{9,8},{10,11... | collective-permute-start | bytes 835592 | tf_op jit(solution)/shard_map/ppermute | solution.py:458
  318.9 6.7 %collective-permute-done.7 = f32[272,256]{1,0:T(8,128)S(1)} collective-permute-done((f32[272,256]{1,0:T(8,128)S(1)}, f32[272,256]{1,0:T(8,128)S(1)}, u32[]{:S(2)}, u32[]{:S(2)}) %collective-permute-start.7) | collective-permute-done | bytes 278560 | tf_op jit(solution)/shard_map/ppermute | solution.py:458
  326.3 16.2 %all_to_all.62.band_ref = f32[4,272,256]{2,1,0:T(8,128)S(1)} all-to-all(f32[4,272,256]{2,1,0:T(8,128)S(1)} %broadcast_in_dim.14), channel_id=1, replica_groups={{0,128,256,384},{64,192,320,448},{1,129,257,385},{65,193,321,449},{2,13..., dimensions={0} | all-to-all | bytes 2228224 | tf_op jit(solution)/shard_map/all_to_all | solution.py:354
  342.5 24.3 %collective-permute-start.8 = (f32[4,272,256]{2,1,0:T(8,128)S(1)}, f32[4,272,256]{2,1,0:T(8,128)}, u32[]{:S(2)}, u32[]{:S(2)}) collective-permute-start(f32[4,272,256]{2,1,0:T(8,128)S(1)} %all_to_all.62.band_ref), channel_id=1, source_target_pairs={{0,64},{64,0},{128,192},{192,128},{256,320},{320,256},{384,448},{4... | collective-permute-start | bytes 3342344 | tf_op jit(solution)/shard_map/ppermute | solution.py:461
  (117 shorter events, 77.8 us)
Async XLA Ops:
  6.5 1.6 copy-start
  8.8 35.9 %collective-permute-start = (f32[136,256]{1,0:T(8,128)}, f32[136,256]{1,0:T(8,128)}, u32[]{:S(2)}, u32[]{:S(2)}) collective-permute-start(f32[136,256]{1,0:T(8,128)} %pad_maximum_fusion.2), channel_id=1, source_target_pairs={{0,1},{1,0},{2,3},{3,2},{4,5},{5,4},{6,7},{7,6},{8,9},{9,8},{10,11... | collective-permute-start | bytes 417800 | tf_op jit(solution)/shard_map/ppermute | solution.py:402
  27.2 4.2 %copy-start.16 = (f32[16,128]{1,0:T(8,128)S(1)}, f32[16,128]{1,0:T(8,128)}, u32[]{:S(2)}) copy-start(f32[16,128]{1,0:T(8,128)} %param.13) | copy-start | bytes 24580
  27.2 18.7 %all-to-all-start = ((f32[4,17,16,256]{3,2,1,0:T(8,128)}), f32[4,17,16,256]{3,2,1,0:T(8,128)S(1)}, u32[]{:S(2)}, u32[]{:S(2)}) async-start(f32[4,17,16,256]{3,2,1,0:T(8,128)} %broadcast_in_dim.10), calls=%async_computation | async-start | bytes 2228224 | tf_op jit(solution)/shard_map/all_to_all | solution.py:354
  31.4 7.7 %copy-start.17 = (s32[300]{0:T(512)S(1)}, s32[300]{0:T(512)}, u32[]{:S(2)}) copy-start(s32[300]{0:T(512)} %param.16) | copy-start | bytes 3604
  34.6 6.5 %copy-start.15 = (f32[300]{0:T(512)S(1)}, f32[300]{0:T(512)}, u32[]{:S(2)}) copy-start(f32[300]{0:T(512)} %param.17) | copy-start | bytes 3604
  46.0 6.4 %collective-permute-start.1 = (f32[4,17,16,256]{3,2,1,0:T(8,128)S(1)}, f32[4,17,16,256]{3,2,1,0:T(8,128)S(1)}, u32[]{:S(2)}, u32[]{:S(2)}) collective-permute-start(f32[4,17,16,256]{3,2,1,0:T(8,128)S(1)} %all-to-all-done.near_ref), channel_id=1, source_target_pairs={{0,64},{64,0},{128,192},{192,128},{256,320},{320,256},{384,448},{4... | collective-permute-start | bytes 3342344 | tf_op jit(solution)/shard_map/ppermute | solution.py:425
  53.5 1.1 copy-start.6
  55.3 4.5 %copy-start.9 = (f32[272,256]{1,0:T(8,128)S(1)}, f32[272,256]{1,0:T(8,128)}, u32[]{:S(2)}) copy-start(f32[272,256]{1,0:T(8,128)} %copy-done.8) | copy-start | bytes 835588
  55.3 20.1 %all-to-all-start.1 = ((f32[4,280,256]{2,1,0:T(8,128)}), f32[4,280,256]{2,1,0:T(8,128)}, u32[]{:S(2)}, u32[]{:S(2)}) async-start(f32[4,280,256]{2,1,0:T(8,128)} %copy-done.6), calls=%async_computation.1 | async-start | bytes 2293760 | tf_op jit(solution)/shard_map/all_to_all | solution.py:354
  59.7 35.8 %copy-start.13 = (s32[4,1024]{1,0:T(4,128)S(1)}, s32[4,1024]{1,0:T(4,128)}, u32[]{:S(2)}) copy-start(s32[4,1024]{1,0:T(4,128)} %param.20) | copy-start | bytes 49156
  59.7 35.9 %copy-start.14 = (f32[4,1024]{1,0:T(4,128)S(1)}, f32[4,1024]{1,0:T(4,128)}, u32[]{:S(2)}) copy-start(f32[4,1024]{1,0:T(4,128)} %param.19) | copy-start | bytes 49156
  59.8 73.2 %all-gather.3.cloned.1.call-start = ((), (), s32[]{:S(2)}) async-start(), calls=%async_computation.12 | async-start | bytes 2359296 | tf_op jit(solution)/shard_map/all_gather | solution.py:432
  59.8 35.7 %collective-permute-start.3 = (f32[272,256]{1,0:T(8,128)S(1)}, f32[272,256]{1,0:T(8,128)S(1)}, u32[]{:S(2)}, u32[]{:S(2)}) collective-permute-start(f32[272,256]{1,0:T(8,128)S(1)} %copy-done.9), channel_id=1, source_target_pairs={{0,1},{1,0},{2,3},{3,2},{4,5},{5,4},{6,7},{7,6},{8,9},{9,8},{10,11... | collective-permute-start | bytes 835592 | tf_op jit(solution)/shard_map/ppermute | solution.py:427
  76.4 18.5 %collective-permute-start.2 = (f32[128,256]{1,0:T(8,128)S(1)}, f32[128,256]{1,0:T(8,128)S(1)}, u32[]{:S(2)}, u32[]{:S(2)}) collective-permute-start(f32[128,256]{1,0:T(8,128)S(1)} %get-tuple-element.46), channel_id=1, source_target_pairs={{0,8},{8,0},{16,24},{24,16},{32,40},{40,32},{48,56},{56,48},{1,9},... | collective-permute-start | bytes 393224 | tf_op jit(solution)/shard_map/ppermute | solution.py:362
  97.5 18.7 %all-to-all-start.2 = ((f32[4,272,256]{2,1,0:T(8,128)}), f32[4,272,256]{2,1,0:T(8,128)S(1)}, u32[]{:S(2)}, u32[]{:S(2)}) async-start(f32[4,272,256]{2,1,0:T(8,128)} %broadcast_in_dim.11), calls=%async_computation.2 | async-start | bytes 2228224 | tf_op jit(solution)/shard_map/all_to_all | solution.py:354
  101.0 8.7 %collective-permute-start.4 = (f32[96,128]{1,0:T(8,128)S(1)}, f32[96,128]{1,0:T(8,128)S(1)}, u32[]{:S(2)}, u32[]{:S(2)}) collective-permute-start(f32[96,128]{1,0:T(8,128)S(1)} %pad_maximum_fusion.4), channel_id=1, source_target_pairs={{0,32},{8,40},{16,48},{24,56},{32,0},{40,8},{48,16},{56,24},{1,33}... | collective-permute-start | bytes 147464 | tf_op jit(solution)/shard_map/ppermute | solution.py:362
  116.2 2.6 copy-start.10
  116.2 9.8 %collective-permute-start.5 = (f32[2,96,128]{2,1,0:T(8,128)S(1)}, f32[2,96,128]{2,1,0:T(8,128)S(1)}, u32[]{:S(2)}, u32[]{:S(2)}) collective-permute-start(f32[2,96,128]{2,1,0:T(8,128)S(1)} %maximum_select_fusion.3), channel_id=1, source_target_pairs={{0,16},{8,24},{16,0},{24,8},{32,48},{40,56},{48,32},{56,40},{1,17}... | collective-permute-start | bytes 294920 | tf_op jit(solution)/shard_map/ppermute | solution.py:362
  121.7 18.6 %all-to-all-start.4 = ((f32[4,272,256]{2,1,0:T(8,128)}), f32[4,272,256]{2,1,0:T(8,128)}, u32[]{:S(2)}, u32[]{:S(2)}) async-start(f32[4,272,256]{2,1,0:T(8,128)} %broadcast_in_dim.13), calls=%async_computation.4 | async-start | bytes 2228224 | tf_op jit(solution)/shard_map/all_to_all | solution.py:354
  126.0 6.8 %collective-permute-start.6 = (f32[2,2,96,128]{3,2,1,0:T(8,128)S(1)}, f32[2,2,96,128]{3,2,1,0:T(8,128)S(1)}, u32[]{:S(2)}, u32[]{:S(2)}) collective-permute-start(f32[2,2,96,128]{3,2,1,0:T(8,128)S(1)} %maximum_select_fusion.2), channel_id=1, source_target_pairs={{0,8},{8,0},{16,24},{24,16},{32,40},{40,32},{48,56},{56,48},{1,9},... | collective-permute-start | bytes 589832 | tf_op jit(solution)/shard_map/ppermute | solution.py:362
  132.9 2.3 copy-start.11
  141.4 17.4 %all-to-all-start.3 = ((f32[4,272,256]{2,1,0:T(8,128)}), f32[4,272,256]{2,1,0:T(8,128)}, u32[]{:S(2)}, u32[]{:S(2)}) async-start(f32[4,272,256]{2,1,0:T(8,128)} %broadcast_in_dim.12), calls=%async_computation.3 | async-start | bytes 2228224 | tf_op jit(solution)/shard_map/all_to_all | solution.py:354
  169.0 32.7 %copy-start.5 = (f32[136,1024]{1,0:T(8,128)S(1)}, f32[136,1024]{1,0:T(8,128)}, u32[]{:S(2)}) copy-start(f32[136,1024]{1,0:T(8,128)} %fusion.25.constant_ref) | copy-start | bytes 1671172
  246.8 17.2 %all-to-all-start.9 = ((f32[4,272,256]{2,1,0:T(8,128)}), f32[4,272,256]{2,1,0:T(8,128)}, u32[]{:S(2)}, u32[]{:S(2)}) async-start(f32[4,272,256]{2,1,0:T(8,128)} %copy-done.2), calls=%async_computation.9 | async-start | bytes 2228224 | tf_op jit(solution)/shard_map/all_to_all | solution.py:354
  264.0 15.2 %all-to-all-start.7 = ((f32[4,272,256]{2,1,0:T(8,128)}), f32[4,272,256]{2,1,0:T(8,128)S(1)}, u32[]{:S(2)}, u32[]{:S(2)}) async-start(f32[4,272,256]{2,1,0:T(8,128)} %copy-done.1), calls=%async_computation.7 | async-start | bytes 2228224 | tf_op jit(solution)/shard_map/all_to_all | solution.py:354
  279.2 14.8 %all-to-all-start.10 = ((f32[4,272,256]{2,1,0:T(8,128)}), f32[4,272,256]{2,1,0:T(8,128)}, u32[]{:S(2)}, u32[]{:S(2)}) async-start(f32[4,272,256]{2,1,0:T(8,128)} %copy-done.3), calls=%async_computation.10 | async-start | bytes 2228224 | tf_op jit(solution)/shard_map/all_to_all | solution.py:354
  294.0 13.6 %all-to-all-start.8 = ((f32[4,272,256]{2,1,0:T(8,128)}), f32[4,272,256]{2,1,0:T(8,128)S(1)}, u32[]{:S(2)}, u32[]{:S(2)}) async-start(f32[4,272,256]{2,1,0:T(8,128)} %copy-done.4), calls=%async_computation.8 | async-start | bytes 2228224 | tf_op jit(solution)/shard_map/all_to_all | solution.py:354
  309.4 16.1 %collective-permute-start.7 = (f32[272,256]{1,0:T(8,128)S(1)}, f32[272,256]{1,0:T(8,128)S(1)}, u32[]{:S(2)}, u32[]{:S(2)}) collective-permute-start(f32[272,256]{1,0:T(8,128)S(1)} %fusion.4), channel_id=1, source_target_pairs={{0,1},{1,0},{2,3},{3,2},{4,5},{5,4},{6,7},{7,6},{8,9},{9,8},{10,11... | collective-permute-start | bytes 835592 | tf_op jit(solution)/shard_map/ppermute | solution.py:458
  326.3 40.5 %copy-start.12 = (f32[16,2,4,8]{0,3,2,1:T(8,128)S(1)}, f32[16,2,4,8]{0,3,2,1:T(8,128)}, u32[]{:S(2)}) copy-start(f32[16,2,4,8]{0,3,2,1:T(8,128)} %copy.35) | copy-start | bytes 12292
  326.3 41.4 %copy-start.7 = (f32[17,16,256]{2,1,0:T(8,128)S(1)}, f32[17,16,256]{2,1,0:T(8,128)}, u32[]{:S(2)}) copy-start(f32[17,16,256]{2,1,0:T(8,128)} %before_ref.1) | copy-start | bytes 835588
  342.5 26.8 %collective-permute-start.8 = (f32[4,272,256]{2,1,0:T(8,128)S(1)}, f32[4,272,256]{2,1,0:T(8,128)}, u32[]{:S(2)}, u32[]{:S(2)}) collective-permute-start(f32[4,272,256]{2,1,0:T(8,128)S(1)} %all_to_all.62.band_ref), channel_id=1, source_target_pairs={{0,64},{64,0},{128,192},{192,128},{256,320},{320,256},{384,448},{4... | collective-permute-start | bytes 3342344 | tf_op jit(solution)/shard_map/ppermute | solution.py:461
  (5 other events, 4.8 us)
Sparse Core Ops, SparseCore 0:
  95.7 28.8 all-gather.2
